TPU v7x, 256 devices: a whole 4x4x8 slice. The times are simulated.
256 devices in a mesh: seq: 32 (over y, z), head: 8 (over x, core).
Axes of the slice: x: 4, y: 4, z: 8, core: 2. Of those that a mesh axis runs over, the one named last changes fastest.
Arguments:
- queries: float32 [8192, 2048], P('seq', 'head'), may hold values from -6 to 6
- reflect_keys: float32 [8192, 2, 2048], P('seq', None, 'head'), may hold values from -6 to 6
- reflect_values: float32 [8192, 2, 2048], P('seq', None, 'head'), may hold values from -0.625 to 0.625
- beta_logit: float32 [2, 16, 8192], P(None, 'head', 'seq'), may hold values from -1.5 to 6, as said below
- out_weight: bfloat16 [2048, 2048], P('head'), may hold values from -0.125 to 0.125
- out_grad: bfloat16 [8192, 2048], P('seq', 'head'), may hold values from -0.125 to 0.125
Outputs:
- output: bfloat16 [8192, 2048], P('seq', 'head')
- query_grad: float32 [8192, 2048], P('seq', 'head')
- key_grad: float32 [8192, 2, 2048], P('seq', None, 'head')
- value_grad: float32 [8192, 2, 2048], P('seq', None, 'head')
- logit_grad: float32 [2, 16, 8192], P(None, 'head', 'seq')
- weight_grad: float32 [2048, 2048], P(('head', 'seq'))
Inputs may be any that keep to these rules, and one draw needn't show every extreme that they name: `beta_logit`: logits of the reflections' strengths.
All inputs are finite; a program needn't handle non-finite values.
Results may differ from a plain program's by a relative error of at most 0.02.
Values may be sent and summed in bfloat16 or wider, within the bound.
No kernel may reach another device: no remote copies, remote signals or barrier semaphores. Data moves between devices by JAX's collectives and lax.ppermute only.
A program may use at most 128 MiB of HBM per device.

v0:
```python
import jax
import jax.numpy as jnp
from jax import lax
from jax.sharding import PartitionSpec as P

HEAD_DIM = 128
BLOCK = 64


HIGHEST_PRECISION = lax.Precision.HIGHEST


def passed_along(shard, axis, by):
    count = lax.axis_size(axis)
    pairs = [(i, i + by) for i in range(count) if 0 <= i + by < count]
    return lax.ppermute(shard, axis, pairs)


def normalize(vectors):
    return vectors * lax.rsqrt(jnp.sum(vectors * vectors, axis=-1, keepdims=True) + 1e-06)


def block_core(carry_state, query_block, key_block, value_block, beta_block):
    pseudo = key_block.shape[1]
    width = key_block.shape[2]
    reflections = pseudo // query_block.shape[1]
    gram = jnp.einsum("hik,hjk->hij", key_block, key_block, precision=HIGHEST_PRECISION)
    row_index = jnp.arange(pseudo)[:, None]
    col_index = jnp.arange(pseudo)[None, :]
    system = jnp.where(col_index < row_index, gram, 0.0) * beta_block[:, :, None] + jnp.eye(
        pseudo, dtype=key_block.dtype
    )
    right_side = jnp.concatenate([key_block, value_block], axis=-1) * beta_block[:, :, None]
    solved = lax.linalg.triangular_solve(
        system, right_side, left_side=True, lower=True, unit_diagonal=True
    )
    key_weights = solved[:, :, :width]
    new_values = solved[:, :, width:] - jnp.einsum(
        "hnk,hvk->hnv", key_weights, carry_state, precision=HIGHEST_PRECISION
    )
    scores = jnp.einsum("hck,hnk->hcn", query_block, key_block, precision=HIGHEST_PRECISION)
    visible = (
        jnp.arange(pseudo)[None, :]
        <= reflections * jnp.arange(query_block.shape[1])[:, None] + reflections - 1
    )
    scores = jnp.where(visible, scores, 0.0)
    mixed_block = jnp.einsum("hvk,hck->hcv", carry_state, query_block, precision=HIGHEST_PRECISION)
    mixed_block = mixed_block + jnp.einsum(
        "hcn,hnv->hcv", scores, new_values, precision=HIGHEST_PRECISION
    )
    next_state = carry_state + jnp.einsum(
        "hnv,hnk->hvk", new_values, key_block, precision=HIGHEST_PRECISION
    )
    return (mixed_block, next_state, key_weights)


def arrange(queries, reflect_keys, reflect_values, beta_logit, head_count):
    tokens_here = queries.shape[0]
    reflections = reflect_keys.shape[1]
    width = queries.shape[1] // head_count
    query_heads = normalize(queries.reshape(tokens_here, head_count, width)).transpose(1, 0, 2)
    key_heads = normalize(reflect_keys.reshape(tokens_here, reflections, head_count, width))
    key_heads = key_heads.transpose(2, 0, 1, 3).reshape(
        head_count, tokens_here * reflections, width
    )
    value_heads = reflect_values.reshape(tokens_here, reflections, head_count, width)
    value_heads = value_heads.transpose(2, 0, 1, 3).reshape(
        head_count, tokens_here * reflections, width
    )
    strengths = 2.0 * jax.nn.sigmoid(
        beta_logit.transpose(1, 2, 0).reshape(head_count, tokens_here * reflections)
    )
    return (query_heads, key_heads, value_heads, strengths)


def mixer(
    queries,
    reflect_keys,
    reflect_values,
    beta_logit,
    start_state,
    head_count,
    block_tokens,
    with_transition,
):
    query_heads, key_heads, value_heads, strengths = arrange(
        queries, reflect_keys, reflect_values, beta_logit, head_count
    )
    width = query_heads.shape[2]
    tokens_here = query_heads.shape[1]
    reflections = key_heads.shape[1] // tokens_here
    blocks = tokens_here // block_tokens
    pseudo = block_tokens * reflections
    query_steps = query_heads.reshape(head_count, blocks, block_tokens, width).transpose(1, 0, 2, 3)
    key_steps = key_heads.reshape(head_count, blocks, pseudo, width).transpose(1, 0, 2, 3)
    value_steps = value_heads.reshape(head_count, blocks, pseudo, width).transpose(1, 0, 2, 3)
    beta_steps = strengths.reshape(head_count, blocks, pseudo).transpose(1, 0, 2)
    identity = jnp.broadcast_to(jnp.eye(width, dtype=start_state.dtype), start_state.shape)

    def advance(carry, block_items):
        carry_state, transition = carry
        query_block, key_block, value_block, beta_block = block_items
        mixed_block, next_state, key_weights = block_core(
            carry_state, query_block, key_block, value_block, beta_block
        )
        if with_transition:
            projected = jnp.einsum(
                "hab,hnb->han", transition, key_weights, precision=HIGHEST_PRECISION
            )
            transition = transition - jnp.einsum(
                "han,hnk->hak", projected, key_block, precision=HIGHEST_PRECISION
            )
        return ((next_state, transition), mixed_block)

    (end_state, transition), mixed_steps = lax.scan(
        advance, (start_state, identity), (query_steps, key_steps, value_steps, beta_steps)
    )
    mixed_out = mixed_steps.transpose(0, 2, 1, 3).reshape(tokens_here, head_count * width)
    return ((mixed_out, end_state), transition)


def body(queries, reflect_keys, reflect_values, beta_logit, out_weight, out_grad):
    full_grad = lax.all_gather(out_grad, "head", axis=1, tiled=True)
    mixed_grad = lax.dot_general(
        full_grad, out_weight, (((1,), (1,)), ((), ())), preferred_element_type=jnp.float32
    )
    head_count = out_weight.shape[0] // HEAD_DIM
    zero_state = jnp.zeros((head_count, HEAD_DIM, HEAD_DIM), jnp.float32)

    def from_state(start_state):
        return mixer(
            queries, reflect_keys, reflect_values, beta_logit, start_state, head_count, BLOCK, True
        )

    (first_mixed, offset), pull_start, transition = jax.vjp(from_state, zero_state, has_aux=True)
    local_adjoint = pull_start((mixed_grad, zero_state))[0]
    back_transition = jnp.swapaxes(transition, 1, 2)
    seq_count = lax.axis_size("seq")

    def forward_turn(turn_index, incoming):
        outgoing = (
            jnp.einsum("hvk,hkl->hvl", incoming, transition, precision=HIGHEST_PRECISION) + offset
        )
        return passed_along(outgoing, "seq", 1)

    def backward_turn(turn_index, incoming):
        outgoing = (
            jnp.einsum("hvk,hkl->hvl", incoming, back_transition, precision=HIGHEST_PRECISION)
            + local_adjoint
        )
        return passed_along(outgoing, "seq", -1)

    state_in = lax.fori_loop(0, seq_count - 1, forward_turn, zero_state)
    adjoint_in = lax.fori_loop(0, seq_count - 1, backward_turn, zero_state)

    def from_inputs(query_arg, key_arg, value_arg, logit_arg, start_state):
        return mixer(
            query_arg, key_arg, value_arg, logit_arg, start_state, head_count, BLOCK, False
        )

    (mixed_out, end_state), pull_all, unused_aux = jax.vjp(
        from_inputs, queries, reflect_keys, reflect_values, beta_logit, state_in, has_aux=True
    )
    query_grad, key_grad, value_grad, logit_grad, start_grad = pull_all((mixed_grad, adjoint_in))
    mixed_bf = mixed_out.astype(jnp.bfloat16)
    partial_out = jnp.dot(mixed_bf, out_weight, preferred_element_type=jnp.float32)
    output = lax.psum_scatter(partial_out, "head", scatter_dimension=1, tiled=True).astype(
        jnp.bfloat16
    )
    row_share = out_weight.shape[0] // lax.axis_size("seq")
    row_block = lax.slice_in_dim(mixed_bf, 0, row_share * lax.axis_size("seq"), axis=1)
    weight_grad = lax.psum_scatter(
        lax.dot_general(
            row_block, full_grad, (((0,), (0,)), ((), ())), preferred_element_type=jnp.float32
        ).astype(jnp.bfloat16),
        "seq",
        scatter_dimension=0,
        tiled=True,
    ).astype(jnp.float32)
    return (output, query_grad, key_grad, value_grad, logit_grad, weight_grad)


def solution(mesh):
    in_specs = (
        P("seq", "head"),
        P("seq", None, "head"),
        P("seq", None, "head"),
        P(None, "head", "seq"),
        P("head", None),
        P("seq", "head"),
    )
    out_specs = (
        P("seq", "head"),
        P("seq", "head"),
        P("seq", None, "head"),
        P("seq", None, "head"),
        P(None, "head", "seq"),
        P(("head", "seq"), None),
    )
    return jax.shard_map(body, mesh=mesh, in_specs=in_specs, out_specs=out_specs, check_vma=False)
```

profile of v0, /device:TPU:32, one launch (start us, length us, event | category | flops | bytes accessed | tf_op | source)
XLA Modules:
  0.0 1002.5 jit_solution(10204920392739022766)
XLA Ops:
  16.5 99.2 %while.115 = (s32[]{:T(128)}, f32[2,128,128]{2,1,0:T(8,128)S(1)}, f32[2,128,128]{2,1,0:T(8,128)S(1)}, f32[4,2,128,128]{3,2,1,0:T(8,128)}, f32[4,2,64,128]{3,2,1,...) while((s32[]{:T(128)}, f32[2,128,128]{2,1,0:T(8,128)S(1)}, ...), condition=%wide.region_3.5_spmd.clone, body=%wide.region_2.4_spmd.clone.sunk | while | flops 378044544 | bytes 4257948 | solution.py:115
  18.0 19.7 %custom-call.29 = f32[2,1,128,128]{2,3,1,0:T(8,128)S(1)} custom-call(f32[2,1,128,128]{3,2,1,0:T(8,128)S(1)} %fusion.369), custom_call_target="InvertDiagBlocksLowerTriangular" | custom-call | tf_op jit(solution)/shard_map/jvp()/while/body/eval_jaxpr/triangular_solve/custom-call.1 | solution.py:34
  42.8 19.7 %custom-call.29 = f32[2,1,128,128]{2,3,1,0:T(8,128)S(1)} custom-call(f32[2,1,128,128]{3,2,1,0:T(8,128)S(1)} %fusion.369), custom_call_target="InvertDiagBlocksLowerTriangular" | custom-call | tf_op jit(solution)/shard_map/jvp()/while/body/eval_jaxpr/triangular_solve/custom-call.1 | solution.py:34
  67.6 19.7 %custom-call.29 = f32[2,1,128,128]{2,3,1,0:T(8,128)S(1)} custom-call(f32[2,1,128,128]{3,2,1,0:T(8,128)S(1)} %fusion.369), custom_call_target="InvertDiagBlocksLowerTriangular" | custom-call | tf_op jit(solution)/shard_map/jvp()/while/body/eval_jaxpr/triangular_solve/custom-call.1 | solution.py:34
  92.4 19.7 %custom-call.29 = f32[2,1,128,128]{2,3,1,0:T(8,128)S(1)} custom-call(f32[2,1,128,128]{3,2,1,0:T(8,128)S(1)} %fusion.369), custom_call_target="InvertDiagBlocksLowerTriangular" | custom-call | tf_op jit(solution)/shard_map/jvp()/while/body/eval_jaxpr/triangular_solve/custom-call.1 | solution.py:34
  115.8 270.7 %while.111 = (s32[]{:T(128)}, f32[2,128,128]{2,1,0:T(8,128)S(1)}, f32[2,128,128]{2,1,0:T(8,128)S(1)}, f32[2,128,128]{2,1,0:T(8,128)S(1)}, s32[]{:T(128)}) while((s32[]{:T(128)}, f32[2,128,128]{2,1,0:T(8,128)S(1)}, f32[2,128,128]{2,1,0:T(8,128)S(1)}, f32[2,128,128]{2,1,0:T(8,128)S(1)}, s32[]{:T(128)}) %tuple.211), condition=%wide.region_5.7_spmd, body=%wide.region_4.6_spmd.sunk | while | flops 50364416 | bytes 1048677 | solution.py:153
  162.6 5.9 collective-permute-start
  223.3 6.0 collective-permute-start
  232.9 5.6 collective-permute-start
  274.7 6.0 collective-permute-start
  283.5 6.4 collective-permute-start
  292.7 6.3 collective-permute-start
  301.7 6.5 collective-permute-start
  311.0 6.9 collective-permute-start
  321.9 6.7 collective-permute-start
  331.7 6.3 collective-permute-start
  340.8 6.8 collective-permute-start
  350.4 6.2 collective-permute-start
  359.4 6.0 collective-permute-start
  368.2 6.5 collective-permute-start
  377.4 6.5 collective-permute-start
  390.6 116.4 %while.113 = (s32[]{:T(128)}, f32[2,128,128]{2,1,0:T(8,128)S(1)}, bf16[4,2,64,128]{3,2,1,0:T(8,128)(2,1)}, f32[4,2,128,1]{2,1,3,0:T(2,128)S(1)}, f32[4,2,128,128...) while((s32[]{:T(128)}, f32[2,128,128]{2,1,0:T(8,128)S(1)}, ...), condition=%wide.region_7.9_spmd.clone, body=%wide.region_6.8_spmd.clone.sunk | while | flops 327762048 | bytes 10093849 | solution.py:115
  393.7 19.7 %custom-call.27 = f32[2,1,128,128]{2,3,1,0:T(8,128)S(1)} custom-call(f32[2,1,128,128]{3,2,1,0:T(8,128)S(1)} %add_bitcast_fusion.4), custom_call_target="InvertDiagBlocksLowerTriangular" | custom-call | tf_op jit(solution)/shard_map/jvp()/while/body/eval_jaxpr/triangular_solve/custom-call.1 | solution.py:34
  422.8 19.7 %custom-call.27 = f32[2,1,128,128]{2,3,1,0:T(8,128)S(1)} custom-call(f32[2,1,128,128]{3,2,1,0:T(8,128)S(1)} %add_bitcast_fusion.4), custom_call_target="InvertDiagBlocksLowerTriangular" | custom-call | tf_op jit(solution)/shard_map/jvp()/while/body/eval_jaxpr/triangular_solve/custom-call.1 | solution.py:34
  451.9 19.7 %custom-call.27 = f32[2,1,128,128]{2,3,1,0:T(8,128)S(1)} custom-call(f32[2,1,128,128]{3,2,1,0:T(8,128)S(1)} %add_bitcast_fusion.4), custom_call_target="InvertDiagBlocksLowerTriangular" | custom-call | tf_op jit(solution)/shard_map/jvp()/while/body/eval_jaxpr/triangular_solve/custom-call.1 | solution.py:34
  481.0 19.7 %custom-call.27 = f32[2,1,128,128]{2,3,1,0:T(8,128)S(1)} custom-call(f32[2,1,128,128]{3,2,1,0:T(8,128)S(1)} %add_bitcast_fusion.4), custom_call_target="InvertDiagBlocksLowerTriangular" | custom-call | tf_op jit(solution)/shard_map/jvp()/while/body/eval_jaxpr/triangular_solve/custom-call.1 | solution.py:34
  515.1 13.5 %while.116 = (s32[]{:T(128)}, f32[2,128,128]{2,1,0:T(8,128)S(1)}, f32[4,2,64,128]{3,2,1,0:T(8,128)S(1)}, f32[4,2,64,128]{3,2,1,0:T(8,128)S(1)}, f32[4,2,128,128]...) while((s32[]{:T(128)}, f32[2,128,128]{2,1,0:T(8,128)S(1)}, ...), condition=%wide.region_10.12_spmd.clone, body=%wide.region_9.11_spmd.clone.sunk | while | flops 151191552 | bytes 1706635 | solution.py:115
  528.6 296.7 %while.112 = (s32[]{:T(128)}, f32[2,128,128]{2,1,0:T(8,128)S(1)}, f32[2,128,128]{2,1,0:T(8,128)S(1)}, f32[2,128,128]{2,1,0:T(8,128)S(1)}, s32[]{:T(128)}) while((s32[]{:T(128)}, f32[2,128,128]{2,1,0:T(8,128)S(1)}, f32[2,128,128]{2,1,0:T(8,128)S(1)}, f32[2,128,128]{2,1,0:T(8,128)S(1)}, s32[]{:T(128)}) %tuple.220), condition=%wide.region_12.14_spmd, body=%wide.region_11.13_spmd.sunk | while | flops 50364416 | bytes 1048677 | solution.py:154
  530.8 7.5 collective-permute-done.1
  540.5 8.6 collective-permute-done.1
  551.3 9.3 collective-permute-done.1
  562.8 7.2 collective-permute-done.1
  572.2 7.9 collective-permute-done.1
  582.3 6.2 collective-permute-done.1
  590.7 6.2 collective-permute-done.1
  599.2 7.1 collective-permute-done.1
  608.5 9.0 collective-permute-done.1
  619.6 8.9 collective-permute-done.1
  630.7 7.1 collective-permute-done.1
  640.0 6.6 collective-permute-done.1
  648.8 6.1 collective-permute-done.1
  657.1 6.7 collective-permute-done.1
  666.0 7.1 collective-permute-done.1
  675.3 8.7 collective-permute-done.1
  686.2 7.8 collective-permute-done.1
  696.3 8.5 collective-permute-done.1
  707.0 6.7 collective-permute-done.1
  715.9 6.1 collective-permute-done.1
  724.3 6.6 collective-permute-done.1
  733.0 7.3 collective-permute-done.1
  742.6 7.4 collective-permute-done.1
  752.2 9.4 collective-permute-done.1
  763.7 7.4 collective-permute-done.1
  773.3 6.6 collective-permute-done.1
  782.2 6.7 collective-permute-done.1
  791.1 6.4 collective-permute-done.1
  799.8 7.0 collective-permute-done.1
  809.0 7.0 collective-permute-done.1
  818.3 7.0 collective-permute-done.1
  827.7 157.6 %while.114 = (s32[]{:T(128)}, f32[2,128,128]{2,1,0:T(8,128)S(1)}, f32[4,2,64,128]{3,2,0,1:T(8,128)}, f32[4,2,128,128]{3,2,0,1:T(8,128)}, f32[4,2,128,128]{3,2,0,...) while((s32[]{:T(128)}, f32[2,128,128]{2,1,0:T(8,128)S(1)}, ...), condition=%wide.region_16.18_spmd.clone, body=%wide.region_13.17_spmd.clone.sunk | while | flops 705675136 | bytes 8299797 | solution.py:115
  841.4 20.5 %custom-call.28 = f32[2,1,128,128]{2,3,1,0:T(8,128)S(1)} custom-call(f32[2,1,128,128]{3,2,1,0:T(8,128)} %add_bitcast_fusion.5), custom_call_target="InvertDiagBlocksLowerTriangular" | custom-call | tf_op jit(solution)/shard_map/transpose(jvp())/while/body/eval_jaxpr/triangular_solve | solution.py:34
  880.9 20.5 %custom-call.28 = f32[2,1,128,128]{2,3,1,0:T(8,128)S(1)} custom-call(f32[2,1,128,128]{3,2,1,0:T(8,128)} %add_bitcast_fusion.5), custom_call_target="InvertDiagBlocksLowerTriangular" | custom-call | tf_op jit(solution)/shard_map/transpose(jvp())/while/body/eval_jaxpr/triangular_solve | solution.py:34
  920.3 20.5 %custom-call.28 = f32[2,1,128,128]{2,3,1,0:T(8,128)S(1)} custom-call(f32[2,1,128,128]{3,2,1,0:T(8,128)} %add_bitcast_fusion.5), custom_call_target="InvertDiagBlocksLowerTriangular" | custom-call | tf_op jit(solution)/shard_map/transpose(jvp())/while/body/eval_jaxpr/triangular_solve | solution.py:34
  959.7 20.5 %custom-call.28 = f32[2,1,128,128]{2,3,1,0:T(8,128)S(1)} custom-call(f32[2,1,128,128]{3,2,1,0:T(8,128)} %add_bitcast_fusion.5), custom_call_target="InvertDiagBlocksLowerTriangular" | custom-call | tf_op jit(solution)/shard_map/transpose(jvp())/while/body/eval_jaxpr/triangular_solve | solution.py:34
  (481 shorter events, 423.6 us)
Async XLA Ops:
  7.2 501.0 %all-gather.2.cloned.1.call-start = ((), (), s32[]{:S(2)}) async-start(), calls=%async_computation.3 | async-start | bytes 1179648 | tf_op jit(solution)/shard_map/all_gather | solution.py:123
  7.9 985.0 %reduce-scatter.5.cloned.1.call-start = ((), (), s32[]{:S(2)}) async-start(), calls=%async_computation.4 | async-start | bytes 1081344 | tf_op jit(solution)/shard_map/reduce_scatter | solution.py:172
  116.1 7.1 collective-permute-start
  130.6 6.9 collective-permute-start
  137.7 7.7 collective-permute-start
  145.7 8.1 collective-permute-start
  154.1 8.2 collective-permute-start
  162.6 9.8 collective-permute-start
  172.6 8.3 collective-permute-start
  181.2 7.6 collective-permute-start
  189.1 8.1 collective-permute-start
  197.4 8.1 collective-permute-start
  205.8 8.1 collective-permute-start
  214.1 8.9 collective-permute-start
  223.3 9.3 collective-permute-start
  232.9 8.2 collective-permute-start
  241.3 8.0 collective-permute-start
  249.6 8.1 collective-permute-start
  258.0 8.1 collective-permute-start
  266.3 8.1 collective-permute-start
  274.7 8.6 collective-permute-start
  283.5 8.9 collective-permute-start
  292.7 8.8 collective-permute-start
  301.7 9.0 collective-permute-start
  311.0 10.6 %collective-permute-start = (f32[2,128,128]{2,1,0:T(8,128)S(1)}, f32[2,128,128]{2,1,0:T(8,128)S(1)}, u32[]{:S(2)}, u32[]{:S(2)}) collective-permute-start(f32[2,128,128]{2,1,0:T(8,128)S(1)} %convolution_add_fusion.16), channel_id=1, source_target_pairs={{0,8},{8,16},{16,24},{24,32},{32,40},{40,48},{48,56},{56,64},{64,7... | collective-permute-start | bytes 393224 | tf_op jit(solution)/shard_map/while/body/eval_jaxpr/ppermute | solution.py:16
  321.9 9.5 collective-permute-start
  331.7 8.8 collective-permute-start
  340.8 9.3 collective-permute-start
  350.4 8.7 collective-permute-start
  359.4 8.5 collective-permute-start
  368.2 9.0 collective-permute-start
  377.4 9.0 collective-permute-start
  510.9 483.4 %reduce-scatter.3.cloned.1.call-start = ((), (), s32[]{:S(2)}) async-start(), calls=%async_computation.2 | async-start | bytes 2359296 | tf_op jit(solution)/shard_map/reduce_scatter | solution.py:167
  528.9 9.4 collective-permute-start.1
  538.6 10.5 %collective-permute-start.1 = (f32[2,128,128]{2,1,0:T(8,128)S(1)}, f32[2,128,128]{2,1,0:T(8,128)S(1)}, u32[]{:S(2)}, u32[]{:S(2)}) collective-permute-start(f32[2,128,128]{2,1,0:T(8,128)S(1)} %convolution_add_fusion.17), channel_id=1, source_target_pairs={{8,0},{16,8},{24,16},{32,24},{40,32},{48,40},{56,48},{64,56},{72,6... | collective-permute-start | bytes 393224 | tf_op jit(solution)/shard_map/while/body/eval_jaxpr/ppermute | solution.py:16
  549.4 11.3 %collective-permute-start.1 = (f32[2,128,128]{2,1,0:T(8,128)S(1)}, f32[2,128,128]{2,1,0:T(8,128)S(1)}, u32[]{:S(2)}, u32[]{:S(2)}) collective-permute-start(f32[2,128,128]{2,1,0:T(8,128)S(1)} %convolution_add_fusion.17), channel_id=1, source_target_pairs={{8,0},{16,8},{24,16},{32,24},{40,32},{48,40},{56,48},{64,56},{72,6... | collective-permute-start | bytes 393224 | tf_op jit(solution)/shard_map/while/body/eval_jaxpr/ppermute | solution.py:16
  560.9 9.1 collective-permute-start.1
  570.3 9.8 collective-permute-start.1
  580.4 8.1 collective-permute-start.1
  588.8 8.2 collective-permute-start.1
  597.2 9.0 collective-permute-start.1
  606.5 10.9 %collective-permute-start.1 = (f32[2,128,128]{2,1,0:T(8,128)S(1)}, f32[2,128,128]{2,1,0:T(8,128)S(1)}, u32[]{:S(2)}, u32[]{:S(2)}) collective-permute-start(f32[2,128,128]{2,1,0:T(8,128)S(1)} %convolution_add_fusion.17), channel_id=1, source_target_pairs={{8,0},{16,8},{24,16},{32,24},{40,32},{48,40},{56,48},{64,56},{72,6... | collective-permute-start | bytes 393224 | tf_op jit(solution)/shard_map/while/body/eval_jaxpr/ppermute | solution.py:16
  617.7 10.8 %collective-permute-start.1 = (f32[2,128,128]{2,1,0:T(8,128)S(1)}, f32[2,128,128]{2,1,0:T(8,128)S(1)}, u32[]{:S(2)}, u32[]{:S(2)}) collective-permute-start(f32[2,128,128]{2,1,0:T(8,128)S(1)} %convolution_add_fusion.17), channel_id=1, source_target_pairs={{8,0},{16,8},{24,16},{32,24},{40,32},{48,40},{56,48},{64,56},{72,6... | collective-permute-start | bytes 393224 | tf_op jit(solution)/shard_map/while/body/eval_jaxpr/ppermute | solution.py:16
  628.8 9.0 collective-permute-start.1
  638.1 8.5 collective-permute-start.1
  646.9 8.1 collective-permute-start.1
  655.2 8.6 collective-permute-start.1
  664.1 9.0 collective-permute-start.1
  673.4 10.7 %collective-permute-start.1 = (f32[2,128,128]{2,1,0:T(8,128)S(1)}, f32[2,128,128]{2,1,0:T(8,128)S(1)}, u32[]{:S(2)}, u32[]{:S(2)}) collective-permute-start(f32[2,128,128]{2,1,0:T(8,128)S(1)} %convolution_add_fusion.17), channel_id=1, source_target_pairs={{8,0},{16,8},{24,16},{32,24},{40,32},{48,40},{56,48},{64,56},{72,6... | collective-permute-start | bytes 393224 | tf_op jit(solution)/shard_map/while/body/eval_jaxpr/ppermute | solution.py:16
  684.3 9.8 collective-permute-start.1
  694.4 10.4 %collective-permute-start.1 = (f32[2,128,128]{2,1,0:T(8,128)S(1)}, f32[2,128,128]{2,1,0:T(8,128)S(1)}, u32[]{:S(2)}, u32[]{:S(2)}) collective-permute-start(f32[2,128,128]{2,1,0:T(8,128)S(1)} %convolution_add_fusion.17), channel_id=1, source_target_pairs={{8,0},{16,8},{24,16},{32,24},{40,32},{48,40},{56,48},{64,56},{72,6... | collective-permute-start | bytes 393224 | tf_op jit(solution)/shard_map/while/body/eval_jaxpr/ppermute | solution.py:16
  705.0 8.7 collective-permute-start.1
  714.0 8.1 collective-permute-start.1
  722.3 8.5 collective-permute-start.1
  731.1 9.3 collective-permute-start.1
  740.6 9.3 collective-permute-start.1
  750.2 11.3 %collective-permute-start.1 = (f32[2,128,128]{2,1,0:T(8,128)S(1)}, f32[2,128,128]{2,1,0:T(8,128)S(1)}, u32[]{:S(2)}, u32[]{:S(2)}) collective-permute-start(f32[2,128,128]{2,1,0:T(8,128)S(1)} %convolution_add_fusion.17), channel_id=1, source_target_pairs={{8,0},{16,8},{24,16},{32,24},{40,32},{48,40},{56,48},{64,56},{72,6... | collective-permute-start | bytes 393224 | tf_op jit(solution)/shard_map/while/body/eval_jaxpr/ppermute | solution.py:16
  761.8 9.3 collective-permute-start.1
  771.4 8.6 collective-permute-start.1
  780.3 8.7 collective-permute-start.1
  789.2 8.4 collective-permute-start.1
  797.9 9.0 collective-permute-start.1
  807.1 9.0 collective-permute-start.1
  816.3 9.0 collective-permute-start.1
  (15 other events, 547.5 us)
Sparse Core Ops, SparseCore 0:
  9.8 28.6 all-gather.1
  511.1 233.2 reduce-scatter.4
  746.9 35.4 reduce-scatter.2
where the time goes:
time: 1020 us; the launch traced here: 1000 us
  waiting for transfers between devices  313 us (31%)
  other arithmetic  257 us (25%)
  starting transfers between devices  238 us (23%)
  matrix products  135 us (13%)
  local copies, waits for them, and re-layouts  43.5 us (4%)
  between operations  14.1 us (1%)
    ppermute x62, waiting for transfers between devices, passed_along(): return lax.ppermute(shard, axis, pairs)  312 us
    another operation x48, other arithmetic, block_core(): lax.linalg.triangular_solve(system, right_side, left_side=True, lower=Tru...  247 us
    ppermute x62, starting transfers between devices, passed_along(): return lax.ppermute(shard, axis, pairs)  237 us
    dot_general x20, matrix products, block_core(): jnp.einsum('hnk,hvk->hnv', key_weights, carry_state, precision=HIGHEST_PR...  20.9 us
  transfers between devices with their start and end apart: 65, of which 62 were waited for; matrix products, arithmetic and copies ran while one was open for 43% of the time, Pallas kernels for 0%

commit v1 on v0

v1 whole, which is shorter than its diff:
```python
import jax
import jax.numpy as jnp
from jax import lax
from jax.experimental import pallas as pl
from jax.experimental.pallas import tpu as pltpu
from jax.sharding import PartitionSpec as P

HEAD_DIM = 128
BLOCK = 64
ROWS = 2 * BLOCK
f32 = jnp.float32
bf16 = jnp.bfloat16
NN = (((1,), (0,)), ((), ()))
NT = (((1,), (1,)), ((), ()))
TN = (((0,), (0,)), ((), ()))
VMEM_LIMIT = 48 * 1024 * 1024


def halves(x):
    high = x.astype(bf16)
    return high, (x - high.astype(f32)).astype(bf16)


def dot(a, b, dims):
    return lax.dot_general(a, b, dims, preferred_element_type=f32)


def product(a, b, dims=NN):
    ah, al = a if isinstance(a, tuple) else halves(a)
    bh, bl = b if isinstance(b, tuple) else halves(b)
    return dot(ah, bh, dims) + (dot(ah, bl, dims) + dot(al, bh, dims))


def inverse_norm(x):
    return lax.rsqrt(jnp.sum(x * x, axis=-1, keepdims=True) + 1e-06)


def strengths(logits):
    return 2.0 / (1.0 + jnp.exp(-logits))


def token_grid():
    row = lax.broadcasted_iota(jnp.int32, (ROWS, ROWS), 0)
    col = lax.broadcasted_iota(jnp.int32, (ROWS, ROWS), 1)
    return row & (BLOCK - 1), col & (BLOCK - 1), row >= BLOCK, col >= BLOCK


def load_pairs(ref, block):
    rows = pl.ds(block * BLOCK, BLOCK)
    return jnp.concatenate([ref[0, rows, :], ref[1, rows, :]], axis=0)


def prepare_kernel(key_ref, value_ref, logit_ref, system_ref, solved_ref, step_ref, prefix_ref):
    blocks = key_ref.shape[1] // BLOCK
    row_token, col_token, row_second, col_second = token_grid()
    row = lax.broadcasted_iota(jnp.int32, (ROWS, ROWS), 0)
    col = lax.broadcasted_iota(jnp.int32, (ROWS, ROWS), 1)
    same_token = row_token == col_token
    pair = same_token & row_second & ~col_second
    eye = row == col
    units, keys, grams, systems = [], [], [], []
    for block in range(blocks):
        key = load_pairs(key_ref, block)
        unit = key * inverse_norm(key)
        parts = halves(unit)
        units.append(unit)
        keys.append(parts)
        grams.append(product(parts, parts, NT))
    for block in range(blocks):
        strength = jnp.broadcast_to(strengths(logit_ref[0, pl.ds(block, 1), :]), (ROWS, ROWS))
        swapped = jnp.broadcast_to(strengths(logit_ref[0, pl.ds(blocks + block, 1), :]), (ROWS, ROWS))
        systems.append(
            jnp.where(eye, strength, 0.0) - jnp.where(pair, grams[block] * (strength * swapped), 0.0)
        )
    size = 1
    while size < BLOCK:
        below = ((row_token & size) != 0) & ((row_token ^ col_token) < 2 * size) & ((col_token & size) == 0)
        now = [halves(system) for system in systems]
        middle = [
            product(jnp.where(below, grams[block], 0.0), now[block]) for block in range(blocks)
        ]
        systems = [
            systems[block] - product(now[block], middle[block]) for block in range(blocks)
        ]
        size *= 2
    prefix = None
    steps = []
    for block in range(blocks):
        value = load_pairs(value_ref, block)
        system_ref[0, block] = systems[block]
        solved = product(systems[block], jnp.concatenate([units[block], value], axis=1))
        solved_ref[0, block] = solved
        moved = product(keys[block], solved, TN)
        steps.append(
            jnp.concatenate(
                [jnp.where(eye, 1.0, 0.0) - moved[:, :HEAD_DIM], moved[:, HEAD_DIM:]], axis=1
            )
        )
        step_ref[0, block] = steps[block][:, :HEAD_DIM]
    prefix = steps[0]
    prefix_ref[0, 0] = prefix
    for block in range(1, blocks):
        moved = product(steps[block][:, :HEAD_DIM], prefix)
        prefix = jnp.concatenate(
            [moved[:, :HEAD_DIM], moved[:, HEAD_DIM:] + steps[block][:, HEAD_DIM:]], axis=1
        )
        prefix_ref[0, block] = prefix


def local_kernel(query_ref, key_ref, solved_ref, step_ref, grad_ref, weight_ref, mixed_grad_ref, reach_ref, inner_ref, drive_ref, adjoint_ref):
    blocks = query_ref.shape[0] // BLOCK
    row = lax.broadcasted_iota(jnp.int32, (BLOCK, ROWS), 0)
    col = lax.broadcasted_iota(jnp.int32, (BLOCK, ROWS), 1)
    visible = (col & (BLOCK - 1)) <= row
    mixed_grad = dot(grad_ref[...], weight_ref[...], NT)
    mixed_grad_ref[...] = mixed_grad
    drives = []
    for block in range(blocks):
        rows = pl.ds(block * BLOCK, BLOCK)
        query = query_ref[rows, :]
        query = query * inverse_norm(query)
        key = load_pairs(key_ref, block)
        key = key * inverse_norm(key)
        scores = jnp.where(visible, product(query, key, NT), 0.0)
        seen = product(scores, solved_ref[0, block])
        reach = query - seen[:, :HEAD_DIM]
        reach_ref[0, block] = reach
        inner_ref[0, block] = seen[:, HEAD_DIM:]
        drive = product(reach, mixed_grad[block * BLOCK : (block + 1) * BLOCK], TN)
        drive_ref[0, block] = drive
        drives.append(drive)
    adjoint = drives[blocks - 1]
    for block in reversed(range(blocks - 1)):
        adjoint = product(step_ref[0, block], adjoint, TN) + drives[block]
    adjoint_ref[0] = adjoint


def mix_kernel(state_ref, prefix_ref, reach_ref, inner_ref, grad_ref, states_ref, mixed_ref, weight_grad_ref):
    blocks = prefix_ref.shape[1]
    start = state_ref[0]
    parts = halves(start)
    for block in range(blocks):
        state = start
        if block:
            before = prefix_ref[0, block - 1]
            state = product(before[:, :HEAD_DIM], parts) + before[:, HEAD_DIM:]
        states_ref[0, block] = state
        mixed = product(reach_ref[0, block], state) + inner_ref[0, block]
        mixed_ref[pl.ds(block * BLOCK, BLOCK), :] = mixed.astype(bf16)
    weight_grad_ref[...] = dot(mixed_ref[...], grad_ref[...], TN).astype(bf16)


def unit_pull(x, unit_grad):
    scale = inverse_norm(x)
    unit = x * scale
    return scale * (unit_grad - unit * jnp.sum(unit * unit_grad, axis=-1, keepdims=True))


def gradient_kernel(
    query_ref, key_ref, logit_ref, system_ref, solved_ref, step_ref, states_ref, drive_ref, mixed_grad_ref, adjoint_ref,
    query_grad_ref, key_grad_ref, value_grad_ref, logit_grad_ref,
):
    blocks = query_ref.shape[0] // BLOCK
    row = lax.broadcasted_iota(jnp.int32, (BLOCK, ROWS), 0)
    col = lax.broadcasted_iota(jnp.int32, (BLOCK, ROWS), 1)
    visible = (col & (BLOCK - 1)) <= row
    row_token, col_token, row_second, col_second = token_grid()
    earlier = (col_token < row_token) | ((col_token == row_token) & row_second & ~col_second)
    ones = jnp.ones((8, HEAD_DIM), bf16)
    adjoint = adjoint_ref[0]
    for block in reversed(range(blocks)):
        rows = pl.ds(block * BLOCK, BLOCK)
        query = query_ref[rows, :]
        key = load_pairs(key_ref, block)
        query_unit = halves(query * inverse_norm(query))
        key_unit = halves(key * inverse_norm(key))
        state = halves(states_ref[0, block])
        solved = solved_ref[0, block]
        fresh = solved[:, HEAD_DIM:] - product(solved[:, :HEAD_DIM], state)
        fresh_parts = halves(fresh)
        out_grad = halves(mixed_grad_ref[rows, :])
        after = halves(adjoint)
        scores = jnp.where(visible, product(query_unit, key_unit, NT), 0.0)
        fresh_grad = product(scores, out_grad, TN) + product(key_unit, after)
        value_grad = product(system_ref[0, block], fresh_grad, TN)
        value_parts = halves(value_grad)
        value_grad_ref[0, rows, :] = value_grad[:BLOCK]
        value_grad_ref[1, rows, :] = value_grad[BLOCK:]
        high, low = halves(value_grad * fresh)
        sums = dot(ones, high, NT) + dot(ones, low, NT)
        logit_grad_ref[0, pl.ds(block, 1), :] = (
            0.5 * jnp.exp(-logit_ref[0, pl.ds(block, 1), :]) * sums[0:1]
        )
        score_grad = halves(jnp.where(visible, product(out_grad, fresh_parts, NT), 0.0))
        query_unit_grad = product(out_grad, state, NT) + product(score_grad, key_unit)
        query_grad_ref[rows, :] = unit_pull(query, query_unit_grad)
        gram_grad = halves(jnp.where(earlier, product(value_parts, fresh_parts, NT), 0.0))
        key_unit_grad = (
            product(score_grad, query_unit, TN)
            + product(fresh_parts, after, NT)
            - product(value_parts, state, NT)
            - (product(gram_grad, key_unit) + product(gram_grad, key_unit, TN))
        )
        key_grad = unit_pull(key, key_unit_grad)
        key_grad_ref[0, rows, :] = key_grad[:BLOCK]
        key_grad_ref[1, rows, :] = key_grad[BLOCK:]
        if block:
            adjoint = product(step_ref[0, block], after, TN) + drive_ref[0, block]


def head_call(kernel, name, heads, outs, *operands):
    def spec(kind, shape):
        rank = len(shape)
        if kind == "first":
            return pl.BlockSpec((1, *shape[1:]), lambda h: (h,) + (0,) * (rank - 1))
        if kind == "last":
            return pl.BlockSpec((*shape[:-1], HEAD_DIM), lambda h: (0,) * (rank - 1) + (h,))
        if kind == "rows":
            return pl.BlockSpec((HEAD_DIM, *shape[1:]), lambda h: (h,) + (0,) * (rank - 1))
        return pl.BlockSpec(shape, lambda h: (0,) * rank)

    return pl.pallas_call(
        kernel,
        name=name,
        grid=(heads,),
        in_specs=[spec(kind, array.shape) for kind, array in operands],
        out_specs=[spec(kind, shape) for kind, shape, _ in outs],
        out_shape=[jax.ShapeDtypeStruct(shape, dtype) for _, shape, dtype in outs],
        compiler_params=pltpu.CompilerParams(
            dimension_semantics=("arbitrary",), vmem_limit_bytes=VMEM_LIMIT
        ),
    )(*[array for _, array in operands])


def shifted(array, by):
    count = lax.axis_size("seq")
    pairs = [(i, i + by) for i in range(count) if 0 <= i + by < count]
    return lax.ppermute(array, "seq", pairs)


def joined(later, earlier):
    moved = jnp.einsum(
        "hab,hbn->han", later[:, :, :HEAD_DIM], earlier, precision=lax.Precision.HIGHEST
    )
    return moved + jnp.concatenate([jnp.zeros_like(moved[:, :, :HEAD_DIM]), later[:, :, HEAD_DIM:]], axis=2)


def arriving(own, sign):
    count = lax.axis_size("seq")
    distance = 1
    while distance < count // 2:
        own = joined(own, shifted(own, sign * distance))
        distance *= 2
    near = shifted(own, sign)
    if count == 1:
        return near[:, :, HEAD_DIM:]
    far = shifted(own[:, :, HEAD_DIM:], sign * (count // 2 + 1))
    return near[:, :, HEAD_DIM:] + jnp.einsum(
        "hab,hbn->han", near[:, :, :HEAD_DIM], far, precision=lax.Precision.HIGHEST
    )


def gathered(array, axis):
    copies = jnp.broadcast_to(array[None], (lax.axis_size(axis), *array.shape))
    return lax.all_to_all(copies, axis, 0, 0, tiled=True)


def project_kernel(mixed_ref, weight_ref, out_ref):
    total = dot(mixed_ref[0], weight_ref[0], NN)
    for part in range(1, mixed_ref.shape[0]):
        total = total + dot(mixed_ref[part], weight_ref[part], NN)
    out_ref[...] = total.astype(bf16)


def body(queries, reflect_keys, reflect_values, beta_logit, out_weight, out_grad):
    tokens, features = queries.shape
    heads = features // HEAD_DIM
    blocks = tokens // BLOCK
    square = (heads, blocks, ROWS, HEAD_DIM)
    double = (heads, blocks, ROWS, 2 * HEAD_DIM)
    keys = reflect_keys.transpose(1, 0, 2)
    values = reflect_values.transpose(1, 0, 2)
    logits = beta_logit.reshape(2, heads, blocks, BLOCK).transpose(1, 2, 0, 3)
    logit_rows = jnp.concatenate(
        [logits.reshape(heads, blocks, ROWS), logits[:, :, ::-1].reshape(heads, blocks, ROWS)], axis=1
    )
    parts = lax.axis_size("head")
    grad_parts = gathered(out_grad, "head")
    weight_parts = lax.all_to_all(
        out_weight.reshape(features, parts, features).transpose(1, 0, 2), "head", 0, 0, tiled=True
    )
    full_grad = grad_parts.transpose(1, 0, 2).reshape(tokens, parts * features)

    system, solved, step, prefix = head_call(
        prepare_kernel,
        "prepare",
        heads,
        [("first", square, f32), ("first", double, f32), ("first", square, f32), ("first", double, f32)],
        ("last", keys),
        ("last", values),
        ("first", logit_rows),
    )
    whole = prefix[:, -1]
    state_in = arriving(whole, 1)
    mixed_grad, reach, inner, drive, adjoint = head_call(
        local_kernel,
        "local",
        heads,
        [
            ("last", (tokens, features), f32),
            ("first", (heads, blocks, BLOCK, HEAD_DIM), f32),
            ("first", (heads, blocks, BLOCK, HEAD_DIM), f32),
            ("first", square, f32),
            ("first", (heads, ROWS, HEAD_DIM), f32),
        ],
        ("last", queries),
        ("last", keys),
        ("first", solved),
        ("first", step),
        ("whole", full_grad),
        ("rows", out_weight),
    )
    adjoint_in = arriving(
        jnp.concatenate([jnp.swapaxes(whole[:, :, :HEAD_DIM], 1, 2), adjoint], axis=2), -1
    )
    states, mixed, weight_share = head_call(
        mix_kernel,
        "mix",
        heads,
        [("first", square, f32), ("last", (tokens, features), bf16), ("rows", out_weight.shape, bf16)],
        ("first", state_in),
        ("first", prefix),
        ("first", reach),
        ("first", inner),
        ("whole", full_grad),
    )
    seq_count = lax.axis_size("seq")
    weight_grad = jnp.sum(
        lax.all_to_all(
            weight_share.reshape(seq_count, features // seq_count, out_weight.shape[1]), "seq", 0, 0, tiled=True
        ).astype(f32),
        axis=0,
    )
    output = pl.pallas_call(
        project_kernel,
        name="project",
        out_shape=jax.ShapeDtypeStruct((tokens, features), bf16),
        compiler_params=pltpu.CompilerParams(vmem_limit_bytes=VMEM_LIMIT),
    )(gathered(mixed, "head"), weight_parts)
    query_grad, key_grad, value_grad, logit_grad = head_call(
        gradient_kernel,
        "gradients",
        heads,
        [
            ("last", queries.shape, f32),
            ("last", keys.shape, f32),
            ("last", values.shape, f32),
            ("first", (heads, blocks, ROWS), f32),
        ],
        ("last", queries),
        ("last", keys),
        ("first", logit_rows),
        ("first", system),
        ("first", solved),
        ("first", step),
        ("first", states),
        ("first", drive),
        ("last", mixed_grad),
        ("first", adjoint_in),
    )
    logit_grad = logit_grad.reshape(heads, blocks, 2, BLOCK).transpose(2, 0, 1, 3).reshape(beta_logit.shape)
    return (
        output,
        query_grad,
        key_grad.transpose(1, 0, 2),
        value_grad.transpose(1, 0, 2),
        logit_grad,
        weight_grad,
    )


def solution(mesh):
    in_specs = (
        P("seq", "head"),
        P("seq", None, "head"),
        P("seq", None, "head"),
        P(None, "head", "seq"),
        P("head", None),
        P("seq", "head"),
    )
    out_specs = (
        P("seq", "head"),
        P("seq", "head"),
        P("seq", None, "head"),
        P("seq", None, "head"),
        P(None, "head", "seq"),
        P(("head", "seq"), None),
    )
    return jax.shard_map(body, mesh=mesh, in_specs=in_specs, out_specs=out_specs, check_vma=False)
```

time: 1020 us -> 223 us (0.22); the launches traced: 1000 us -> 222 us
  other arithmetic: 257 us -> 3.71 us
  waiting for transfers between devices: 313 us -> 86.6 us
  starting transfers between devices: 238 us -> 77.8 us
  matrix products: 135 us -> 7.21 us
  Pallas kernels: 0 us -> 26.7 us
  local copies, waits for them, and re-layouts: 43.5 us -> 18.8 us
  between operations: 14.1 us -> 1.06 us
    another operation x51 -> x0, other arithmetic: 247 us -> none  [the longest x48 247 us: block_core(): lax.linalg.triangular_solve(system, right_side, left_side=True, lower=Tru...]
    ppermute x62 -> x12, waiting for transfers between devices: 312 us -> 75 us  [shifted(): return lax.ppermute(array, 'seq', pairs)]
    ppermute x62 -> x12, starting transfers between devices: 237 us -> 53.1 us  [shifted(): return lax.ppermute(array, 'seq', pairs)]
    dot_general x181 -> x10, matrix products: 117 us -> 7.21 us  [the longest x8 6.68 us: joined(): jnp.einsum('hab,hbn->han', later[:, :, :HEAD_DIM], earlier, precision=lax...]
    pallas_call x0 -> x5, Pallas kernels: none -> 26.7 us  [the longest x4 24.4 us: head_call(): pl.pallas_call(kernel, name=name, grid=(heads,), in_specs=[spec(kind, arr...]
    all_to_all x0 -> x4, starting transfers between devices: none -> 24.6 us  [the longest x1 11.3 us: body(): lax.all_to_all(weight_share.reshape(seq_count, features // seq_count, out...]
    another operation x16 -> x0, matrix products: 17.7 us -> none  [block_core(): lax.linalg.triangular_solve(system, right_side, left_side=True, lower=Tru...]
    all_to_all x0 -> x4, waiting for transfers between devices: none -> 11.6 us  [the longest x2 11.6 us: gathered(): return lax.all_to_all(copies, axis, 0, 0, tiled=True)]
  transfers between devices with their start and end apart: 65 -> 16, of which waited for: 62 -> 8; matrix products, arithmetic and copies ran while one was open for 43% -> 9% of each run, Pallas kernels for 0% -> 9%
where the time goes in v1:
time: 223 us; the launch traced here: 222 us
  waiting for transfers between devices  86.6 us (39%)
  starting transfers between devices  77.8 us (35%)
  Pallas kernels  26.7 us (12%)
  local copies, waits for them, and re-layouts  18.8 us (8%)
  matrix products  7.21 us (3%)
  other arithmetic  3.71 us (2%)
    ppermute x12, waiting for transfers between devices, shifted(): return lax.ppermute(array, 'seq', pairs)  75 us
    ppermute x12, starting transfers between devices, shifted(): return lax.ppermute(array, 'seq', pairs)  53.1 us
    pallas_call x4, Pallas kernels, head_call(): pl.pallas_call(kernel, name=name, grid=(heads,), in_specs=[spec(kind, arr...  24.4 us
    all_to_all x2, waiting for transfers between devices, gathered(): return lax.all_to_all(copies, axis, 0, 0, tiled=True)  11.6 us
    all_to_all x1, starting transfers between devices, body(): lax.all_to_all(weight_share.reshape(seq_count, features // seq_count, out...  11.3 us
    all_to_all x2, starting transfers between devices, gathered(): return lax.all_to_all(copies, axis, 0, 0, tiled=True)  9.1 us
    unnamed x33, local copies, waits for them, and re-layouts  7.52 us
    dot_general x8, matrix products, joined(): jnp.einsum('hab,hbn->han', later[:, :, :HEAD_DIM], earlier, precision=lax...  6.68 us
  transfers between devices with their start and end apart: 16, of which 8 were waited for; matrix products, arithmetic and copies ran while one was open for 9% of the time, Pallas kernels for 9%

profile of v1, /device:TPU:32, one launch (start us, length us, event | category | flops | bytes accessed | tf_op | source)
XLA Modules:
  0.0 221.8 jit_solution(16119271379835695772)
XLA Ops:
  0.6 0.8 reshape.38
  1.4 0.1 reshape.39
  1.5 0.1 reshape.40
  1.6 1.3 copy_bitcast_fusion
  2.9 7.6 %prepare.1 = (f32[2,4,128,128]{3,2,1,0:T(8,128)S(1)}, f32[2,4,128,256]{3,2,1,0:T(8,128)S(1)}, f32[2,4,128,128]{3,2,1,0:T(8,128)S(1)}, f32[2,4,128,256]{3,2,1,0:T(8,128)S(1)}) custom-call(f32[2,256,256]{2,1,0:T(8,128)S(1)} %get-tuple-element.59.key_ref, f32[2,256,256]{2,1,0:T(8,128)S(1)} %get-tuple-element.58.value_ref, ...), custom_call_target="tpu_custom_call" | custom-call | tf_op jit(solution)/shard_map/prepare/pallas_call | solution.py:222
  10.5 0.0 copy-start.5
  10.5 0.8 copy-done.5
  11.3 4.0 %collective-permute-start = (f32[2,128,256]{2,1,0:T(8,128)S(1)}, f32[2,128,256]{2,1,0:T(8,128)S(1)}, u32[]{:S(2)}, u32[]{:S(2)}) collective-permute-start(f32[2,128,256]{2,1,0:T(8,128)S(1)} %slice_bitcast_fusion), channel_id=1, source_target_pairs={{0,8},{8,16},{16,24},{24,32},{32,40},{40,48},{48,56},{56,64},{64,7... | collective-permute-start | bytes 786440 | tf_op jit(solution)/shard_map/ppermute | solution.py:238
  15.3 0.7 slice_bitcast_fusion.1
  16.0 5.4 %collective-permute-done = f32[2,128,256]{2,1,0:T(8,128)S(1)} collective-permute-done((f32[2,128,256]{2,1,0:T(8,128)S(1)}, f32[2,128,256]{2,1,0:T(8,128)S(1)}, u32[]{:S(2)}, u32[]{:S(2)}) %collective-permute-start) | collective-permute-done | bytes 262176 | tf_op jit(solution)/shard_map/ppermute | solution.py:238
  21.4 1.1 convolution_add_fusion.7
  22.5 6.5 %collective-permute-start.1 = (f32[2,128,256]{2,1,0:T(8,128)}, f32[2,128,256]{2,1,0:T(8,128)}, u32[]{:S(2)}, u32[]{:S(2)}) collective-permute-start(f32[2,128,256]{2,1,0:T(8,128)} %convolution_add_fusion.7), channel_id=1, source_target_pairs={{0,16},{8,24},{16,32},{24,40},{32,48},{40,56},{48,64},{56,72},{64,... | collective-permute-start | bytes 786440 | tf_op jit(solution)/shard_map/ppermute | solution.py:238
  29.0 1.0 broadcast_in_dim.4
  30.0 4.3 %all-to-all-start = ((bf16[8,256,256]{2,1,0:T(8,128)(2,1)}), bf16[8,256,256]{2,1,0:T(8,128)(2,1)}, u32[]{:S(2)}, u32[]{:S(2)}) async-start(bf16[8,256,256]{2,1,0:T(8,128)(2,1)} %broadcast_in_dim.4), calls=%async_computation | async-start | bytes 2097152 | tf_op jit(solution)/shard_map/all_to_all | solution.py:265
  34.3 1.0 slice.89
  35.3 0.6 collective-permute-done.1
  35.9 1.4 convolution_add_fusion.6
  37.3 7.5 %collective-permute-start.2 = (f32[2,128,256]{2,1,0:T(8,128)S(1)}, f32[2,128,256]{2,1,0:T(8,128)S(1)}, u32[]{:S(2)}, u32[]{:S(2)}) collective-permute-start(f32[2,128,256]{2,1,0:T(8,128)S(1)} %convolution_add_fusion.6), channel_id=1, source_target_pairs={{0,32},{8,40},{16,48},{24,56},{32,64},{40,72},{48,80},{56,88},{64,... | collective-permute-start | bytes 786440 | tf_op jit(solution)/shard_map/ppermute | solution.py:238
  44.9 3.9 %collective-permute-done.2 = f32[2,128,256]{2,1,0:T(8,128)S(1)} collective-permute-done((f32[2,128,256]{2,1,0:T(8,128)S(1)}, f32[2,128,256]{2,1,0:T(8,128)S(1)}, u32[]{:S(2)}, u32[]{:S(2)}) %collective-permute-start.2) | collective-permute-done | bytes 262176 | tf_op jit(solution)/shard_map/ppermute | solution.py:238
  48.8 0.4 convolution_add_fusion.5
  49.1 7.7 %collective-permute-start.3 = (f32[2,128,256]{2,1,0:T(8,128)S(1)}, f32[2,128,256]{2,1,0:T(8,128)}, u32[]{:S(2)}, u32[]{:S(2)}) collective-permute-start(f32[2,128,256]{2,1,0:T(8,128)S(1)} %convolution_add_fusion.5), channel_id=1, source_target_pairs={{0,64},{8,72},{16,80},{24,88},{32,96},{40,104},{48,112},{56,120},{... | collective-permute-start | bytes 786440 | tf_op jit(solution)/shard_map/ppermute | solution.py:238
  56.9 1.3 copy.39
  58.2 2.3 %copy.40 = bf16[256,8,256]{2,0,1:T(8,128)(2,1)} copy(bf16[256,8,256]{0,2,1:T(8,128)(2,1)} %bitcast.36) | data formatting | bytes 2097152 | tf_op jit(solution)/shard_map/reshape | solution.py:290
  60.5 4.2 %all-to-all-start.2 = ((bf16[8,256,256]{2,1,0:T(8,128)(2,1)}), bf16[8,256,256]{2,1,0:T(8,128)(2,1)}, u32[]{:S(2)}, u32[]{:S(2)}) async-start(bf16[8,256,256]{2,1,0:T(8,128)(2,1)} %bitcast.35), calls=%async_computation.2 | async-start | bytes 2097152 | tf_op jit(solution)/shard_map/all_to_all | solution.py:289
  64.8 1.3 convolution_add_fusion.4
  66.1 7.5 %collective-permute-start.4 = (f32[2,128,256]{2,1,0:T(8,128)S(1)}, f32[2,128,256]{2,1,0:T(8,128)S(1)}, u32[]{:S(2)}, u32[]{:S(2)}) collective-permute-start(f32[2,128,256]{2,1,0:T(8,128)S(1)} %convolution_add_fusion.4), channel_id=1, source_target_pairs={{0,8},{8,16},{16,24},{24,32},{32,40},{40,48},{48,56},{56,64},{64,7... | collective-permute-start | bytes 786440 | tf_op jit(solution)/shard_map/ppermute | solution.py:238
  73.6 7.1 %collective-permute-start.5 = (f32[2,128,128]{2,1,0:T(8,128)S(1)}, f32[2,128,128]{2,1,0:T(8,128)S(1)}, u32[]{:S(2)}, u32[]{:S(2)}) collective-permute-start(f32[2,128,128]{2,1,0:T(8,128)S(1)} %slice.96), channel_id=1, source_target_pairs={{0,136},{8,144},{16,152},{24,160},{32,168},{40,176},{48,184},{56,1... | collective-permute-start | bytes 393224 | tf_op jit(solution)/shard_map/ppermute | solution.py:238
  80.7 0.0 copy-start.3
  80.8 1.4 copy.49
  82.2 5.3 %local.1 = (f32[256,256]{1,0:T(8,128)S(1)}, f32[2,4,64,128]{3,2,1,0:T(8,128)S(1)}, f32[2,4,64,128]{3,2,1,0:T(8,128)S(1)}, f32[2,4,128,128]{3,2,1,0:T(8,128)S(1)}, f32[2,128,128]{2,1,0:T(8,128)S(1)}) custom-call(f32[256,256]{1,0:T(8,128)S(1)} %copy-done.3, f32[2,256,256]{2,1,0:T(8,128)S(1)} %get-tuple-element.59.key_ref, ...), custom_call_target="tpu_custom_call" | custom-call | tf_op jit(solution)/shard_map/local/pallas_call | solution.py:222
  87.5 0.8 copy-done.7
  88.3 0.3 slice_add_fusion.1.state_ref
  88.5 0.4 copy-done.11
  88.9 1.7 mix.1
  90.6 1.0 copy-done.4
  91.6 0.8 copy-done.9
  92.4 1.1 broadcast_in_dim.5
  93.4 4.8 %all-to-all-start.1 = ((bf16[8,256,256]{2,1,0:T(8,128)(2,1)}), bf16[8,256,256]{2,1,0:T(8,128)(2,1)S(1)}, u32[]{:S(2)}, u32[]{:S(2)}) async-start(bf16[8,256,256]{2,1,0:T(8,128)(2,1)} %broadcast_in_dim.5), calls=%async_computation.1 | async-start | bytes 2097152 | tf_op jit(solution)/shard_map/all_to_all | solution.py:265
  98.2 0.8 copy.41
  99.0 1.7 pad_maximum_fusion
  100.7 1.9 collective-permute-start.6
  102.6 11.6 %all-to-all-done.1.mixed_ref = bf16[8,256,256]{2,1,0:T(8,128)(2,1)S(1)} async-done(((bf16[8,256,256]{2,1,0:T(8,128)(2,1)}), bf16[8,256,256]{2,1,0:T(8,128)(2,1)S(1)}, u32[]{:S(2)}, u32[]{:S(2)}) %all-to-all-start.1) | async-done | bytes 1048608 | tf_op jit(solution)/shard_map/all_to_all | solution.py:265
  114.2 11.3 %all-to-all-start.3 = ((bf16[32,8,2048]{2,1,0:T(8,128)(2,1)}), bf16[32,8,2048]{2,1,0:T(8,128)(2,1)}, u32[]{:S(2)}, u32[]{:S(2)}) async-start(bf16[32,8,2048]{2,1,0:T(8,128)(2,1)} %bitcast.32), calls=%async_computation.3 | async-start | bytes 2097152 | tf_op jit(solution)/shard_map/all_to_all | solution.py:339
  125.5 1.4 convolution_add_fusion.3
  127.0 1.3 collective-permute-start.7
  128.3 28.4 %collective-permute-done.7 = f32[2,128,256]{2,1,0:T(8,128)S(1)} collective-permute-done((f32[2,128,256]{2,1,0:T(8,128)S(1)}, f32[2,128,256]{2,1,0:T(8,128)S(1)}, u32[]{:S(2)}, u32[]{:S(2)}) %collective-permute-start.7) | collective-permute-done | bytes 262176 | tf_op jit(solution)/shard_map/ppermute | solution.py:238
  156.7 0.4 convolution_add_fusion.2
  157.1 1.3 collective-permute-start.8
  158.4 14.1 %collective-permute-done.8 = f32[2,128,256]{2,1,0:T(8,128)S(1)} collective-permute-done((f32[2,128,256]{2,1,0:T(8,128)S(1)}, f32[2,128,256]{2,1,0:T(8,128)S(1)}, u32[]{:S(2)}, u32[]{:S(2)}) %collective-permute-start.8) | collective-permute-done | bytes 262176 | tf_op jit(solution)/shard_map/ppermute | solution.py:238
  172.5 0.4 convolution_add_fusion.1
  172.9 1.4 collective-permute-start.9
  174.4 6.9 %collective-permute-done.9 = f32[2,128,256]{2,1,0:T(8,128)S(1)} collective-permute-done((f32[2,128,256]{2,1,0:T(8,128)S(1)}, f32[2,128,256]{2,1,0:T(8,128)S(1)}, u32[]{:S(2)}, u32[]{:S(2)}) %collective-permute-start.9) | collective-permute-done | bytes 262176 | tf_op jit(solution)/shard_map/ppermute | solution.py:238
  181.3 0.4 convolution_add_fusion
  181.7 5.3 %collective-permute-start.10 = (f32[2,128,256]{2,1,0:T(8,128)S(1)}, f32[2,128,256]{2,1,0:T(8,128)S(1)}, u32[]{:S(2)}, u32[]{:S(2)}) collective-permute-start(f32[2,128,256]{2,1,0:T(8,128)S(1)} %convolution_add_fusion), channel_id=1, source_target_pairs={{8,0},{16,8},{24,16},{32,24},{40,32},{48,40},{56,48},{64,56},{72,6... | collective-permute-start | bytes 786440 | tf_op jit(solution)/shard_map/ppermute | solution.py:238
  187.0 1.5 collective-permute-start.11
  188.5 15.6 %collective-permute-done.11 = f32[2,128,128]{2,1,0:T(8,128)S(1)} collective-permute-done((f32[2,128,128]{2,1,0:T(8,128)S(1)}, f32[2,128,128]{2,1,0:T(8,128)S(1)}, u32[]{:S(2)}, u32[]{:S(2)}) %collective-permute-start.11) | collective-permute-done | bytes 131104 | tf_op jit(solution)/shard_map/ppermute | solution.py:238
  204.1 0.3 slice_add_fusion.adjoint_ref
  204.4 9.9 %gradients.1 = (f32[256,256]{1,0:T(8,128)}, f32[2,256,256]{2,1,0:T(8,128)S(1)}, f32[2,256,256]{2,1,0:T(8,128)S(1)}, f32[2,4,128]{2,1,0:T(4,128)S(1)}) custom-call(f32[256,256]{1,0:T(8,128)S(1)} %copy-done.3, f32[2,256,256]{2,1,0:T(8,128)S(1)} %get-tuple-element.59.key_ref, f32[2,8,128]{2,1,0:T(8,128)S(1)} %pad_maximum_fusion.1.logit_ref, ...), custom_call_target="tpu_custom_call" | custom-call | tf_op jit(solution)/shard_map/gradients/pallas_call | solution.py:222
  214.3 1.2 copy.45
  215.5 1.2 copy.46
  216.7 0.1 reshape.43
  216.8 0.7 reshape.44
  217.5 2.3 %project.1 = bf16[256,256]{1,0:T(8,128)(2,1)} custom-call(bf16[8,256,256]{2,1,0:T(8,128)(2,1)S(1)} %all-to-all-done.1.mixed_ref, bf16[8,256,256]{2,1,0:T(8,128)(2,1)} %all-to-all-done.2.weight_ref), custom_call_target="tpu_custom_call" | custom-call | tf_op jit(solution)/shard_map/project/pallas_call | solution.py:344
  219.8 2.0 convert_reduce_fusion
  (43 shorter events, 0.2 us)
Async XLA Ops:
  10.5 0.8 copy-start.5
  11.3 18.8 %copy-start.1 = (f32[2,4,128,256]{3,2,1,0:T(8,128)}, f32[2,4,128,256]{3,2,1,0:T(8,128)S(1)}, u32[]{:S(2)}) copy-start(f32[2,4,128,256]{3,2,1,0:T(8,128)S(1)} %get-tuple-element.22.prefix_ref) | copy-start | bytes 3145732
  11.3 17.7 %copy-start.14 = (bf16[256,256]{1,0:T(8,128)(2,1)S(1)}, bf16[256,256]{1,0:T(8,128)(2,1)}, u32[]{:S(2)}) copy-start(bf16[256,256]{1,0:T(8,128)(2,1)} %param.11) | copy-start | bytes 393220
  11.3 10.1 %copy-start.13 = (f32[2,128,256]{2,1,0:T(8,128)}, f32[2,128,256]{2,1,0:T(8,128)S(1)}, u32[]{:S(2)}) copy-start(f32[2,128,256]{2,1,0:T(8,128)S(1)} %slice_bitcast_fusion) | copy-start | bytes 786436
  11.3 10.1 %collective-permute-start = (f32[2,128,256]{2,1,0:T(8,128)S(1)}, f32[2,128,256]{2,1,0:T(8,128)S(1)}, u32[]{:S(2)}, u32[]{:S(2)}) collective-permute-start(f32[2,128,256]{2,1,0:T(8,128)S(1)} %slice_bitcast_fusion), channel_id=1, source_target_pairs={{0,8},{8,16},{16,24},{24,32},{32,40},{40,48},{48,56},{56,64},{64,7... | collective-permute-start | bytes 786440 | tf_op jit(solution)/shard_map/ppermute | solution.py:238
  22.5 13.4 %collective-permute-start.1 = (f32[2,128,256]{2,1,0:T(8,128)}, f32[2,128,256]{2,1,0:T(8,128)}, u32[]{:S(2)}, u32[]{:S(2)}) collective-permute-start(f32[2,128,256]{2,1,0:T(8,128)} %convolution_add_fusion.7), channel_id=1, source_target_pairs={{0,16},{8,24},{16,32},{24,40},{32,48},{40,56},{48,64},{56,72},{64,... | collective-permute-start | bytes 786440 | tf_op jit(solution)/shard_map/ppermute | solution.py:238
  30.0 30.4 %all-to-all-start = ((bf16[8,256,256]{2,1,0:T(8,128)(2,1)}), bf16[8,256,256]{2,1,0:T(8,128)(2,1)}, u32[]{:S(2)}, u32[]{:S(2)}) async-start(bf16[8,256,256]{2,1,0:T(8,128)(2,1)} %broadcast_in_dim.4), calls=%async_computation | async-start | bytes 2097152 | tf_op jit(solution)/shard_map/all_to_all | solution.py:265
  34.3 22.6 %copy-start = (bf16[256,2048]{1,0:T(8,128)(2,1)S(1)}, bf16[256,2048]{1,0:T(8,128)(2,1)}, u32[]{:S(2)}) copy-start(bf16[256,2048]{1,0:T(8,128)(2,1)} %weight_ref.1) | copy-start | bytes 3145732
  37.3 11.5 %collective-permute-start.2 = (f32[2,128,256]{2,1,0:T(8,128)S(1)}, f32[2,128,256]{2,1,0:T(8,128)S(1)}, u32[]{:S(2)}, u32[]{:S(2)}) collective-permute-start(f32[2,128,256]{2,1,0:T(8,128)S(1)} %convolution_add_fusion.6), channel_id=1, source_target_pairs={{0,32},{8,40},{16,48},{24,56},{32,64},{40,72},{48,80},{56,88},{64,... | collective-permute-start | bytes 786440 | tf_op jit(solution)/shard_map/ppermute | solution.py:238
  49.1 15.6 %collective-permute-start.3 = (f32[2,128,256]{2,1,0:T(8,128)S(1)}, f32[2,128,256]{2,1,0:T(8,128)}, u32[]{:S(2)}, u32[]{:S(2)}) collective-permute-start(f32[2,128,256]{2,1,0:T(8,128)S(1)} %convolution_add_fusion.5), channel_id=1, source_target_pairs={{0,64},{8,72},{16,80},{24,88},{32,96},{40,104},{48,112},{56,120},{... | collective-permute-start | bytes 786440 | tf_op jit(solution)/shard_map/ppermute | solution.py:238
  60.5 31.9 %all-to-all-start.2 = ((bf16[8,256,256]{2,1,0:T(8,128)(2,1)}), bf16[8,256,256]{2,1,0:T(8,128)(2,1)}, u32[]{:S(2)}, u32[]{:S(2)}) async-start(bf16[8,256,256]{2,1,0:T(8,128)(2,1)} %bitcast.35), calls=%async_computation.2 | async-start | bytes 2097152 | tf_op jit(solution)/shard_map/all_to_all | solution.py:289
  66.1 22.2 %collective-permute-start.4 = (f32[2,128,256]{2,1,0:T(8,128)S(1)}, f32[2,128,256]{2,1,0:T(8,128)S(1)}, u32[]{:S(2)}, u32[]{:S(2)}) collective-permute-start(f32[2,128,256]{2,1,0:T(8,128)S(1)} %convolution_add_fusion.4), channel_id=1, source_target_pairs={{0,8},{8,16},{16,24},{24,32},{32,40},{40,48},{48,56},{56,64},{64,7... | collective-permute-start | bytes 786440 | tf_op jit(solution)/shard_map/ppermute | solution.py:238
  73.6 14.7 %collective-permute-start.5 = (f32[2,128,128]{2,1,0:T(8,128)S(1)}, f32[2,128,128]{2,1,0:T(8,128)S(1)}, u32[]{:S(2)}, u32[]{:S(2)}) collective-permute-start(f32[2,128,128]{2,1,0:T(8,128)S(1)} %slice.96), channel_id=1, source_target_pairs={{0,136},{8,144},{16,152},{24,160},{32,168},{40,176},{48,184},{56,1... | collective-permute-start | bytes 393224 | tf_op jit(solution)/shard_map/ppermute | solution.py:238
  80.7 1.4 copy-start.3
  82.2 6.8 %copy-start.2 = (f32[2,4,128,256]{3,2,1,0:T(8,128)S(1)}, f32[2,4,128,256]{3,2,1,0:T(8,128)}, u32[]{:S(2)}) copy-start(f32[2,4,128,256]{3,2,1,0:T(8,128)} %copy-done.1) | copy-start | bytes 3145732
  87.4 0.8 copy-start.7
  88.2 0.7 copy-start.11
  90.6 1.0 copy-start.4
  91.6 0.8 copy-start.9
  93.4 20.8 %all-to-all-start.1 = ((bf16[8,256,256]{2,1,0:T(8,128)(2,1)}), bf16[8,256,256]{2,1,0:T(8,128)(2,1)S(1)}, u32[]{:S(2)}, u32[]{:S(2)}) async-start(bf16[8,256,256]{2,1,0:T(8,128)(2,1)} %broadcast_in_dim.5), calls=%async_computation.1 | async-start | bytes 2097152 | tf_op jit(solution)/shard_map/all_to_all | solution.py:265
  100.7 24.8 %collective-permute-start.6 = (f32[2,128,256]{1,2,0:T(8,128)}, f32[2,128,256]{1,2,0:T(8,128)}, u32[]{:S(2)}, u32[]{:S(2)}) collective-permute-start(f32[2,128,256]{1,2,0:T(8,128)} %pad_maximum_fusion), channel_id=1, source_target_pairs={{8,0},{16,8},{24,16},{32,24},{40,32},{48,40},{56,48},{64,56},{72,6... | collective-permute-start | bytes 786440 | tf_op jit(solution)/shard_map/ppermute | solution.py:238
  114.2 105.6 %all-to-all-start.3 = ((bf16[32,8,2048]{2,1,0:T(8,128)(2,1)}), bf16[32,8,2048]{2,1,0:T(8,128)(2,1)}, u32[]{:S(2)}, u32[]{:S(2)}) async-start(bf16[32,8,2048]{2,1,0:T(8,128)(2,1)} %bitcast.32), calls=%async_computation.3 | async-start | bytes 2097152 | tf_op jit(solution)/shard_map/all_to_all | solution.py:339
  127.0 29.8 %collective-permute-start.7 = (f32[2,128,256]{2,1,0:T(8,128)S(1)}, f32[2,128,256]{2,1,0:T(8,128)S(1)}, u32[]{:S(2)}, u32[]{:S(2)}) collective-permute-start(f32[2,128,256]{2,1,0:T(8,128)S(1)} %convolution_add_fusion.3), channel_id=1, source_target_pairs={{16,0},{24,8},{32,16},{40,24},{48,32},{56,40},{64,48},{72,56},{80,... | collective-permute-start | bytes 786440 | tf_op jit(solution)/shard_map/ppermute | solution.py:238
  157.1 15.4 %collective-permute-start.8 = (f32[2,128,256]{2,1,0:T(8,128)S(1)}, f32[2,128,256]{2,1,0:T(8,128)S(1)}, u32[]{:S(2)}, u32[]{:S(2)}) collective-permute-start(f32[2,128,256]{2,1,0:T(8,128)S(1)} %convolution_add_fusion.2), channel_id=1, source_target_pairs={{32,0},{40,8},{48,16},{56,24},{64,32},{72,40},{80,48},{88,56},{96,... | collective-permute-start | bytes 786440 | tf_op jit(solution)/shard_map/ppermute | solution.py:238
  172.5 31.9 %copy-start.12 = (f32[256,256]{1,0:T(8,128)S(1)}, f32[256,256]{1,0:T(8,128)}, u32[]{:S(2)}) copy-start(f32[256,256]{1,0:T(8,128)} %copy-done.11) | copy-start | bytes 786436
  172.9 31.5 %copy-start.6 = (f32[2,4,128,128]{3,2,1,0:T(8,128)S(1)}, f32[2,4,128,128]{3,2,1,0:T(8,128)}, u32[]{:S(2)}) copy-start(f32[2,4,128,128]{3,2,1,0:T(8,128)} %copy-done.5) | copy-start | bytes 1572868
  172.9 31.5 %copy-start.8 = (f32[2,4,128,128]{3,2,1,0:T(8,128)S(1)}, f32[2,4,128,128]{3,2,1,0:T(8,128)}, u32[]{:S(2)}) copy-start(f32[2,4,128,128]{3,2,1,0:T(8,128)} %copy-done.7) | copy-start | bytes 1572868
  172.9 31.5 %copy-start.10 = (f32[2,4,128,128]{3,2,1,0:T(8,128)S(1)}, f32[2,4,128,128]{3,2,1,0:T(8,128)}, u32[]{:S(2)}) copy-start(f32[2,4,128,128]{3,2,1,0:T(8,128)} %copy-done.9) | copy-start | bytes 1572868
  172.9 8.4 %collective-permute-start.9 = (f32[2,128,256]{2,1,0:T(8,128)S(1)}, f32[2,128,256]{2,1,0:T(8,128)S(1)}, u32[]{:S(2)}, u32[]{:S(2)}) collective-permute-start(f32[2,128,256]{2,1,0:T(8,128)S(1)} %convolution_add_fusion.1), channel_id=1, source_target_pairs={{64,0},{72,8},{80,16},{88,24},{96,32},{104,40},{112,48},{120,56},{... | collective-permute-start | bytes 786440 | tf_op jit(solution)/shard_map/ppermute | solution.py:238
  181.7 22.4 %collective-permute-start.10 = (f32[2,128,256]{2,1,0:T(8,128)S(1)}, f32[2,128,256]{2,1,0:T(8,128)S(1)}, u32[]{:S(2)}, u32[]{:S(2)}) collective-permute-start(f32[2,128,256]{2,1,0:T(8,128)S(1)} %convolution_add_fusion), channel_id=1, source_target_pairs={{8,0},{16,8},{24,16},{32,24},{40,32},{48,40},{56,48},{64,56},{72,6... | collective-permute-start | bytes 786440 | tf_op jit(solution)/shard_map/ppermute | solution.py:238
  187.0 17.1 %collective-permute-start.11 = (f32[2,128,128]{2,1,0:T(8,128)S(1)}, f32[2,128,128]{2,1,0:T(8,128)S(1)}, u32[]{:S(2)}, u32[]{:S(2)}) collective-permute-start(f32[2,128,128]{2,1,0:T(8,128)S(1)} %slice.105), channel_id=1, source_target_pairs={{136,0},{144,8},{152,16},{160,24},{168,32},{176,40},{184,48},{192,... | collective-permute-start | bytes 393224 | tf_op jit(solution)/shard_map/ppermute | solution.py:238

commit v2 on v1

--- a/solution.py
+++ b/solution.py
@@ -1,3 +1,5 @@
+import functools
+
 import jax
 import jax.numpy as jnp
 from jax import lax
@@ -8,12 +10,13 @@
 HEAD_DIM = 128
 BLOCK = 64
 ROWS = 2 * BLOCK
+RING = 8
 f32 = jnp.float32
 bf16 = jnp.bfloat16
 NN = (((1,), (0,)), ((), ()))
 NT = (((1,), (1,)), ((), ()))
 TN = (((0,), (0,)), ((), ()))
-VMEM_LIMIT = 48 * 1024 * 1024
+VMEM_LIMIT = 24 * 1024 * 1024
 
 
 def halves(x):
@@ -47,11 +50,13 @@
 
 def load_pairs(ref, block):
     rows = pl.ds(block * BLOCK, BLOCK)
-    return jnp.concatenate([ref[0, rows, :], ref[1, rows, :]], axis=0)
-
-
-def prepare_kernel(key_ref, value_ref, logit_ref, system_ref, solved_ref, step_ref, prefix_ref):
-    blocks = key_ref.shape[1] // BLOCK
+    return jnp.concatenate([ref[rows, 0, :], ref[rows, 1, :]], axis=0)
+
+
+def prepare_kernel(
+    key_ref, value_ref, logit_ref, system_ref, solved_ref, step_ref, prefix_ref, whole_ref
+):
+    blocks = key_ref.shape[0] // BLOCK
     row_token, col_token, row_second, col_second = token_grid()
     row = lax.broadcasted_iota(jnp.int32, (ROWS, ROWS), 0)
     col = lax.broadcasted_iota(jnp.int32, (ROWS, ROWS), 1)
@@ -105,14 +110,24 @@
             [moved[:, :HEAD_DIM], moved[:, HEAD_DIM:] + steps[block][:, HEAD_DIM:]], axis=1
         )
         prefix_ref[0, block] = prefix
-
-
-def local_kernel(query_ref, key_ref, solved_ref, step_ref, grad_ref, weight_ref, mixed_grad_ref, reach_ref, inner_ref, drive_ref, adjoint_ref):
+    whole_ref[0] = prefix
+
+
+def columns(place_ref, mask, width):
+    return pl.ds(pl.multiple_of((place_ref[0] ^ mask) * width, width), width)
+
+
+def local_kernel(place_ref, query_ref, key_ref, solved_ref, step_ref, weight_ref, *refs):
+    grad_refs = refs[:-5]
+    mixed_grad_ref, reach_ref, inner_ref, drive_ref, adjoint_ref = refs[-5:]
     blocks = query_ref.shape[0] // BLOCK
     row = lax.broadcasted_iota(jnp.int32, (BLOCK, ROWS), 0)
     col = lax.broadcasted_iota(jnp.int32, (BLOCK, ROWS), 1)
     visible = (col & (BLOCK - 1)) <= row
-    mixed_grad = dot(grad_ref[...], weight_ref[...], NT)
+    mixed_grad = None
+    for mask, grad_ref in enumerate(grad_refs):
+        term = dot(grad_ref[...], weight_ref[:, columns(place_ref, mask, grad_ref.shape[1])], NT)
+        mixed_grad = term if mixed_grad is None else mixed_grad + term
     mixed_grad_ref[...] = mixed_grad
     drives = []
     for block in range(blocks):
@@ -135,19 +150,76 @@
     adjoint_ref[0] = adjoint
 
 
-def mix_kernel(state_ref, prefix_ref, reach_ref, inner_ref, grad_ref, states_ref, mixed_ref, weight_grad_ref):
+def merge_kernel(first, upper_ref, next_upper_ref, own_ref, far_ref, *refs):
+    extra_refs, refs = refs[:2], refs[2:]
+    before_out, after_out, send_ref = refs[:3]
+    total_out = refs[3] if len(refs) > 3 else None
+    upper = upper_ref[0] == 1
+    d = HEAD_DIM
+    for head in range(own_ref.shape[0]):
+        own = own_ref[head]
+        far = far_ref[head].astype(f32)
+        if first:
+            own = jnp.concatenate([own, extra_refs[0][head]], axis=1)
+            far = jnp.concatenate([far, extra_refs[1][head]], axis=1)
+        low = jnp.where(upper, far, own)
+        high = jnp.where(upper, own, far)
+        low_parts, high_parts = halves(low), halves(high)
+        head_of = lambda parts, cut: tuple(part[:, cut] for part in parts)
+        forward = product(head_of(high_parts, slice(0, d)), head_of(low_parts, slice(0, 2 * d)))
+        state = forward[:, d:] + high[:, d : 2 * d]
+        adjoint = product(head_of(low_parts, slice(0, d)), head_of(high_parts, slice(2 * d, 3 * d)), TN) + low[:, 2 * d :]
+        step = forward[:, :d]
+        far_step = far[:, :d]
+        beside = jnp.where(
+            upper, far[:, : 2 * d], jnp.concatenate([far_step.T, far[:, 2 * d :]], axis=1)
+        )
+        if first:
+            identity = jnp.where(
+                lax.broadcasted_iota(jnp.int32, (d, 2 * d), 0) == lax.broadcasted_iota(jnp.int32, (d, 2 * d), 1), 1.0, 0.0
+            )
+            before_out[head] = jnp.where(upper, beside, identity)
+            after_out[head] = jnp.where(upper, identity, beside)
+        else:
+            before, after = extra_refs[0][head], extra_refs[1][head]
+            near = jnp.where(upper, before, after)
+            moved = product(near[:, :d], beside)
+            moved = jnp.concatenate([moved[:, :d], moved[:, d:] + near[:, d:]], axis=1)
+            before_out[head] = jnp.where(upper, moved, before)
+            after_out[head] = jnp.where(upper, after, moved)
+        if total_out is None:
+            send_ref[head] = jnp.where(next_upper_ref[0] == 1, adjoint, state).astype(send_ref.dtype)
+        else:
+            total = jnp.concatenate([step, state, adjoint], axis=1)
+            total_out[head] = total
+            send_ref[head] = total.astype(send_ref.dtype)
+
+
+def mix_kernel(
+    place_ref, upper_ref, before_ref, after_ref, far_ref, prefix_ref, reach_ref, inner_ref, *refs
+):
+    grad_refs = refs[:-4]
+    states_ref, adjoint_ref, mixed_ref, weight_grad_ref = refs[-4:]
     blocks = prefix_ref.shape[1]
-    start = state_ref[0]
+    upper = upper_ref[0] == 1
+    before, after = before_ref[0], after_ref[0]
+    near = jnp.where(upper, before, after)
+    moved = product(near[:, :HEAD_DIM], far_ref[0].astype(f32)) + near[:, HEAD_DIM:]
+    start = jnp.where(upper, moved, before[:, HEAD_DIM:])
+    adjoint_ref[0] = jnp.where(upper, after[:, HEAD_DIM:], moved)
     parts = halves(start)
     for block in range(blocks):
         state = start
         if block:
-            before = prefix_ref[0, block - 1]
-            state = product(before[:, :HEAD_DIM], parts) + before[:, HEAD_DIM:]
+            ahead = prefix_ref[0, block - 1]
+            state = product(ahead[:, :HEAD_DIM], parts) + ahead[:, HEAD_DIM:]
         states_ref[0, block] = state
         mixed = product(reach_ref[0, block], state) + inner_ref[0, block]
         mixed_ref[pl.ds(block * BLOCK, BLOCK), :] = mixed.astype(bf16)
-    weight_grad_ref[...] = dot(mixed_ref[...], grad_ref[...], TN).astype(bf16)
+    mixed = mixed_ref[...]
+    for mask, grad_ref in enumerate(grad_refs):
+        part = columns(place_ref, mask, grad_ref.shape[1])
+        weight_grad_ref[:, part] = dot(mixed, grad_ref[...], TN).astype(bf16)
 
 
 def unit_pull(x, unit_grad):
@@ -184,8 +256,8 @@
         fresh_grad = product(scores, out_grad, TN) + product(key_unit, after)
         value_grad = product(system_ref[0, block], fresh_grad, TN)
         value_parts = halves(value_grad)
-        value_grad_ref[0, rows, :] = value_grad[:BLOCK]
-        value_grad_ref[1, rows, :] = value_grad[BLOCK:]
+        value_grad_ref[rows, 0, :] = value_grad[:BLOCK]
+        value_grad_ref[rows, 1, :] = value_grad[BLOCK:]
         high, low = halves(value_grad * fresh)
         sums = dot(ones, high, NT) + dot(ones, low, NT)
         logit_grad_ref[0, pl.ds(block, 1), :] = (
@@ -202,8 +274,8 @@
             - (product(gram_grad, key_unit) + product(gram_grad, key_unit, TN))
         )
         key_grad = unit_pull(key, key_unit_grad)
-        key_grad_ref[0, rows, :] = key_grad[:BLOCK]
-        key_grad_ref[1, rows, :] = key_grad[BLOCK:]
+        key_grad_ref[rows, 0, :] = key_grad[:BLOCK]
+        key_grad_ref[rows, 1, :] = key_grad[BLOCK:]
         if block:
             adjoint = product(step_ref[0, block], after, TN) + drive_ref[0, block]
 
@@ -211,10 +283,12 @@
 def head_call(kernel, name, heads, outs, *operands):
     def spec(kind, shape):
         rank = len(shape)
-        if kind == "first":
+        if kind in ("first", "free"):
             return pl.BlockSpec((1, *shape[1:]), lambda h: (h,) + (0,) * (rank - 1))
         if kind == "last":
             return pl.BlockSpec((*shape[:-1], HEAD_DIM), lambda h: (0,) * (rank - 1) + (h,))
+        if kind == "scalar":
+            return pl.BlockSpec(memory_space=pltpu.SMEM)
         if kind == "rows":
             return pl.BlockSpec((HEAD_DIM, *shape[1:]), lambda h: (h,) + (0,) * (rank - 1))
         return pl.BlockSpec(shape, lambda h: (0,) * rank)
@@ -225,50 +299,63 @@
         grid=(heads,),
         in_specs=[spec(kind, array.shape) for kind, array in operands],
         out_specs=[spec(kind, shape) for kind, shape, _ in outs],
-        out_shape=[jax.ShapeDtypeStruct(shape, dtype) for _, shape, dtype in outs],
+        out_shape=[pltpu.HBM(shape, dtype) for _, shape, dtype in outs],
         compiler_params=pltpu.CompilerParams(
             dimension_semantics=("arbitrary",), vmem_limit_bytes=VMEM_LIMIT
         ),
-    )(*[array for _, array in operands])
-
-
-def shifted(array, by):
-    count = lax.axis_size("seq")
-    pairs = [(i, i + by) for i in range(count) if 0 <= i + by < count]
-    return lax.ppermute(array, "seq", pairs)
-
-
-def joined(later, earlier):
-    moved = jnp.einsum(
-        "hab,hbn->han", later[:, :, :HEAD_DIM], earlier, precision=lax.Precision.HIGHEST
-    )
-    return moved + jnp.concatenate([jnp.zeros_like(moved[:, :, :HEAD_DIM]), later[:, :, HEAD_DIM:]], axis=2)
-
-
-def arriving(own, sign):
-    count = lax.axis_size("seq")
-    distance = 1
-    while distance < count // 2:
-        own = joined(own, shifted(own, sign * distance))
-        distance *= 2
-    near = shifted(own, sign)
-    if count == 1:
-        return near[:, :, HEAD_DIM:]
-    far = shifted(own[:, :, HEAD_DIM:], sign * (count // 2 + 1))
-    return near[:, :, HEAD_DIM:] + jnp.einsum(
-        "hab,hbn->han", near[:, :, :HEAD_DIM], far, precision=lax.Precision.HIGHEST
-    )
+    )(
+        *[
+            array if kind in ("scalar", "free", "whole free") else pltpu.with_memory_space_constraint(array, pltpu.HBM)
+            for kind, array in operands
+        ]
+    )
+
+
+def exchanged(array, axis, mask):
+    return lax.ppermute(array, axis, [(i, i ^ mask) for i in range(lax.axis_size(axis))])
+
+
+def merged(first, upper, next_upper, own, far, extra, send_dtype, last):
+    heads = own.shape[0]
+    near = ("first", (heads, HEAD_DIM, 2 * HEAD_DIM), f32)
+    outs = [near, near]
+    if last:
+        outs += [("first", (heads, HEAD_DIM, HEAD_DIM), send_dtype)]
+    else:
+        whole = (heads, HEAD_DIM, 3 * HEAD_DIM)
+        outs += [("first", whole, send_dtype), ("first", whole, f32)]
+    return head_call(
+        functools.partial(merge_kernel, first),
+        "merge",
+        heads,
+        outs,
+        ("scalar", upper),
+        ("scalar", next_upper),
+        ("first", own),
+        ("free", far),
+        ("first", extra[0]),
+        ("free" if first else "first", extra[1]),
+    )
+
+
+def level_masks(count):
+    masks, size = [], 1
+    while size < count:
+        masks.append(2 * size - 1 if size < RING else 2 * size - RING)
+        size *= 2
+    return masks
 
 
 def gathered(array, axis):
-    copies = jnp.broadcast_to(array[None], (lax.axis_size(axis), *array.shape))
-    return lax.all_to_all(copies, axis, 0, 0, tiled=True)
-
-
-def project_kernel(mixed_ref, weight_ref, out_ref):
-    total = dot(mixed_ref[0], weight_ref[0], NN)
-    for part in range(1, mixed_ref.shape[0]):
-        total = total + dot(mixed_ref[part], weight_ref[part], NN)
+    return [array] + [exchanged(array, axis, mask) for mask in range(1, lax.axis_size(axis))]
+
+
+def project_kernel(place_ref, weight_ref, *refs):
+    out_ref = refs[-1]
+    total = None
+    for mask, mixed_ref in enumerate(refs[:-1]):
+        term = dot(mixed_ref[...], weight_ref[place_ref[0] ^ mask], NN)
+        total = term if total is None else total + term
     out_ref[...] = total.astype(bf16)
 
 
@@ -278,30 +365,38 @@
     blocks = tokens // BLOCK
     square = (heads, blocks, ROWS, HEAD_DIM)
     double = (heads, blocks, ROWS, 2 * HEAD_DIM)
-    keys = reflect_keys.transpose(1, 0, 2)
-    values = reflect_values.transpose(1, 0, 2)
+    parts = lax.axis_size("head")
+    seq_count = lax.axis_size("seq")
+    place = lax.axis_index("seq")
+    head_place = lax.axis_index("head").astype(jnp.int32).reshape(1)
+    grad_parts = gathered(out_grad, "head")
+    keys, values = reflect_keys, reflect_values
     logits = beta_logit.reshape(2, heads, blocks, BLOCK).transpose(1, 2, 0, 3)
     logit_rows = jnp.concatenate(
         [logits.reshape(heads, blocks, ROWS), logits[:, :, ::-1].reshape(heads, blocks, ROWS)], axis=1
     )
-    parts = lax.axis_size("head")
-    grad_parts = gathered(out_grad, "head")
-    weight_parts = lax.all_to_all(
-        out_weight.reshape(features, parts, features).transpose(1, 0, 2), "head", 0, 0, tiled=True
-    )
-    full_grad = grad_parts.transpose(1, 0, 2).reshape(tokens, parts * features)
-
-    system, solved, step, prefix = head_call(
+
+    system, solved, step, prefix, whole = head_call(
         prepare_kernel,
         "prepare",
         heads,
-        [("first", square, f32), ("first", double, f32), ("first", square, f32), ("first", double, f32)],
+        [
+            ("first", square, f32),
+            ("first", double, f32),
+            ("first", square, f32),
+            ("first", double, f32),
+            ("first", (heads, HEAD_DIM, 2 * HEAD_DIM), f32),
+        ],
         ("last", keys),
         ("last", values),
         ("first", logit_rows),
     )
-    whole = prefix[:, -1]
-    state_in = arriving(whole, 1)
+    masks = level_masks(seq_count)
+    far = exchanged(whole, "seq", masks[0])
+    weight_source, whole = lax.optimization_barrier((out_weight, whole))
+    weight_parts = lax.all_to_all(
+        weight_source.reshape(features, parts, features).transpose(1, 0, 2), "head", 0, 0, tiled=True
+    )
     mixed_grad, reach, inner, drive, adjoint = head_call(
         local_kernel,
         "local",
@@ -313,40 +408,52 @@
             ("first", square, f32),
             ("first", (heads, ROWS, HEAD_DIM), f32),
         ],
+        ("scalar", head_place),
         ("last", queries),
         ("last", keys),
         ("first", solved),
         ("first", step),
-        ("whole", full_grad),
         ("rows", out_weight),
-    )
-    adjoint_in = arriving(
-        jnp.concatenate([jnp.swapaxes(whole[:, :, :HEAD_DIM], 1, 2), adjoint], axis=2), -1
-    )
-    states, mixed, weight_share = head_call(
+        *[("whole free", part) for part in grad_parts],
+    )
+    far_tail = exchanged(adjoint, "seq", masks[0])
+    total, extra = whole, (adjoint, far_tail)
+    upper = [((place >> level) & 1).astype(jnp.int32).reshape(1) for level in range(len(masks))]
+    for level in range(len(masks) - 1):
+        last = level == len(masks) - 2
+        send_dtype = bf16 if 0 <= level < 2 and not last else f32
+        result = merged(
+            level == 0, upper[level], upper[level + 1], total, far, extra, send_dtype, last
+        )
+        extra, sent = result[:2], result[2]
+        total = None if last else result[3]
+        far = exchanged(sent, "seq", masks[level + 1])
+    states, adjoint_in, mixed, weight_share = head_call(
         mix_kernel,
         "mix",
         heads,
-        [("first", square, f32), ("last", (tokens, features), bf16), ("rows", out_weight.shape, bf16)],
-        ("first", state_in),
+        [
+            ("first", square, f32),
+            ("first", (heads, ROWS, HEAD_DIM), f32),
+            ("last", (tokens, features), bf16),
+            ("rows", out_weight.shape, bf16),
+        ],
+        ("scalar", head_place),
+        ("scalar", upper[-1]),
+        ("first", extra[0]),
+        ("first", extra[1]),
+        ("free", far),
         ("first", prefix),
         ("first", reach),
         ("first", inner),
-        ("whole", full_grad),
-    )
-    seq_count = lax.axis_size("seq")
+        *[("whole", part) for part in grad_parts],
+    )
     weight_grad = jnp.sum(
         lax.all_to_all(
             weight_share.reshape(seq_count, features // seq_count, out_weight.shape[1]), "seq", 0, 0, tiled=True
         ).astype(f32),
         axis=0,
     )
-    output = pl.pallas_call(
-        project_kernel,
-        name="project",
-        out_shape=jax.ShapeDtypeStruct((tokens, features), bf16),
-        compiler_params=pltpu.CompilerParams(vmem_limit_bytes=VMEM_LIMIT),
-    )(gathered(mixed, "head"), weight_parts)
     query_grad, key_grad, value_grad, logit_grad = head_call(
         gradient_kernel,
         "gradients",
@@ -368,12 +475,22 @@
         ("last", mixed_grad),
         ("first", adjoint_in),
     )
+    mixed_parts = gathered(mixed, "head")
+    vmem = pl.BlockSpec(memory_space=pltpu.VMEM)
+    output = pl.pallas_call(
+        project_kernel,
+        name="project",
+        in_specs=[pl.BlockSpec(memory_space=pltpu.SMEM)] + [vmem] * (1 + parts),
+        out_specs=vmem,
+        out_shape=jax.ShapeDtypeStruct((tokens, features), bf16),
+        compiler_params=pltpu.CompilerParams(vmem_limit_bytes=VMEM_LIMIT),
+    )(head_place, weight_parts, *mixed_parts)
     logit_grad = logit_grad.reshape(heads, blocks, 2, BLOCK).transpose(2, 0, 1, 3).reshape(beta_logit.shape)
     return (
         output,
         query_grad,
-        key_grad.transpose(1, 0, 2),
-        value_grad.transpose(1, 0, 2),
+        key_grad,
+        value_grad,
         logit_grad,
         weight_grad,
     )

time: 223 us -> 126 us (0.57)
  the two profiles are of different devices: /device:TPU:32 before, /device:TPU:2 now
where the time goes in v2:
time: 126 us
  Pallas kernels  44.2 us (35%)
  starting transfers between devices  43.3 us (34%)
  waiting for transfers between devices  31.7 us (25%)
  local copies, waits for them, and re-layouts  4.29 us (3%)
  other arithmetic  1.38 us (1%)
    pallas_call x8, Pallas kernels, head_call(): pl.pallas_call(kernel, name=name, grid=(heads,), in_specs=[spec(kind, arr...  43.1 us
    ppermute x20, starting transfers between devices, exchanged(): lax.ppermute(array, axis, [(i, i ^ mask) for i in range(lax.axis_size(axi...  29.8 us
    ppermute x20, waiting for transfers between devices, exchanged(): lax.ppermute(array, axis, [(i, i ^ mask) for i in range(lax.axis_size(axi...  27.1 us
    all_to_all x1, starting transfers between devices, body(): lax.all_to_all(weight_share.reshape(seq_count, features // seq_count, out...  8.3 us
    all_to_all x1, starting transfers between devices, body(): lax.all_to_all(weight_source.reshape(features, parts, features).transpose...  5.19 us
    all_to_all x1, waiting for transfers between devices, body(): lax.all_to_all(weight_share.reshape(seq_count, features // seq_count, out...  4.53 us
  transfers between devices with their start and end apart: 22, of which 6 were waited for; matrix products, arithmetic and copies ran while one was open for 4% of the time, Pallas kernels for 33%

profile of v2, /device:TPU:2, one launch (start us, length us, event | category | flops | bytes accessed | tf_op | source)
XLA Modules:
  0.0 125.6 jit_solution(2825422649960850926)
XLA Ops:
  0.6 0.0 copy-start
  0.6 0.1 collective-permute-start.1
  0.7 2.4 %collective-permute-start.2 = (bf16[256,256]{1,0:T(8,128)(2,1)}, bf16[256,256]{1,0:T(8,128)(2,1)S(1)}, u32[]{:S(2)}, u32[]{:S(2)}) collective-permute-start(bf16[256,256]{1,0:T(8,128)(2,1)} %refs_0_.3), channel_id=1, source_target_pairs={{0,2},{1,3},{2,0},{3,1},{4,6},{5,7},{6,4},{7,5},{8,10},{9,11},{10,... | collective-permute-start | bytes 393224 | tf_op jit(solution)/shard_map/ppermute | solution.py:315
  3.1 0.1 collective-permute-start.3
  3.2 1.6 %collective-permute-start.4 = (bf16[256,256]{1,0:T(8,128)(2,1)}, bf16[256,256]{1,0:T(8,128)(2,1)S(1)}, u32[]{:S(2)}, u32[]{:S(2)}) collective-permute-start(bf16[256,256]{1,0:T(8,128)(2,1)} %refs_0_.3), channel_id=1, source_target_pairs={{0,4},{1,5},{2,6},{3,7},{4,0},{5,1},{6,2},{7,3},{8,12},{9,13},{10,... | collective-permute-start | bytes 393224 | tf_op jit(solution)/shard_map/ppermute | solution.py:315
  4.8 1.4 %collective-permute-start.5 = (bf16[256,256]{1,0:T(8,128)(2,1)}, bf16[256,256]{1,0:T(8,128)(2,1)S(1)}, u32[]{:S(2)}, u32[]{:S(2)}) collective-permute-start(bf16[256,256]{1,0:T(8,128)(2,1)} %refs_0_.3), channel_id=1, source_target_pairs={{0,5},{1,4},{2,7},{3,6},{4,1},{5,0},{6,3},{7,2},{8,13},{9,12},{10,... | collective-permute-start | bytes 393224 | tf_op jit(solution)/shard_map/ppermute | solution.py:315
  6.2 0.8 reshape.52
  7.0 0.1 reshape.53
  7.1 0.1 reshape.54
  7.2 0.0 collective-permute-done.1.refs_1_
  7.2 1.2 collective-permute-start.6
  8.3 0.0 collective-permute-done.2.refs_2_
  8.3 0.8 collective-permute-start.7
  9.2 0.6 pad_maximum_fusion.logit_ref
  9.8 9.5 %prepare.1 = (f32[2,4,128,128]{3,2,1,0:T(8,128)}, f32[2,4,128,256]{3,2,1,0:T(8,128)}, f32[2,4,128,128]{3,2,1,0:T(8,128)}, f32[2,4,128,256]{3,2,1,0:T(8,128)}, f32[2,128,256]{2,1,0:T(8,128)}) custom-call(f32[256,2,256]{2,1,0:T(2,128)} %key_ref.5, f32[256,2,256]{2,1,0:T(2,128)} %value_ref.1, f32[2,8,128]{2,1,0:T(8,128)} %pad_maximum_fusion.logit_ref), custom_call_target="tpu_custom_call" | custom-call | tf_op jit(solution)/shard_map/prepare/pallas_call | solution.py:296
  19.3 0.0 collective-permute-done.3.refs_3_
  19.3 1.5 %collective-permute-start = (f32[2,128,256]{2,1,0:T(8,128)}, f32[2,128,256]{2,1,0:T(8,128)S(1)}, u32[]{:S(2)}, u32[]{:S(2)}) collective-permute-start(f32[2,128,256]{2,1,0:T(8,128)} %get-tuple-element.43.own_ref), channel_id=1, source_target_pairs={{0,8},{8,0},{16,24},{24,16},{32,40},{40,32},{48,56},{56,48},{64,72... | collective-permute-start | bytes 786440 | tf_op jit(solution)/shard_map/ppermute | solution.py:315
  20.7 0.0 collective-permute-done.4.refs_4_
  20.8 0.0 collective-permute-done.5.refs_5_
  20.8 0.0 collective-permute-done.6.refs_6_
  20.8 0.7 collective-permute-done.7.refs_7_
  21.5 7.4 %local.1 = (f32[256,256]{1,0:T(8,128)}, f32[2,4,64,128]{3,2,1,0:T(8,128)}, f32[2,4,64,128]{3,2,1,0:T(8,128)}, f32[2,4,128,128]{3,2,1,0:T(8,128)}, f32[2,128,128]{2,1,0:T(8,128)}) custom-call(s32[1]{0:T(128)} %bitcast.place_ref, f32[256,256]{1,0:T(8,128)} %query_ref.3, f32[256,2,256]{2,1,0:T(2,128)} %key_ref.5, ...), custom_call_target="tpu_custom_call" | custom-call | tf_op jit(solution)/shard_map/local/pallas_call | solution.py:296
  28.9 1.6 %collective-permute-start.8 = (f32[2,128,128]{2,1,0:T(8,128)}, f32[2,128,128]{2,1,0:T(8,128)S(1)}, u32[]{:S(2)}, u32[]{:S(2)}) collective-permute-start(f32[2,128,128]{2,1,0:T(8,128)} %get-tuple-element.46.refs_0_), channel_id=1, source_target_pairs={{0,8},{8,0},{16,24},{24,16},{32,40},{40,32},{48,56},{56,48},{64,72... | collective-permute-start | bytes 393224 | tf_op jit(solution)/shard_map/ppermute | solution.py:315
  30.5 4.2 %collective-permute-done.8.refs_1_ = f32[2,128,128]{2,1,0:T(8,128)S(1)} collective-permute-done((f32[2,128,128]{2,1,0:T(8,128)}, f32[2,128,128]{2,1,0:T(8,128)S(1)}, u32[]{:S(2)}, u32[]{:S(2)}) %collective-permute-start.8) | collective-permute-done | bytes 131104 | tf_op jit(solution)/shard_map/ppermute | solution.py:315
  34.7 0.0 collective-permute-done.far_ref
  34.7 2.2 %merge.4 = (f32[2,128,256]{2,1,0:T(8,128)}, f32[2,128,256]{2,1,0:T(8,128)}, bf16[2,128,384]{2,1,0:T(8,128)(2,1)}, f32[2,128,384]{2,1,0:T(8,128)}) custom-call(s32[1]{0:T(128)} %bitcast.8.upper_ref, s32[1]{0:T(128)} %bitcast.7.next_upper_ref.upper_ref, f32[2,128,256]{2,1,0:T(8,128)} %get-tuple-element.43.own_ref, ...), custom_call_target="tpu_custom_call" | custom-call | tf_op jit(solution)/shard_map/merge/pallas_call | solution.py:296
  36.9 4.2 %collective-permute-start.9 = (bf16[2,128,384]{2,1,0:T(8,128)(2,1)}, bf16[2,128,384]{2,1,0:T(8,128)(2,1)S(1)}, u32[]{:S(2)}, u32[]{:S(2)}) collective-permute-start(bf16[2,128,384]{2,1,0:T(8,128)(2,1)} %get-tuple-element.48), channel_id=1, source_target_pairs={{0,24},{8,16},{16,8},{24,0},{32,56},{40,48},{48,40},{56,32},{64,88... | collective-permute-start | bytes 589832 | tf_op jit(solution)/shard_map/ppermute | solution.py:315
  41.1 0.5 copy.15
  41.6 1.3 %copy.16 = bf16[256,8,256]{2,0,1:T(8,128)(2,1)} copy(bf16[256,8,256]{0,2,1:T(8,128)(2,1)S(1)} %bitcast.13) | data formatting | bytes 2097152 | tf_op jit(solution)/shard_map/reshape | solution.py:398
  42.9 5.2 %all-to-all-start = ((bf16[8,256,256]{2,1,0:T(8,128)(2,1)}), bf16[8,256,256]{2,1,0:T(8,128)(2,1)S(1)}, u32[]{:S(2)}, u32[]{:S(2)}) async-start(bf16[8,256,256]{2,1,0:T(8,128)(2,1)} %bitcast.3), calls=%async_computation | async-start | bytes 2097152 | tf_op jit(solution)/shard_map/all_to_all | solution.py:397
  48.1 0.0 collective-permute-done.9.far_ref
  48.1 2.5 %merge.5 = (f32[2,128,256]{2,1,0:T(8,128)}, f32[2,128,256]{2,1,0:T(8,128)}, bf16[2,128,384]{2,1,0:T(8,128)(2,1)}, f32[2,128,384]{2,1,0:T(8,128)}) custom-call(s32[1]{0:T(128)} %bitcast.7.next_upper_ref.upper_ref, s32[1]{0:T(128)} %bitcast.6.next_upper_ref.upper_ref, f32[2,128,384]{2,1,0:T(8,128)} %get-tuple-element.47.own_ref, ...), custom_call_target="tpu_custom_call" | custom-call | tf_op jit(solution)/shard_map/merge/pallas_call | solution.py:296
  50.6 3.2 %collective-permute-start.10 = (bf16[2,128,384]{2,1,0:T(8,128)(2,1)}, bf16[2,128,384]{2,1,0:T(8,128)(2,1)S(1)}, u32[]{:S(2)}, u32[]{:S(2)}) collective-permute-start(bf16[2,128,384]{2,1,0:T(8,128)(2,1)} %get-tuple-element.52), channel_id=1, source_target_pairs={{0,56},{8,48},{16,40},{24,32},{32,24},{40,16},{48,8},{56,0},{64,12... | collective-permute-start | bytes 589832 | tf_op jit(solution)/shard_map/ppermute | solution.py:315
  53.8 9.6 %collective-permute-done.10.far_ref = bf16[2,128,384]{2,1,0:T(8,128)(2,1)S(1)} collective-permute-done((bf16[2,128,384]{2,1,0:T(8,128)(2,1)}, bf16[2,128,384]{2,1,0:T(8,128)(2,1)S(1)}, u32[]{:S(2)}, u32[]{:S(2)}) %collective-permute-start.10) | collective-permute-done | bytes 196640 | tf_op jit(solution)/shard_map/ppermute | solution.py:315
  63.5 2.5 %merge.6 = (f32[2,128,256]{2,1,0:T(8,128)}, f32[2,128,256]{2,1,0:T(8,128)}, f32[2,128,384]{2,1,0:T(8,128)}, f32[2,128,384]{2,1,0:T(8,128)}) custom-call(s32[1]{0:T(128)} %bitcast.6.next_upper_ref.upper_ref, s32[1]{0:T(128)} %bitcast.5.next_upper_ref.upper_ref, f32[2,128,384]{2,1,0:T(8,128)} %get-tuple-element.51.own_ref, ...), custom_call_target="tpu_custom_call" | custom-call | tf_op jit(solution)/shard_map/merge/pallas_call | solution.py:296
  66.0 1.8 %collective-permute-start.11 = (f32[2,128,384]{2,1,0:T(8,128)}, f32[2,128,384]{2,1,0:T(8,128)S(1)}, u32[]{:S(2)}, u32[]{:S(2)}) collective-permute-start(f32[2,128,384]{2,1,0:T(8,128)} %get-tuple-element.56), channel_id=1, source_target_pairs={{0,64},{8,72},{16,80},{24,88},{32,96},{40,104},{48,112},{56,120},{... | collective-permute-start | bytes 1179656 | tf_op jit(solution)/shard_map/ppermute | solution.py:315
  67.8 9.2 %collective-permute-done.11.far_ref = f32[2,128,384]{2,1,0:T(8,128)S(1)} collective-permute-done((f32[2,128,384]{2,1,0:T(8,128)}, f32[2,128,384]{2,1,0:T(8,128)S(1)}, u32[]{:S(2)}, u32[]{:S(2)}) %collective-permute-start.11) | collective-permute-done | bytes 393248 | tf_op jit(solution)/shard_map/ppermute | solution.py:315
  77.0 2.5 %merge.7 = (f32[2,128,256]{2,1,0:T(8,128)}, f32[2,128,256]{2,1,0:T(8,128)}, f32[2,128,128]{2,1,0:T(8,128)}) custom-call(s32[1]{0:T(128)} %bitcast.5.next_upper_ref.upper_ref, s32[1]{0:T(128)} %bitcast.4.next_upper_ref.upper_ref, f32[2,128,384]{2,1,0:T(8,128)} %get-tuple-element.55.own_ref, f32[2,128,384]{2,1,0:T(8,128)S(1)} %collective-permute-done.11.far_ref, ...), custom_call_target="tpu_custom_call" | custom-call | tf_op jit(solution)/shard_map/merge/pallas_call | solution.py:296
  79.5 3.0 %collective-permute-start.12 = (f32[2,128,128]{2,1,0:T(8,128)}, f32[2,128,128]{2,1,0:T(8,128)S(1)}, u32[]{:S(2)}, u32[]{:S(2)}) collective-permute-start(f32[2,128,128]{2,1,0:T(8,128)} %get-tuple-element.61), channel_id=1, source_target_pairs={{0,192},{8,200},{16,208},{24,216},{32,224},{40,232},{48,240},{56,2... | collective-permute-start | bytes 393224 | tf_op jit(solution)/shard_map/ppermute | solution.py:315
  82.5 3.3 %collective-permute-done.12.far_ref = f32[2,128,128]{2,1,0:T(8,128)S(1)} collective-permute-done((f32[2,128,128]{2,1,0:T(8,128)}, f32[2,128,128]{2,1,0:T(8,128)S(1)}, u32[]{:S(2)}, u32[]{:S(2)}) %collective-permute-start.12) | collective-permute-done | bytes 131104 | tf_op jit(solution)/shard_map/ppermute | solution.py:315
  85.9 4.6 %mix.1 = (f32[2,4,128,128]{3,2,1,0:T(8,128)}, f32[2,128,128]{2,1,0:T(8,128)}, bf16[256,256]{1,0:T(8,128)(2,1)}, bf16[256,2048]{1,0:T(8,128)(2,1)}) custom-call(s32[1]{0:T(128)} %bitcast.place_ref, s32[1]{0:T(128)} %bitcast.4.next_upper_ref.upper_ref, f32[2,128,256]{2,1,0:T(8,128)} %get-tuple-element.59.before_ref, ...), custom_call_target="tpu_custom_call" | custom-call | tf_op jit(solution)/shard_map/mix/pallas_call | solution.py:296
  90.4 0.0 all-to-all-done.weight_ref
  90.4 0.0 copy-start.8
  90.5 8.3 %all-to-all-start.1 = ((bf16[32,8,2048]{2,1,0:T(8,128)(2,1)}), bf16[32,8,2048]{2,1,0:T(8,128)(2,1)S(1)}, u32[]{:S(2)}, u32[]{:S(2)}) async-start(bf16[32,8,2048]{2,1,0:T(8,128)(2,1)} %bitcast.14), calls=%async_computation.1 | async-start | bytes 2097152 | tf_op jit(solution)/shard_map/all_to_all | solution.py:452
  98.8 0.1 collective-permute-start.13
  98.9 0.1 collective-permute-start.14
  99.0 1.8 %collective-permute-start.15 = (bf16[256,256]{1,0:T(8,128)(2,1)S(1)}, bf16[256,256]{1,0:T(8,128)(2,1)S(1)}, u32[]{:S(2)}, u32[]{:S(2)}) collective-permute-start(bf16[256,256]{1,0:T(8,128)(2,1)S(1)} %copy-done.8), channel_id=1, source_target_pairs={{0,3},{1,2},{2,1},{3,0},{4,7},{5,6},{6,5},{7,4},{8,11},{9,10},{10,... | collective-permute-start | bytes 393224 | tf_op jit(solution)/shard_map/ppermute | solution.py:315
  100.7 2.1 %collective-permute-start.16 = (bf16[256,256]{1,0:T(8,128)(2,1)S(1)}, bf16[256,256]{1,0:T(8,128)(2,1)S(1)}, u32[]{:S(2)}, u32[]{:S(2)}) collective-permute-start(bf16[256,256]{1,0:T(8,128)(2,1)S(1)} %copy-done.8), channel_id=1, source_target_pairs={{0,4},{1,5},{2,6},{3,7},{4,0},{5,1},{6,2},{7,3},{8,12},{9,13},{10,... | collective-permute-start | bytes 393224 | tf_op jit(solution)/shard_map/ppermute | solution.py:315
  102.9 1.1 collective-permute-start.17
  104.0 0.0 collective-permute-done.13.refs_1_
  104.0 1.5 %collective-permute-start.18 = (bf16[256,256]{1,0:T(8,128)(2,1)S(1)}, bf16[256,256]{1,0:T(8,128)(2,1)S(1)}, u32[]{:S(2)}, u32[]{:S(2)}) collective-permute-start(bf16[256,256]{1,0:T(8,128)(2,1)S(1)} %copy-done.8), channel_id=1, source_target_pairs={{0,6},{1,7},{2,4},{3,5},{4,2},{5,3},{6,0},{7,1},{8,14},{9,15},{10,... | collective-permute-start | bytes 393224 | tf_op jit(solution)/shard_map/ppermute | solution.py:315
  105.4 0.0 collective-permute-done.14.refs_2_
  105.4 0.3 collective-permute-start.19
  105.8 12.0 %gradients.1 = (f32[256,256]{1,0:T(8,128)}, f32[256,2,256]{2,1,0:T(2,128)}, f32[256,2,256]{2,1,0:T(2,128)}, f32[2,4,128]{2,1,0:T(4,128)}) custom-call(f32[256,256]{1,0:T(8,128)} %query_ref.3, f32[256,2,256]{2,1,0:T(2,128)} %key_ref.5, f32[2,8,128]{2,1,0:T(8,128)} %pad_maximum_fusion.logit_ref, f32[2,4,128,128]{3,2,1,0:T(8,128)} %get-tuple-element.66.system_ref, ...), custom_call_target="tpu_custom_call" | custom-call | tf_op jit(solution)/shard_map/gradients/pallas_call | solution.py:296
  117.7 0.8 reshape.61
  118.5 0.7 reshape.62
  119.2 0.0 collective-permute-done.15.refs_3_
  119.2 0.0 collective-permute-done.16.refs_4_
  119.2 0.0 collective-permute-done.17.refs_5_
  119.2 0.0 collective-permute-done.18.refs_6_
  119.2 0.0 collective-permute-done.19.refs_7_
  119.2 1.1 project.1
  120.3 4.5 %all-to-all-done.1 = bf16[32,8,2048]{2,1,0:T(8,128)(2,1)S(1)} async-done(((bf16[32,8,2048]{2,1,0:T(8,128)(2,1)}), bf16[32,8,2048]{2,1,0:T(8,128)(2,1)S(1)}, u32[]{:S(2)}, u32[]{:S(2)}) %all-to-all-start.1) | async-done | bytes 1048608 | tf_op jit(solution)/shard_map/all_to_all | solution.py:452
  124.8 0.8 convert_reduce_fusion
  (21 shorter events, 0.1 us)
Async XLA Ops:
  0.6 20.8 %copy-start = (bf16[256,256]{1,0:T(8,128)(2,1)S(1)}, bf16[256,256]{1,0:T(8,128)(2,1)}, u32[]{:S(2)}) copy-start(bf16[256,256]{1,0:T(8,128)(2,1)} %refs_0_.3) | copy-start | bytes 393220
  0.6 6.5 %collective-permute-start.1 = (bf16[256,256]{1,0:T(8,128)(2,1)}, bf16[256,256]{1,0:T(8,128)(2,1)S(1)}, u32[]{:S(2)}, u32[]{:S(2)}) collective-permute-start(bf16[256,256]{1,0:T(8,128)(2,1)} %refs_0_.3), channel_id=1, source_target_pairs={{0,1},{1,0},{2,3},{3,2},{4,5},{5,4},{6,7},{7,6},{8,9},{9,8},{10,11... | collective-permute-start | bytes 393224 | tf_op jit(solution)/shard_map/ppermute | solution.py:315
  0.7 7.6 %collective-permute-start.2 = (bf16[256,256]{1,0:T(8,128)(2,1)}, bf16[256,256]{1,0:T(8,128)(2,1)S(1)}, u32[]{:S(2)}, u32[]{:S(2)}) collective-permute-start(bf16[256,256]{1,0:T(8,128)(2,1)} %refs_0_.3), channel_id=1, source_target_pairs={{0,2},{1,3},{2,0},{3,1},{4,6},{5,7},{6,4},{7,5},{8,10},{9,11},{10,... | collective-permute-start | bytes 393224 | tf_op jit(solution)/shard_map/ppermute | solution.py:315
  3.1 16.2 %collective-permute-start.3 = (bf16[256,256]{1,0:T(8,128)(2,1)}, bf16[256,256]{1,0:T(8,128)(2,1)S(1)}, u32[]{:S(2)}, u32[]{:S(2)}) collective-permute-start(bf16[256,256]{1,0:T(8,128)(2,1)} %refs_0_.3), channel_id=1, source_target_pairs={{0,3},{1,2},{2,1},{3,0},{4,7},{5,6},{6,5},{7,4},{8,11},{9,10},{10,... | collective-permute-start | bytes 393224 | tf_op jit(solution)/shard_map/ppermute | solution.py:315
  3.2 17.6 %collective-permute-start.4 = (bf16[256,256]{1,0:T(8,128)(2,1)}, bf16[256,256]{1,0:T(8,128)(2,1)S(1)}, u32[]{:S(2)}, u32[]{:S(2)}) collective-permute-start(bf16[256,256]{1,0:T(8,128)(2,1)} %refs_0_.3), channel_id=1, source_target_pairs={{0,4},{1,5},{2,6},{3,7},{4,0},{5,1},{6,2},{7,3},{8,12},{9,13},{10,... | collective-permute-start | bytes 393224 | tf_op jit(solution)/shard_map/ppermute | solution.py:315
  4.8 16.0 %collective-permute-start.5 = (bf16[256,256]{1,0:T(8,128)(2,1)}, bf16[256,256]{1,0:T(8,128)(2,1)S(1)}, u32[]{:S(2)}, u32[]{:S(2)}) collective-permute-start(bf16[256,256]{1,0:T(8,128)(2,1)} %refs_0_.3), channel_id=1, source_target_pairs={{0,5},{1,4},{2,7},{3,6},{4,1},{5,0},{6,3},{7,2},{8,13},{9,12},{10,... | collective-permute-start | bytes 393224 | tf_op jit(solution)/shard_map/ppermute | solution.py:315
  7.2 21.7 %copy-start.1 = (bf16[256,256]{1,0:T(8,128)(2,1)}, bf16[256,256]{1,0:T(8,128)(2,1)S(1)}, u32[]{:S(2)}) copy-start(bf16[256,256]{1,0:T(8,128)(2,1)S(1)} %collective-permute-done.1.refs_1_) | copy-start | bytes 393220
  7.2 13.6 %collective-permute-start.6 = (bf16[256,256]{1,0:T(8,128)(2,1)}, bf16[256,256]{1,0:T(8,128)(2,1)S(1)}, u32[]{:S(2)}, u32[]{:S(2)}) collective-permute-start(bf16[256,256]{1,0:T(8,128)(2,1)} %refs_0_.3), channel_id=1, source_target_pairs={{0,6},{1,7},{2,4},{3,5},{4,2},{5,3},{6,0},{7,1},{8,14},{9,15},{10,... | collective-permute-start | bytes 393224 | tf_op jit(solution)/shard_map/ppermute | solution.py:315
  8.3 20.5 %copy-start.2 = (bf16[256,256]{1,0:T(8,128)(2,1)}, bf16[256,256]{1,0:T(8,128)(2,1)S(1)}, u32[]{:S(2)}) copy-start(bf16[256,256]{1,0:T(8,128)(2,1)S(1)} %collective-permute-done.2.refs_2_) | copy-start | bytes 393220
  8.3 13.1 %collective-permute-start.7 = (bf16[256,256]{1,0:T(8,128)(2,1)}, bf16[256,256]{1,0:T(8,128)(2,1)S(1)}, u32[]{:S(2)}, u32[]{:S(2)}) collective-permute-start(bf16[256,256]{1,0:T(8,128)(2,1)} %refs_0_.3), channel_id=1, source_target_pairs={{0,7},{1,6},{2,5},{3,4},{4,3},{5,2},{6,1},{7,0},{8,15},{9,14},{10,... | collective-permute-start | bytes 393224 | tf_op jit(solution)/shard_map/ppermute | solution.py:315
  19.3 9.6 %copy-start.3 = (bf16[256,256]{1,0:T(8,128)(2,1)}, bf16[256,256]{1,0:T(8,128)(2,1)S(1)}, u32[]{:S(2)}) copy-start(bf16[256,256]{1,0:T(8,128)(2,1)S(1)} %collective-permute-done.3.refs_3_) | copy-start | bytes 393220
  19.3 15.4 %collective-permute-start = (f32[2,128,256]{2,1,0:T(8,128)}, f32[2,128,256]{2,1,0:T(8,128)S(1)}, u32[]{:S(2)}, u32[]{:S(2)}) collective-permute-start(f32[2,128,256]{2,1,0:T(8,128)} %get-tuple-element.43.own_ref), channel_id=1, source_target_pairs={{0,8},{8,0},{16,24},{24,16},{32,40},{40,32},{48,56},{56,48},{64,72... | collective-permute-start | bytes 786440 | tf_op jit(solution)/shard_map/ppermute | solution.py:315
  20.8 8.1 %copy-start.4 = (bf16[256,256]{1,0:T(8,128)(2,1)}, bf16[256,256]{1,0:T(8,128)(2,1)S(1)}, u32[]{:S(2)}) copy-start(bf16[256,256]{1,0:T(8,128)(2,1)S(1)} %collective-permute-done.4.refs_4_) | copy-start | bytes 393220
  20.8 8.1 %copy-start.5 = (bf16[256,256]{1,0:T(8,128)(2,1)}, bf16[256,256]{1,0:T(8,128)(2,1)S(1)}, u32[]{:S(2)}) copy-start(bf16[256,256]{1,0:T(8,128)(2,1)S(1)} %collective-permute-done.5.refs_5_) | copy-start | bytes 393220
  20.8 8.1 %copy-start.6 = (bf16[256,256]{1,0:T(8,128)(2,1)}, bf16[256,256]{1,0:T(8,128)(2,1)S(1)}, u32[]{:S(2)}) copy-start(bf16[256,256]{1,0:T(8,128)(2,1)S(1)} %collective-permute-done.6.refs_6_) | copy-start | bytes 393220
  21.4 7.4 %copy-start.7 = (bf16[256,256]{1,0:T(8,128)(2,1)}, bf16[256,256]{1,0:T(8,128)(2,1)S(1)}, u32[]{:S(2)}) copy-start(bf16[256,256]{1,0:T(8,128)(2,1)S(1)} %collective-permute-done.7.refs_7_) | copy-start | bytes 393220
  21.5 19.6 %copy-start.9 = (bf16[256,2048]{1,0:T(8,128)(2,1)S(1)}, bf16[256,2048]{1,0:T(8,128)(2,1)}, u32[]{:S(2)}) copy-start(bf16[256,2048]{1,0:T(8,128)(2,1)} %weight_ref.1) | copy-start | bytes 3145732
  28.9 5.8 %collective-permute-start.8 = (f32[2,128,128]{2,1,0:T(8,128)}, f32[2,128,128]{2,1,0:T(8,128)S(1)}, u32[]{:S(2)}, u32[]{:S(2)}) collective-permute-start(f32[2,128,128]{2,1,0:T(8,128)} %get-tuple-element.46.refs_0_), channel_id=1, source_target_pairs={{0,8},{8,0},{16,24},{24,16},{32,40},{40,32},{48,56},{56,48},{64,72... | collective-permute-start | bytes 393224 | tf_op jit(solution)/shard_map/ppermute | solution.py:315
  36.9 11.2 %collective-permute-start.9 = (bf16[2,128,384]{2,1,0:T(8,128)(2,1)}, bf16[2,128,384]{2,1,0:T(8,128)(2,1)S(1)}, u32[]{:S(2)}, u32[]{:S(2)}) collective-permute-start(bf16[2,128,384]{2,1,0:T(8,128)(2,1)} %get-tuple-element.48), channel_id=1, source_target_pairs={{0,24},{8,16},{16,8},{24,0},{32,56},{40,48},{48,40},{56,32},{64,88... | collective-permute-start | bytes 589832 | tf_op jit(solution)/shard_map/ppermute | solution.py:315
  42.9 47.5 %all-to-all-start = ((bf16[8,256,256]{2,1,0:T(8,128)(2,1)}), bf16[8,256,256]{2,1,0:T(8,128)(2,1)S(1)}, u32[]{:S(2)}, u32[]{:S(2)}) async-start(bf16[8,256,256]{2,1,0:T(8,128)(2,1)} %bitcast.3), calls=%async_computation | async-start | bytes 2097152 | tf_op jit(solution)/shard_map/all_to_all | solution.py:397
  50.6 12.8 %collective-permute-start.10 = (bf16[2,128,384]{2,1,0:T(8,128)(2,1)}, bf16[2,128,384]{2,1,0:T(8,128)(2,1)S(1)}, u32[]{:S(2)}, u32[]{:S(2)}) collective-permute-start(bf16[2,128,384]{2,1,0:T(8,128)(2,1)} %get-tuple-element.52), channel_id=1, source_target_pairs={{0,56},{8,48},{16,40},{24,32},{32,24},{40,16},{48,8},{56,0},{64,12... | collective-permute-start | bytes 589832 | tf_op jit(solution)/shard_map/ppermute | solution.py:315
  66.0 11.0 %collective-permute-start.11 = (f32[2,128,384]{2,1,0:T(8,128)}, f32[2,128,384]{2,1,0:T(8,128)S(1)}, u32[]{:S(2)}, u32[]{:S(2)}) collective-permute-start(f32[2,128,384]{2,1,0:T(8,128)} %get-tuple-element.56), channel_id=1, source_target_pairs={{0,64},{8,72},{16,80},{24,88},{32,96},{40,104},{48,112},{56,120},{... | collective-permute-start | bytes 1179656 | tf_op jit(solution)/shard_map/ppermute | solution.py:315
  79.5 6.4 %collective-permute-start.12 = (f32[2,128,128]{2,1,0:T(8,128)}, f32[2,128,128]{2,1,0:T(8,128)S(1)}, u32[]{:S(2)}, u32[]{:S(2)}) collective-permute-start(f32[2,128,128]{2,1,0:T(8,128)} %get-tuple-element.61), channel_id=1, source_target_pairs={{0,192},{8,200},{16,208},{24,216},{32,224},{40,232},{48,240},{56,2... | collective-permute-start | bytes 393224 | tf_op jit(solution)/shard_map/ppermute | solution.py:315
  90.4 8.3 %copy-start.8 = (bf16[256,256]{1,0:T(8,128)(2,1)S(1)}, bf16[256,256]{1,0:T(8,128)(2,1)}, u32[]{:S(2)}) copy-start(bf16[256,256]{1,0:T(8,128)(2,1)} %get-tuple-element.65.refs_0_) | copy-start | bytes 393220
  90.5 34.4 %all-to-all-start.1 = ((bf16[32,8,2048]{2,1,0:T(8,128)(2,1)}), bf16[32,8,2048]{2,1,0:T(8,128)(2,1)S(1)}, u32[]{:S(2)}, u32[]{:S(2)}) async-start(bf16[32,8,2048]{2,1,0:T(8,128)(2,1)} %bitcast.14), calls=%async_computation.1 | async-start | bytes 2097152 | tf_op jit(solution)/shard_map/all_to_all | solution.py:452
  98.8 5.2 %collective-permute-start.13 = (bf16[256,256]{1,0:T(8,128)(2,1)S(1)}, bf16[256,256]{1,0:T(8,128)(2,1)S(1)}, u32[]{:S(2)}, u32[]{:S(2)}) collective-permute-start(bf16[256,256]{1,0:T(8,128)(2,1)S(1)} %copy-done.8), channel_id=1, source_target_pairs={{0,1},{1,0},{2,3},{3,2},{4,5},{5,4},{6,7},{7,6},{8,9},{9,8},{10,11... | collective-permute-start | bytes 393224 | tf_op jit(solution)/shard_map/ppermute | solution.py:315
  98.9 6.6 %collective-permute-start.14 = (bf16[256,256]{1,0:T(8,128)(2,1)S(1)}, bf16[256,256]{1,0:T(8,128)(2,1)S(1)}, u32[]{:S(2)}, u32[]{:S(2)}) collective-permute-start(bf16[256,256]{1,0:T(8,128)(2,1)S(1)} %copy-done.8), channel_id=1, source_target_pairs={{0,2},{1,3},{2,0},{3,1},{4,6},{5,7},{6,4},{7,5},{8,10},{9,11},{10,... | collective-permute-start | bytes 393224 | tf_op jit(solution)/shard_map/ppermute | solution.py:315
  99.0 20.2 %collective-permute-start.15 = (bf16[256,256]{1,0:T(8,128)(2,1)S(1)}, bf16[256,256]{1,0:T(8,128)(2,1)S(1)}, u32[]{:S(2)}, u32[]{:S(2)}) collective-permute-start(bf16[256,256]{1,0:T(8,128)(2,1)S(1)} %copy-done.8), channel_id=1, source_target_pairs={{0,3},{1,2},{2,1},{3,0},{4,7},{5,6},{6,5},{7,4},{8,11},{9,10},{10,... | collective-permute-start | bytes 393224 | tf_op jit(solution)/shard_map/ppermute | solution.py:315
  100.7 18.4 %collective-permute-start.16 = (bf16[256,256]{1,0:T(8,128)(2,1)S(1)}, bf16[256,256]{1,0:T(8,128)(2,1)S(1)}, u32[]{:S(2)}, u32[]{:S(2)}) collective-permute-start(bf16[256,256]{1,0:T(8,128)(2,1)S(1)} %copy-done.8), channel_id=1, source_target_pairs={{0,4},{1,5},{2,6},{3,7},{4,0},{5,1},{6,2},{7,3},{8,12},{9,13},{10,... | collective-permute-start | bytes 393224 | tf_op jit(solution)/shard_map/ppermute | solution.py:315
  102.9 16.3 %collective-permute-start.17 = (bf16[256,256]{1,0:T(8,128)(2,1)S(1)}, bf16[256,256]{1,0:T(8,128)(2,1)S(1)}, u32[]{:S(2)}, u32[]{:S(2)}) collective-permute-start(bf16[256,256]{1,0:T(8,128)(2,1)S(1)} %copy-done.8), channel_id=1, source_target_pairs={{0,5},{1,4},{2,7},{3,6},{4,1},{5,0},{6,3},{7,2},{8,13},{9,12},{10,... | collective-permute-start | bytes 393224 | tf_op jit(solution)/shard_map/ppermute | solution.py:315
  104.0 15.2 %collective-permute-start.18 = (bf16[256,256]{1,0:T(8,128)(2,1)S(1)}, bf16[256,256]{1,0:T(8,128)(2,1)S(1)}, u32[]{:S(2)}, u32[]{:S(2)}) collective-permute-start(bf16[256,256]{1,0:T(8,128)(2,1)S(1)} %copy-done.8), channel_id=1, source_target_pairs={{0,6},{1,7},{2,4},{3,5},{4,2},{5,3},{6,0},{7,1},{8,14},{9,15},{10,... | collective-permute-start | bytes 393224 | tf_op jit(solution)/shard_map/ppermute | solution.py:315
  105.4 13.8 %collective-permute-start.19 = (bf16[256,256]{1,0:T(8,128)(2,1)S(1)}, bf16[256,256]{1,0:T(8,128)(2,1)S(1)}, u32[]{:S(2)}, u32[]{:S(2)}) collective-permute-start(bf16[256,256]{1,0:T(8,128)(2,1)S(1)} %copy-done.8), channel_id=1, source_target_pairs={{0,7},{1,6},{2,5},{3,4},{4,3},{5,2},{6,1},{7,0},{8,15},{9,14},{10,... | collective-permute-start | bytes 393224 | tf_op jit(solution)/shard_map/ppermute | solution.py:315

commit v3 on v2

v3 whole, which is shorter than its diff:
```python
import functools

import jax
import jax.numpy as jnp
from jax import lax
from jax.experimental import pallas as pl
from jax.experimental.pallas import tpu as pltpu
from jax.sharding import PartitionSpec as P

HEAD_DIM = 128
BLOCK = 64
ROWS = 2 * BLOCK
RING = 8
f32 = jnp.float32
bf16 = jnp.bfloat16
NN = (((1,), (0,)), ((), ()))
NT = (((1,), (1,)), ((), ()))
TN = (((0,), (0,)), ((), ()))
SCALE = 1_000_000_000
COST = {
    "prepare": 9, "local": 5, "merge": 2, "merge_adjoint": 2, "cut": 2, "mix": 5, "gradients": 10, "project": 2
}
VMEM_LIMIT = 24 * 1024 * 1024


def halves(x):
    high = x.astype(bf16)
    return high, (x - high.astype(f32)).astype(bf16)


def dot(a, b, dims):
    return lax.dot_general(a, b, dims, preferred_element_type=f32)


def product(a, b, dims=NN):
    ah, al = a if isinstance(a, tuple) else halves(a)
    bh, bl = b if isinstance(b, tuple) else halves(b)
    (a_axis,), (b_axis,) = dims[0]
    wide = jnp.concatenate([bh, bl], axis=1 - b_axis)
    both = dot(jnp.concatenate([ah, al], axis=a_axis), jnp.concatenate([wide, wide], axis=b_axis), dims)
    cut = both.shape[1] // 2
    return both[:, :cut] + both[:, cut:]


def inverse_norm(x):
    return lax.rsqrt(jnp.sum(x * x, axis=-1, keepdims=True) + 1e-06)


def strengths(logits):
    return 2.0 / (1.0 + jnp.exp(-logits))


def token_grid():
    row = lax.broadcasted_iota(jnp.int32, (ROWS, ROWS), 0)
    col = lax.broadcasted_iota(jnp.int32, (ROWS, ROWS), 1)
    return row & (BLOCK - 1), col & (BLOCK - 1), row >= BLOCK, col >= BLOCK


def load_pairs(ref, block):
    rows = pl.ds(block * BLOCK, BLOCK)
    return jnp.concatenate([ref[rows, 0, :], ref[rows, 1, :]], axis=0)


def prepare_kernel(
    query_ref, key_ref, value_ref, logit_ref,
    system_ref, solved_ref, step_ref, prefix_ref, whole_ref, reach_ref, inner_ref,
):
    blocks = key_ref.shape[0] // BLOCK
    row_token, col_token, row_second, col_second = token_grid()
    row = lax.broadcasted_iota(jnp.int32, (ROWS, ROWS), 0)
    col = lax.broadcasted_iota(jnp.int32, (ROWS, ROWS), 1)
    same_token = row_token == col_token
    pair = same_token & row_second & ~col_second
    eye = row == col
    visible = col_token[:BLOCK] <= row_token[:BLOCK]
    units, keys, grams, systems = [], [], [], []
    for block in range(blocks):
        key = load_pairs(key_ref, block)
        unit = key * inverse_norm(key)
        parts = halves(unit)
        units.append(unit)
        keys.append(parts)
        grams.append(product(parts, parts, NT))
    for block in range(blocks):
        strength = jnp.broadcast_to(strengths(logit_ref[0, pl.ds(block, 1), :]), (ROWS, ROWS))
        swapped = jnp.broadcast_to(strengths(logit_ref[0, pl.ds(blocks + block, 1), :]), (ROWS, ROWS))
        systems.append(
            jnp.where(eye, strength, 0.0) - jnp.where(pair, grams[block] * (strength * swapped), 0.0)
        )
    size = 1
    while size < BLOCK:
        below = ((row_token & size) != 0) & ((row_token ^ col_token) < 2 * size) & ((col_token & size) == 0)
        now = [halves(system) for system in systems]
        middle = [
            product(jnp.where(below, grams[block], 0.0), now[block]) for block in range(blocks)
        ]
        systems = [
            systems[block] - product(now[block], middle[block]) for block in range(blocks)
        ]
        size *= 2
    prefix = None
    steps = []
    for block in range(blocks):
        value = load_pairs(value_ref, block)
        system_ref[0, block] = systems[block]
        solved = product(systems[block], jnp.concatenate([units[block], value], axis=1))
        solved_ref[0, block] = solved
        solved_parts = halves(solved)
        moved = product(keys[block], solved_parts, TN)
        steps.append(
            jnp.concatenate(
                [jnp.where(eye, 1.0, 0.0) - moved[:, :HEAD_DIM], moved[:, HEAD_DIM:]], axis=1
            )
        )
        step_ref[0, block] = steps[block][:, :HEAD_DIM]
        query = query_ref[pl.ds(block * BLOCK, BLOCK), :]
        query = query * inverse_norm(query)
        scores = jnp.where(visible, product(query, keys[block], NT), 0.0)
        seen = product(scores, solved_parts)
        reach_ref[0, block] = query - seen[:, :HEAD_DIM]
        inner_ref[0, block] = seen[:, HEAD_DIM:]
    prefix = steps[0]
    prefix_ref[0, 0] = prefix
    for block in range(1, blocks):
        moved = product(steps[block][:, :HEAD_DIM], prefix)
        prefix = jnp.concatenate(
            [moved[:, :HEAD_DIM], moved[:, HEAD_DIM:] + steps[block][:, HEAD_DIM:]], axis=1
        )
        prefix_ref[0, block] = prefix
    whole_ref[0] = prefix


def columns(place_ref, mask, width):
    return pl.ds(pl.multiple_of((place_ref[0] ^ mask) * width, width), width)


def local_kernel(place_ref, reach_ref, step_ref, weight_ref, *refs):
    grad_refs = refs[:-3]
    mixed_grad_ref, drive_ref, adjoint_ref = refs[-3:]
    blocks = reach_ref.shape[1]
    mixed_grad = None
    for mask, grad in each(grad_refs):
        term = dot(grad, weight_ref[:, columns(place_ref, mask, grad.shape[1])], NT)
        mixed_grad = term if mixed_grad is None else mixed_grad + term
    mixed_grad_ref[...] = mixed_grad
    drives = []
    for block in range(blocks):
        drive = product(reach_ref[0, block], mixed_grad[block * BLOCK : (block + 1) * BLOCK], TN)
        drive_ref[0, block] = drive
        drives.append(drive)
    adjoint = drives[blocks - 1]
    for block in reversed(range(blocks - 1)):
        adjoint = product(step_ref[0, block], adjoint, TN) + drives[block]
    adjoint_ref[0] = adjoint


def identity(width):
    row = lax.broadcasted_iota(jnp.int32, (HEAD_DIM, width), 0)
    return jnp.where(row == lax.broadcasted_iota(jnp.int32, (HEAD_DIM, width), 1), 1.0, 0.0)


def merge_kernel(first, last, upper_ref, own_ref, far_ref, *refs):
    before_ref, after_ref = (None, None) if first else refs[:2]
    before_out, after_out, low_out, send_ref = refs[-4:] if last else refs[-5:-1]
    upper = upper_ref[0] == 1
    d = HEAD_DIM
    for head in range(own_ref.shape[0]):
        own, far = own_ref[head], far_ref[head].astype(f32)
        low, high = jnp.where(upper, far, own), jnp.where(upper, own, far)
        cut = d if last else 0
        total = product(high[:, :d], low[:, cut:])
        total = total + high[:, d:] if last else jnp.concatenate([total[:, :d], total[:, d:] + high[:, d:]], axis=1)
        send_ref[head] = total.astype(send_ref.dtype)
        low_out[head] = low[:, :d]
        if not last:
            refs[-1][head] = total
        back = far[:, :d].T
        if first:
            before_out[head] = jnp.where(upper, far, identity(2 * d))
            after_out[head] = jnp.where(upper, identity(d), back)
        else:
            before, after = before_ref[head], after_ref[head]
            beside = jnp.where(upper, far, jnp.concatenate([back, jnp.zeros_like(back)], axis=1))
            moved = product(jnp.where(upper, before[:, :d], after), beside)
            ahead = jnp.concatenate([moved[:, :d], moved[:, d:] + before[:, d:]], axis=1)
            before_out[head] = jnp.where(upper, ahead, before)
            after_out[head] = jnp.where(upper, after, moved[:, :d])


def adjoint_kernel(first, upper_ref, own_ref, far_ref, low_ref, *refs):
    after_ref, behind_ref = (None, None) if first else refs[:2]
    behind_out, send_ref, total_out = refs[-3:]
    upper = upper_ref[0] == 1
    for head in range(own_ref.shape[0]):
        own, far = own_ref[head], far_ref[head].astype(f32)
        low, high = jnp.where(upper, far, own), jnp.where(upper, own, far)
        total = product(low_ref[head], high, TN) + low
        total_out[head] = total
        send_ref[head] = total.astype(send_ref.dtype)
        if first:
            behind_out[head] = jnp.where(upper, 0.0, far)
        else:
            behind = behind_ref[head]
            behind_out[head] = jnp.where(upper, behind, product(after_ref[head], far) + behind)


def mix_kernel(place_ref, before_ref, far_ref, prefix_ref, reach_ref, inner_ref, *refs):
    grad_refs = refs[:-3]
    states_ref, mixed_ref, weight_grad_ref = refs[-3:]
    blocks = prefix_ref.shape[1]
    before = before_ref[0]
    start = product(before[:, :HEAD_DIM], far_ref[0]) + before[:, HEAD_DIM:]
    parts = halves(start)
    for block in range(blocks):
        state = start
        if block:
            ahead = prefix_ref[0, block - 1]
            state = product(ahead[:, :HEAD_DIM], parts) + ahead[:, HEAD_DIM:]
        states_ref[0, block] = state
        mixed = product(reach_ref[0, block], state) + inner_ref[0, block]
        mixed_ref[pl.ds(block * BLOCK, BLOCK), :] = mixed.astype(bf16)
    mixed = mixed_ref[...]
    for mask, grad in each(grad_refs):
        part = columns(place_ref, mask, grad.shape[1])
        weight_grad_ref[:, part] = dot(mixed, grad, TN).astype(bf16)


def unit_pull(x, unit_grad):
    scale = inverse_norm(x)
    unit = x * scale
    return scale * (unit_grad - unit * jnp.sum(unit * unit_grad, axis=-1, keepdims=True))


def gradient_kernel(
    query_ref, key_ref, logit_ref, system_ref, solved_ref, step_ref, states_ref, drive_ref, mixed_grad_ref,
    after_ref, behind_ref, far_ref,
    query_grad_ref, key_grad_ref, value_grad_ref, logit_grad_ref,
):
    blocks = query_ref.shape[0] // BLOCK
    row = lax.broadcasted_iota(jnp.int32, (BLOCK, ROWS), 0)
    col = lax.broadcasted_iota(jnp.int32, (BLOCK, ROWS), 1)
    visible = (col & (BLOCK - 1)) <= row
    row_token, col_token, row_second, col_second = token_grid()
    earlier = (col_token < row_token) | ((col_token == row_token) & row_second & ~col_second)
    ones = jnp.ones((8, HEAD_DIM), bf16)
    adjoint = product(after_ref[0], far_ref[0]) + behind_ref[0]
    for block in reversed(range(blocks)):
        rows = pl.ds(block * BLOCK, BLOCK)
        query = query_ref[rows, :]
        key = load_pairs(key_ref, block)
        query_unit = halves(query * inverse_norm(query))
        key_unit = halves(key * inverse_norm(key))
        state = halves(states_ref[0, block])
        solved = solved_ref[0, block]
        fresh = solved[:, HEAD_DIM:] - product(solved[:, :HEAD_DIM], state)
        fresh_parts = halves(fresh)
        out_grad = halves(mixed_grad_ref[rows, :])
        after = halves(adjoint)
        scores = jnp.where(visible, product(query_unit, key_unit, NT), 0.0)
        fresh_grad = product(scores, out_grad, TN) + product(key_unit, after)
        value_grad = product(system_ref[0, block], fresh_grad, TN)
        value_parts = halves(value_grad)
        value_grad_ref[rows, 0, :] = value_grad[:BLOCK]
        value_grad_ref[rows, 1, :] = value_grad[BLOCK:]
        high, low = halves(value_grad * fresh)
        sums = dot(ones, high, NT) + dot(ones, low, NT)
        logit_grad_ref[0, pl.ds(block, 1), :] = (
            0.5 * jnp.exp(-logit_ref[0, pl.ds(block, 1), :]) * sums[0:1]
        )
        score_grad = halves(jnp.where(visible, product(out_grad, fresh_parts, NT), 0.0))
        query_unit_grad = product(out_grad, state, NT) + product(score_grad, key_unit)
        query_grad_ref[rows, :] = unit_pull(query, query_unit_grad)
        gram_grad = halves(jnp.where(earlier, product(value_parts, fresh_parts, NT), 0.0))
        key_unit_grad = (
            product(score_grad, query_unit, TN)
            + product(fresh_parts, after, NT)
            - product(value_parts, state, NT)
            - (product(gram_grad, key_unit) + product(gram_grad, key_unit, TN))
        )
        key_grad = unit_pull(key, key_unit_grad)
        key_grad_ref[rows, 0, :] = key_grad[:BLOCK]
        key_grad_ref[rows, 1, :] = key_grad[BLOCK:]
        if block:
            adjoint = product(step_ref[0, block], after, TN) + drive_ref[0, block]


def head_call(kernel, name, heads, outs, *operands, steps=None, following=()):
    def spec(kind, shape):
        rank = len(shape)
        if steps == 1 and kind != "scalar":
            return pl.BlockSpec(shape, lambda h: (0,) * rank)
        if kind in ("first", "free"):
            return pl.BlockSpec((1, *shape[1:]), lambda h: (h,) + (0,) * (rank - 1))
        if kind == "last":
            return pl.BlockSpec((*shape[:-1], HEAD_DIM), lambda h: (0,) * (rank - 1) + (h,))
        if kind == "scalar":
            return pl.BlockSpec(memory_space=pltpu.SMEM)
        if kind == "rows":
            return pl.BlockSpec((HEAD_DIM, *shape[1:]), lambda h: (h,) + (0,) * (rank - 1))
        return pl.BlockSpec(shape, lambda h: (0,) * rank)

    def run(*refs):
        kernel(*refs[len(following) :])

    return pl.pallas_call(
        run,
        name=name,
        grid=(steps or heads,),
        in_specs=[pl.BlockSpec(memory_space=pl.ANY)] * len(following)
        + [spec(kind, array.shape) for kind, array in operands],
        out_specs=[spec(kind, shape) for kind, shape, _ in outs],
        out_shape=[pltpu.HBM(shape, dtype) for _, shape, dtype in outs],
        cost_estimate=pl.CostEstimate(flops=COST[name] * SCALE, bytes_accessed=0, transcendentals=0),
        compiler_params=pltpu.CompilerParams(
            dimension_semantics=("arbitrary",), vmem_limit_bytes=VMEM_LIMIT
        ),
    )(
        *[pltpu.with_memory_space_constraint(array, pltpu.HBM) for array in following],
        *[
            array if kind in ("scalar", "free", "whole free") else pltpu.with_memory_space_constraint(array, pltpu.HBM)
            for kind, array in operands
        ]
    )


def exchanged(array, axis, mask):
    return lax.ppermute(array, axis, [(i, i ^ mask) for i in range(lax.axis_size(axis))])


def passed(array, mask, to_upper):
    half = (mask + 1) // 2 if mask < RING else mask & ~(mask >> 1)
    pairs = [(i, i ^ mask) for i in range(lax.axis_size("seq")) if ((i & half) == 0) == to_upper]
    return lax.ppermute(array, "seq", pairs)


def level_masks(count):
    masks, size = [], 1
    while size < count:
        masks.append(2 * size - 1 if size < RING else 2 * size - RING)
        size *= 2
    return masks


def gathered(array, axis):
    if lax.axis_size(axis) == 1:
        return [array[None]]
    pair = jnp.stack([array, exchanged(array, axis, 1)])
    return [pair] + [exchanged(pair, axis, mask) for mask in range(2, lax.axis_size(axis), 2)]


def each(refs):
    for place, ref in enumerate(refs):
        for part in range(ref.shape[0]):
            yield 2 * place + part, ref[part]


def cut_kernel(weight_ref, out_ref):
    width = out_ref.shape[2]
    for part in range(out_ref.shape[0]):
        out_ref[part] = weight_ref[:, part * width : (part + 1) * width]


def project_kernel(place_ref, weight_ref, *refs):
    out_ref = refs[-1]
    total = None
    for mask, mixed in each(refs[:-1]):
        term = dot(mixed, weight_ref[place_ref[0] ^ mask], NN)
        total = term if total is None else total + term
    out_ref[...] = total.astype(bf16)


def body(queries, reflect_keys, reflect_values, beta_logit, out_weight, out_grad):
    tokens, features = queries.shape
    heads = features // HEAD_DIM
    blocks = tokens // BLOCK
    square = (heads, blocks, ROWS, HEAD_DIM)
    double = (heads, blocks, ROWS, 2 * HEAD_DIM)
    parts = lax.axis_size("head")
    seq_count = lax.axis_size("seq")
    place = lax.axis_index("seq")
    head_place = lax.axis_index("head").astype(jnp.int32).reshape(1)
    grad_parts = gathered(out_grad, "head")
    keys, values = reflect_keys, reflect_values
    logits = beta_logit.reshape(2, heads, blocks, BLOCK).transpose(1, 2, 0, 3)
    logit_rows = jnp.concatenate(
        [logits.reshape(heads, blocks, ROWS), logits[:, :, ::-1].reshape(heads, blocks, ROWS)], axis=1
    )

    system, solved, step, prefix, whole, reach, inner = head_call(
        prepare_kernel,
        "prepare",
        heads,
        [
            ("first", square, f32),
            ("first", double, f32),
            ("first", square, f32),
            ("first", double, f32),
            ("first", (heads, HEAD_DIM, 2 * HEAD_DIM), f32),
            ("first", (heads, blocks, BLOCK, HEAD_DIM), f32),
            ("first", (heads, blocks, BLOCK, HEAD_DIM), f32),
        ],
        ("last", queries),
        ("last", keys),
        ("last", values),
        ("first", logit_rows),
    )
    masks = level_masks(seq_count)
    far = exchanged(whole, "seq", masks[0])
    mixed_grad, drive, adjoint = head_call(
        local_kernel,
        "local",
        heads,
        [
            ("last", (tokens, features), f32),
            ("first", square, f32),
            ("first", (heads, ROWS, HEAD_DIM), f32),
        ],
        ("scalar", head_place),
        ("first", reach),
        ("first", step),
        ("rows", out_weight),
        *[("whole free", part) for part in grad_parts],
    )
    upper = [((place >> level) & 1).astype(jnp.int32).reshape(1) for level in range(len(masks))]
    tile = (heads, HEAD_DIM, HEAD_DIM)
    wide = (heads, HEAD_DIM, 2 * HEAD_DIM)
    far_adjoint = exchanged(adjoint, "seq", masks[0])
    levels = len(masks) - 1
    total, before, after, behind = whole, None, None, None
    held = []

    def join_adjoint(level, following):
        nonlocal behind, adjoint, far_adjoint
        first, last = level == 0, level == levels - 1
        low, after_before = held[level]
        send_dtype = bf16 if level < 2 and not last else f32
        behind, sent, adjoint = head_call(
            functools.partial(adjoint_kernel, first),
            "merge_adjoint",
            heads,
            [("first", tile, f32), ("first", tile, send_dtype), ("first", tile, f32)],
            ("scalar", upper[level]),
            ("first", adjoint),
            ("free", far_adjoint),
            ("first", low),
            *([] if first else [("first", after_before), ("first", behind)]),
            steps=1,
            following=following,
        )
        far_adjoint = (
            passed(sent, masks[-1], False) if last else exchanged(sent, "seq", masks[level + 1])
        )

    for level in range(levels):
        first, last = level == 0, level == levels - 1
        if level >= 1:
            join_adjoint(level - 1, ())
        if level == min(2, levels - 1):
            (weight_cut,) = head_call(
                cut_kernel,
                "cut",
                heads,
                [("whole", (parts, features, features), bf16)],
                ("whole", out_weight),
                steps=1,
                following=(adjoint,),
            )
            weight_parts = lax.all_to_all(weight_cut, "head", 0, 0, tiled=True)
        send_dtype = bf16 if level < 2 and not last else f32
        before_join = after
        before, after, low, sent, *rest = head_call(
            functools.partial(merge_kernel, first, last),
            "merge",
            heads,
            [("first", wide, f32), ("first", tile, f32), ("first", tile, f32)]
            + ([("first", tile, f32)] if last else [("first", wide, send_dtype), ("first", wide, f32)]),
            ("scalar", upper[level]),
            ("first", total),
            ("free", far),
            *([] if first else [("first", before), ("first", after)]),
            steps=1,
            following=(adjoint, weight_cut) if level == 3 else (adjoint,),
        )
        held.append((low, before_join))
        total = rest[0] if rest else None
        far = passed(sent, masks[-1], True) if last else exchanged(sent, "seq", masks[level + 1])
    join_adjoint(levels - 1, ())
    states, mixed, weight_share = head_call(
        mix_kernel,
        "mix",
        heads,
        [("first", square, f32), ("last", (tokens, features), bf16), ("rows", out_weight.shape, bf16)],
        ("scalar", head_place),
        ("first", before),
        ("free", far),
        ("first", prefix),
        ("first", reach),
        ("first", inner),
        *[("whole", part) for part in grad_parts],
        following=(adjoint,),
    )
    weight_grad = jnp.sum(
        lax.all_to_all(
            weight_share.reshape(seq_count, features // seq_count, out_weight.shape[1]), "seq", 0, 0, tiled=True
        ).astype(f32),
        axis=0,
    )
    query_grad, key_grad, value_grad, logit_grad = head_call(
        gradient_kernel,
        "gradients",
        heads,
        [
            ("last", queries.shape, f32),
            ("last", keys.shape, f32),
            ("last", values.shape, f32),
            ("first", (heads, blocks, ROWS), f32),
        ],
        ("last", queries),
        ("last", keys),
        ("first", logit_rows),
        ("first", system),
        ("first", solved),
        ("first", step),
        ("first", states),
        ("first", drive),
        ("last", mixed_grad),
        ("first", after),
        ("first", behind),
        ("free", far_adjoint),
    )
    mixed_parts = gathered(mixed, "head")
    vmem = pl.BlockSpec(memory_space=pltpu.VMEM)
    output = pl.pallas_call(
        project_kernel,
        name="project",
        in_specs=[pl.BlockSpec(memory_space=pltpu.SMEM)] + [vmem] * (1 + len(mixed_parts)),
        out_specs=vmem,
        out_shape=jax.ShapeDtypeStruct((tokens, features), bf16),
        compiler_params=pltpu.CompilerParams(vmem_limit_bytes=VMEM_LIMIT),
    )(head_place, weight_parts, *mixed_parts)
    logit_grad = logit_grad.reshape(heads, blocks, 2, BLOCK).transpose(2, 0, 1, 3).reshape(beta_logit.shape)
    return (
        output,
        query_grad,
        key_grad,
        value_grad,
        logit_grad,
        weight_grad,
    )


def solution(mesh):
    in_specs = (
        P("seq", "head"),
        P("seq", None, "head"),
        P("seq", None, "head"),
        P(None, "head", "seq"),
        P("head", None),
        P("seq", "head"),
    )
    out_specs = (
        P("seq", "head"),
        P("seq", "head"),
        P("seq", None, "head"),
        P("seq", None, "head"),
        P(None, "head", "seq"),
        P(("head", "seq"), None),
    )
    return jax.shard_map(body, mesh=mesh, in_specs=in_specs, out_specs=out_specs, check_vma=False)
```

time: 126 us -> 117 us (0.929)
  the two profiles are of different devices: /device:TPU:2 before, /device:TPU:32 now
where the time goes in v3:
time: 117 us; the launch traced here: 116 us
  Pallas kernels  48.9 us (42%)
  starting transfers between devices  43.7 us (37%)
  waiting for transfers between devices  17.6 us (15%)
  local copies, waits for them, and re-layouts  2.46 us (2%)
  other arithmetic  2.34 us (2%)
    pallas_call x13, Pallas kernels, head_call(): pl.pallas_call(run, name=name, grid=(steps or heads,), in_specs=[pl.Block...  47.8 us
    ppermute x16, starting transfers between devices, exchanged(): lax.ppermute(array, axis, [(i, i ^ mask) for i in range(lax.axis_size(axi...  22.6 us
    all_to_all x1, starting transfers between devices, body(): lax.all_to_all(weight_share.reshape(seq_count, features // seq_count, out...  10.6 us
    ppermute x2, waiting for transfers between devices, passed(): return lax.ppermute(array, 'seq', pairs)  6.83 us
    ppermute x16, waiting for transfers between devices, exchanged(): lax.ppermute(array, axis, [(i, i ^ mask) for i in range(lax.axis_size(axi...  6.75 us
    ppermute x2, starting transfers between devices, passed(): return lax.ppermute(array, 'seq', pairs)  6.21 us
    all_to_all x1, starting transfers between devices, body(): weight_parts = lax.all_to_all(weight_cut, 'head', 0, 0, tiled=True)  4.3 us
    all_to_all x1, waiting for transfers between devices, body(): lax.all_to_all(weight_share.reshape(seq_count, features // seq_count, out...  3.99 us
  transfers between devices with their start and end apart: 20, of which 7 were waited for; matrix products, arithmetic and copies ran while one was open for 3% of the time, Pallas kernels for 42%

profile of v3, /device:TPU:32, one launch (start us, length us, event | category | flops | bytes accessed | tf_op | source)
XLA Modules:
  0.0 115.8 jit_solution(4951882970324674055)
XLA Ops:
  0.6 0.1 collective-permute-start
  0.7 0.8 reshape.48
  1.5 0.1 reshape.49
  1.6 0.1 reshape.50
  1.7 0.6 pad_maximum_fusion.2.refs_3_.refs_2_
  2.3 0.0 collective-permute-done
  2.3 0.9 pad_maximum_fusion.refs_4_.refs_7_
  3.3 0.0 copy-start
  3.3 2.8 %collective-permute-start.3 = (bf16[2,256,256]{2,1,0:T(8,128)(2,1)S(1)}, bf16[2,256,256]{2,1,0:T(8,128)(2,1)S(1)}, u32[]{:S(2)}, u32[]{:S(2)}) collective-permute-start(bf16[2,256,256]{2,1,0:T(8,128)(2,1)S(1)} %pad_maximum_fusion.refs_4_.refs_7_), channel_id=1, source_target_pairs={{0,6},{1,7},{2,4},{3,5},{4,2},{5,3},{6,0},{7,1},{8,14},{9,15},{10,... | collective-permute-start | bytes 786440 | tf_op jit(solution)/shard_map/ppermute | solution.py:327
  6.1 0.8 collective-permute-start.2
  6.9 0.5 collective-permute-start.1
  7.5 9.3 %prepare.1 = (f32[2,4,128,128]{3,2,1,0:T(8,128)}, f32[2,4,128,256]{3,2,1,0:T(8,128)}, f32[2,4,128,128]{3,2,1,0:T(8,128)}, f32[2,4,128,256]{3,2,1,0:T(8,128)}, f3...) custom-call(f32[256,256]{1,0:T(8,128)} %refs_0_.3, f32[256,2,256]{2,1,0:T(2,128)} %refs_1_.5, ...), custom_call_target="tpu_custom_call" | custom-call | flops 8999999488 | tf_op jit(solution)/shard_map/prepare/pallas_call | solution.py:305
  16.7 1.9 %collective-permute-start.5 = (f32[2,128,256]{2,1,0:T(8,128)}, f32[2,128,256]{2,1,0:T(8,128)S(1)}, u32[]{:S(2)}, u32[]{:S(2)}) collective-permute-start(f32[2,128,256]{2,1,0:T(8,128)} %get-tuple-element.57.refs_2_), channel_id=1, source_target_pairs={{0,8},{8,0},{16,24},{24,16},{32,40},{40,32},{48,56},{56,48},{64,72... | collective-permute-start | bytes 786440 | tf_op jit(solution)/shard_map/ppermute | solution.py:327
  18.6 0.3 collective-permute-done.3.refs_7_.refs_10_
  18.9 0.0 collective-permute-done.2.refs_6_.refs_9_
  18.9 0.6 collective-permute-done.1.refs_5_.refs_8_
  19.5 0.0 copy-done
  19.5 4.5 %local.1 = (f32[256,256]{1,0:T(8,128)}, f32[2,4,128,128]{3,2,1,0:T(8,128)}, f32[2,128,128]{2,1,0:T(8,128)}) custom-call(s32[1]{0:T(128)} %bitcast.refs_0_.refs_1_.place_ref, f32[2,4,64,128]{3,2,1,0:T(8,128)} %get-tuple-element.54.refs_1_.refs_5_, f32[2,4,128,128]{3,2,1,0:T(8,128)} %get-tuple-element.55.refs_2_.refs_5_, bf16[256,2048]{1,0:T(8,128)(2,1)} %refs_1_.4, ...), custom_call_target="tpu_custom_call" | custom-call | flops 5000000000 | tf_op jit(solution)/shard_map/local/pallas_call | solution.py:305
  24.0 1.9 %collective-permute-start.4 = (f32[2,128,128]{2,1,0:T(8,128)}, f32[2,128,128]{2,1,0:T(8,128)S(1)}, u32[]{:S(2)}, u32[]{:S(2)}) collective-permute-start(f32[2,128,128]{2,1,0:T(8,128)} %get-tuple-element.56.refs_0_.refs_1_), channel_id=1, source_target_pairs={{0,8},{8,0},{16,24},{24,16},{32,40},{40,32},{48,56},{56,48},{64,72... | collective-permute-start | bytes 393224 | tf_op jit(solution)/shard_map/ppermute | solution.py:327
  26.0 0.0 collective-permute-done.5.refs_3_
  26.0 2.1 %merge.4 = (f32[2,128,256]{2,1,0:T(8,128)}, f32[2,128,128]{2,1,0:T(8,128)}, f32[2,128,128]{2,1,0:T(8,128)}, bf16[2,128,256]{2,1,0:T(8,128)(2,1)}, f32[2,128,256]{2,1,0:T(8,128)}) custom-call(f32[2,128,128]{2,1,0:T(8,128)} %get-tuple-element.56.refs_0_.refs_1_, s32[1]{0:T(128)} %bitcast.2.refs_1_.refs_0_, f32[2,128,256]{2,1,0:T(8,128)} %get-tuple-element.57.refs_2_, ...), custom_call_target="tpu_custom_call" | custom-call | flops 2000000000 | tf_op jit(solution)/shard_map/merge/pallas_call | solution.py:305
  28.1 2.0 %collective-permute-start.7 = (bf16[2,128,256]{2,1,0:T(8,128)(2,1)}, bf16[2,128,256]{2,1,0:T(8,128)(2,1)S(1)}, u32[]{:S(2)}, u32[]{:S(2)}) collective-permute-start(bf16[2,128,256]{2,1,0:T(8,128)(2,1)} %get-tuple-element.62), channel_id=1, source_target_pairs={{0,24},{8,16},{16,8},{24,0},{32,56},{40,48},{48,40},{56,32},{64,88... | collective-permute-start | bytes 393224 | tf_op jit(solution)/shard_map/ppermute | solution.py:327
  30.0 0.0 collective-permute-done.4.refs_2_
  30.1 1.9 %merge_adjoint.4 = (f32[2,128,128]{2,1,0:T(8,128)}, bf16[2,128,128]{2,1,0:T(8,128)(2,1)}, f32[2,128,128]{2,1,0:T(8,128)}) custom-call(s32[1]{0:T(128)} %bitcast.2.refs_1_.refs_0_, f32[2,128,128]{2,1,0:T(8,128)} %get-tuple-element.56.refs_0_.refs_1_, f32[2,128,128]{2,1,0:T(8,128)S(1)} %collective-permute-done.4.refs_2_, f32[2,128,128]{2,1,0:T(8,128)} %get-tuple-element.58.refs_3_), custom_call_target="tpu_custom_call" | custom-call | flops 2000000000 | tf_op jit(solution)/shard_map/merge_adjoint/pallas_call | solution.py:305
  31.9 1.2 %collective-permute-start.6 = (bf16[2,128,128]{2,1,0:T(8,128)(2,1)}, bf16[2,128,128]{2,1,0:T(8,128)(2,1)S(1)}, u32[]{:S(2)}, u32[]{:S(2)}) collective-permute-start(bf16[2,128,128]{2,1,0:T(8,128)(2,1)} %get-tuple-element.60), channel_id=1, source_target_pairs={{0,24},{8,16},{16,8},{24,0},{32,56},{40,48},{48,40},{56,32},{64,88... | collective-permute-start | bytes 196616 | tf_op jit(solution)/shard_map/ppermute | solution.py:327
  33.1 4.1 %collective-permute-done.7.refs_3_ = bf16[2,128,256]{2,1,0:T(8,128)(2,1)S(1)} collective-permute-done((bf16[2,128,256]{2,1,0:T(8,128)(2,1)}, bf16[2,128,256]{2,1,0:T(8,128)(2,1)S(1)}, u32[]{:S(2)}, u32[]{:S(2)}) %collective-permute-start.7) | collective-permute-done | bytes 131104 | tf_op jit(solution)/shard_map/ppermute | solution.py:327
  37.2 2.3 %merge.5 = (f32[2,128,256]{2,1,0:T(8,128)}, f32[2,128,128]{2,1,0:T(8,128)}, f32[2,128,128]{2,1,0:T(8,128)}, bf16[2,128,256]{2,1,0:T(8,128)(2,1)}, f32[2,128,256]{2,1,0:T(8,128)}) custom-call(f32[2,128,128]{2,1,0:T(8,128)} %get-tuple-element.59.refs_0_.refs_1_, s32[1]{0:T(128)} %bitcast.1.refs_1_.refs_0_, f32[2,128,256]{2,1,0:T(8,128)} %get-tuple-element.61.refs_2_, ...), custom_call_target="tpu_custom_call" | custom-call | flops 2000000000 | tf_op jit(solution)/shard_map/merge/pallas_call | solution.py:305
  39.4 4.9 %collective-permute-start.9 = (bf16[2,128,256]{2,1,0:T(8,128)(2,1)}, bf16[2,128,256]{2,1,0:T(8,128)(2,1)S(1)}, u32[]{:S(2)}, u32[]{:S(2)}) collective-permute-start(bf16[2,128,256]{2,1,0:T(8,128)(2,1)} %get-tuple-element.70), channel_id=1, source_target_pairs={{0,56},{8,48},{16,40},{24,32},{32,24},{40,16},{48,8},{56,0},{64,12... | collective-permute-start | bytes 393224 | tf_op jit(solution)/shard_map/ppermute | solution.py:327
  44.3 0.0 collective-permute-done.6.refs_2_
  44.3 2.0 %merge_adjoint.5 = (f32[2,128,128]{2,1,0:T(8,128)}, bf16[2,128,128]{2,1,0:T(8,128)(2,1)}, f32[2,128,128]{2,1,0:T(8,128)}) custom-call(s32[1]{0:T(128)} %bitcast.1.refs_1_.refs_0_, f32[2,128,128]{2,1,0:T(8,128)} %get-tuple-element.59.refs_0_.refs_1_, bf16[2,128,128]{2,1,0:T(8,128)(2,1)S(1)} %collective-permute-done.6.refs_2_, ...), custom_call_target="tpu_custom_call" | custom-call | flops 2000000000 | tf_op jit(solution)/shard_map/merge_adjoint/pallas_call | solution.py:305
  46.4 0.2 collective-permute-start.8
  46.5 1.8 %collective-permute-done.9.refs_3_ = bf16[2,128,256]{2,1,0:T(8,128)(2,1)S(1)} collective-permute-done((bf16[2,128,256]{2,1,0:T(8,128)(2,1)}, bf16[2,128,256]{2,1,0:T(8,128)(2,1)S(1)}, u32[]{:S(2)}, u32[]{:S(2)}) %collective-permute-start.9) | collective-permute-done | bytes 131104 | tf_op jit(solution)/shard_map/ppermute | solution.py:327
  48.3 2.3 %merge.6 = (f32[2,128,256]{2,1,0:T(8,128)}, f32[2,128,128]{2,1,0:T(8,128)}, f32[2,128,128]{2,1,0:T(8,128)}, f32[2,128,256]{2,1,0:T(8,128)}, f32[2,128,256]{2,1,0:T(8,128)}) custom-call(f32[2,128,128]{2,1,0:T(8,128)} %get-tuple-element.67.refs_0_.refs_1_, s32[1]{0:T(128)} %bitcast.7.refs_1_.refs_0_, f32[2,128,256]{2,1,0:T(8,128)} %get-tuple-element.69.refs_2_, ...), custom_call_target="tpu_custom_call" | custom-call | flops 2000000000 | tf_op jit(solution)/shard_map/merge/pallas_call | solution.py:305
  50.6 1.6 %collective-permute-start.11 = (f32[2,128,256]{2,1,0:T(8,128)}, f32[2,128,256]{2,1,0:T(8,128)S(1)}, u32[]{:S(2)}, u32[]{:S(2)}) collective-permute-start(f32[2,128,256]{2,1,0:T(8,128)} %get-tuple-element.78), channel_id=1, source_target_pairs={{0,64},{8,72},{16,80},{24,88},{32,96},{40,104},{48,112},{56,120},{... | collective-permute-start | bytes 786440 | tf_op jit(solution)/shard_map/ppermute | solution.py:327
  52.2 2.3 %cut.1.refs_1_ = bf16[8,256,256]{2,1,0:T(8,128)(2,1)} custom-call(f32[2,128,128]{2,1,0:T(8,128)} %get-tuple-element.67.refs_0_.refs_1_, bf16[256,2048]{1,0:T(8,128)(2,1)} %refs_1_.4), custom_call_target="tpu_custom_call" | custom-call | flops 2000000000 | tf_op jit(solution)/shard_map/cut/pallas_call | solution.py:305
  54.5 4.3 %all-to-all-start = ((bf16[8,256,256]{2,1,0:T(8,128)(2,1)}), bf16[8,256,256]{2,1,0:T(8,128)(2,1)S(1)}, u32[]{:S(2)}, u32[]{:S(2)}) async-start(bf16[8,256,256]{2,1,0:T(8,128)(2,1)} %cut.1.refs_1_), calls=%async_computation | async-start | bytes 2097152 | tf_op jit(solution)/shard_map/all_to_all | solution.py:468
  58.8 0.0 collective-permute-done.8.refs_2_
  58.8 2.1 %merge_adjoint.6 = (f32[2,128,128]{2,1,0:T(8,128)}, f32[2,128,128]{2,1,0:T(8,128)}, f32[2,128,128]{2,1,0:T(8,128)}) custom-call(s32[1]{0:T(128)} %bitcast.7.refs_1_.refs_0_, f32[2,128,128]{2,1,0:T(8,128)} %get-tuple-element.67.refs_0_.refs_1_, bf16[2,128,128]{2,1,0:T(8,128)(2,1)S(1)} %collective-permute-done.8.refs_2_, ...), custom_call_target="tpu_custom_call" | custom-call | flops 2000000000 | tf_op jit(solution)/shard_map/merge_adjoint/pallas_call | solution.py:305
  60.9 0.4 collective-permute-start.10
  61.4 0.0 collective-permute-done.11.refs_4_
  61.4 2.2 %merge.7 = (f32[2,128,256]{2,1,0:T(8,128)}, f32[2,128,128]{2,1,0:T(8,128)}, f32[2,128,128]{2,1,0:T(8,128)}, f32[2,128,128]{2,1,0:T(8,128)}) custom-call(f32[2,128,128]{2,1,0:T(8,128)} %get-tuple-element.75.refs_0_.refs_1_, bf16[8,256,256]{2,1,0:T(8,128)(2,1)} %cut.1.refs_1_, s32[1]{0:T(128)} %bitcast.6.refs_2_.refs_0_, ...), custom_call_target="tpu_custom_call" | custom-call | flops 2000000000 | tf_op jit(solution)/shard_map/merge/pallas_call | solution.py:305
  63.6 4.9 %collective-permute-start.12 = (f32[2,128,128]{2,1,0:T(8,128)}, f32[2,128,128]{2,1,0:T(8,128)S(1)}, u32[]{:S(2)}, u32[]{:S(2)}) collective-permute-start(f32[2,128,128]{2,1,0:T(8,128)} %get-tuple-element.85), channel_id=1, source_target_pairs={{0,192},{8,200},{16,208},{24,216},{32,224},{40,232},{48,240},{56,2... | collective-permute-start | bytes 393224 | tf_op jit(solution)/shard_map/ppermute | solution.py:333
  68.5 0.0 collective-permute-done.10.refs_2_
  68.5 2.1 %merge_adjoint.7 = (f32[2,128,128]{2,1,0:T(8,128)}, f32[2,128,128]{2,1,0:T(8,128)}, f32[2,128,128]{2,1,0:T(8,128)}) custom-call(s32[1]{0:T(128)} %bitcast.6.refs_2_.refs_0_, f32[2,128,128]{2,1,0:T(8,128)} %get-tuple-element.75.refs_0_.refs_1_, f32[2,128,128]{2,1,0:T(8,128)S(1)} %collective-permute-done.10.refs_2_, f32[2,128,128]{2,1,0:T(8,128)} %get-tuple-element.81.refs_3_, ...), custom_call_target="tpu_custom_call" | custom-call | flops 2000000000 | tf_op jit(solution)/shard_map/merge_adjoint/pallas_call | solution.py:305
  70.6 1.3 %collective-permute-done.12.refs_3_ = f32[2,128,128]{2,1,0:T(8,128)S(1)} collective-permute-done((f32[2,128,128]{2,1,0:T(8,128)}, f32[2,128,128]{2,1,0:T(8,128)S(1)}, u32[]{:S(2)}, u32[]{:S(2)}) %collective-permute-start.12) | collective-permute-done | bytes 131104 | tf_op jit(solution)/shard_map/ppermute | solution.py:333
  71.9 4.4 %mix.1 = (f32[2,4,128,128]{3,2,1,0:T(8,128)}, bf16[256,256]{1,0:T(8,128)(2,1)}, bf16[256,2048]{1,0:T(8,128)(2,1)}) custom-call(f32[2,128,128]{2,1,0:T(8,128)} %get-tuple-element.83.refs_0_, s32[1]{0:T(128)} %bitcast.refs_0_.refs_1_.place_ref, f32[2,128,256]{2,1,0:T(8,128)} %get-tuple-element.84.refs_2_, f32[2,128,128]{2,1,0:T(8,128)S(1)} %collective-permute-done.12.refs_3_, ...), custom_call_target="tpu_custom_call" | custom-call | flops 5000000000 | tf_op jit(solution)/shard_map/mix/pallas_call | solution.py:305
  76.3 0.0 all-to-all-done.weight_ref
  76.4 10.6 %all-to-all-start.1 = ((bf16[32,8,2048]{2,1,0:T(8,128)(2,1)}), bf16[32,8,2048]{2,1,0:T(8,128)(2,1)S(1)}, u32[]{:S(2)}, u32[]{:S(2)}) async-start(bf16[32,8,2048]{2,1,0:T(8,128)(2,1)} %bitcast.14), calls=%async_computation.1 | async-start | bytes 2097152 | tf_op jit(solution)/shard_map/all_to_all | solution.py:503
  87.0 0.1 collective-permute-start.13
  87.1 1.3 %collective-permute-start.17 = (f32[2,128,128]{2,1,0:T(8,128)S(1)}, f32[2,128,128]{2,1,0:T(8,128)S(1)}, u32[]{:S(2)}, u32[]{:S(2)}) collective-permute-start(f32[2,128,128]{2,1,0:T(8,128)S(1)} %copy-done.5), channel_id=1, source_target_pairs={{128,64},{136,72},{144,80},{152,88},{160,96},{168,104},{176,112},{... | collective-permute-start | bytes 393224 | tf_op jit(solution)/shard_map/ppermute | solution.py:333
  88.4 0.0 collective-permute-done.13
  88.4 3.0 %collective-permute-start.16 = (bf16[2,256,256]{2,1,0:T(8,128)(2,1)S(1)}, bf16[2,256,256]{2,1,0:T(8,128)(2,1)S(1)}, u32[]{:S(2)}, u32[]{:S(2)}) collective-permute-start(bf16[2,256,256]{2,1,0:T(8,128)(2,1)S(1)} %pad_maximum_fusion.1.refs_0_), channel_id=1, source_target_pairs={{0,6},{1,7},{2,4},{3,5},{4,2},{5,3},{6,0},{7,1},{8,14},{9,15},{10,... | collective-permute-start | bytes 786440 | tf_op jit(solution)/shard_map/ppermute | solution.py:327
  91.4 0.9 collective-permute-start.15
  92.3 0.4 collective-permute-start.14
  92.6 5.5 %collective-permute-done.17.refs_11_ = f32[2,128,128]{2,1,0:T(8,128)S(1)} collective-permute-done((f32[2,128,128]{2,1,0:T(8,128)S(1)}, f32[2,128,128]{2,1,0:T(8,128)S(1)}, u32[]{:S(2)}, u32[]{:S(2)}) %collective-permute-start.17) | collective-permute-done | bytes 131104 | tf_op jit(solution)/shard_map/ppermute | solution.py:333
  98.2 10.3 %gradients.1 = (f32[256,256]{1,0:T(8,128)}, f32[256,2,256]{2,1,0:T(2,128)}, f32[256,2,256]{2,1,0:T(2,128)}, f32[2,4,128]{2,1,0:T(4,128)}) custom-call(f32[256,256]{1,0:T(8,128)} %refs_0_.3, f32[256,2,256]{2,1,0:T(2,128)} %refs_1_.5, f32[2,8,128]{2,1,0:T(8,128)} %pad_maximum_fusion.2.refs_3_.refs_2_, f32[2,4,128,128]{3,2,1,0:T(8,128)} %get-tuple-element.89.refs_3_, ...), custom_call_target="tpu_custom_call" | custom-call | flops 10000000000 | tf_op jit(solution)/shard_map/gradients/pallas_call | solution.py:305
  108.5 0.8 reshape.53
  109.3 0.7 reshape.54
  110.0 0.0 collective-permute-done.16.refs_3_
  110.0 0.0 collective-permute-done.15.refs_2_
  110.0 0.0 collective-permute-done.14.refs_1_
  110.0 1.1 project.1
  111.1 4.0 %all-to-all-done.1 = bf16[32,8,2048]{2,1,0:T(8,128)(2,1)S(1)} async-done(((bf16[32,8,2048]{2,1,0:T(8,128)(2,1)}), bf16[32,8,2048]{2,1,0:T(8,128)(2,1)S(1)}, u32[]{:S(2)}, u32[]{:S(2)}) %all-to-all-start.1) | async-done | bytes 1048608 | tf_op jit(solution)/shard_map/all_to_all | solution.py:503
  115.0 0.8 convert_reduce_fusion
  (14 shorter events, 0.1 us)
Async XLA Ops:
  0.6 1.7 %collective-permute-start = (bf16[256,256]{1,0:T(8,128)(2,1)}, bf16[256,256]{1,0:T(8,128)(2,1)S(1)}, u32[]{:S(2)}, u32[]{:S(2)}) collective-permute-start(bf16[256,256]{1,0:T(8,128)(2,1)} %param.11), channel_id=1, source_target_pairs={{0,1},{1,0},{2,3},{3,2},{4,5},{5,4},{6,7},{7,6},{8,9},{9,8},{10,11... | collective-permute-start | bytes 393224 | tf_op jit(solution)/shard_map/ppermute | solution.py:327
  3.3 16.3 %copy-start = (bf16[2,256,256]{2,1,0:T(8,128)(2,1)}, bf16[2,256,256]{2,1,0:T(8,128)(2,1)S(1)}, u32[]{:S(2)}) copy-start(bf16[2,256,256]{2,1,0:T(8,128)(2,1)S(1)} %pad_maximum_fusion.refs_4_.refs_7_) | copy-start | bytes 786436
  3.3 15.6 %collective-permute-start.3 = (bf16[2,256,256]{2,1,0:T(8,128)(2,1)S(1)}, bf16[2,256,256]{2,1,0:T(8,128)(2,1)S(1)}, u32[]{:S(2)}, u32[]{:S(2)}) collective-permute-start(bf16[2,256,256]{2,1,0:T(8,128)(2,1)S(1)} %pad_maximum_fusion.refs_4_.refs_7_), channel_id=1, source_target_pairs={{0,6},{1,7},{2,4},{3,5},{4,2},{5,3},{6,0},{7,1},{8,14},{9,15},{10,... | collective-permute-start | bytes 786440 | tf_op jit(solution)/shard_map/ppermute | solution.py:327
  6.1 12.8 %collective-permute-start.2 = (bf16[2,256,256]{2,1,0:T(8,128)(2,1)S(1)}, bf16[2,256,256]{2,1,0:T(8,128)(2,1)S(1)}, u32[]{:S(2)}, u32[]{:S(2)}) collective-permute-start(bf16[2,256,256]{2,1,0:T(8,128)(2,1)S(1)} %pad_maximum_fusion.refs_4_.refs_7_), channel_id=1, source_target_pairs={{0,4},{1,5},{2,6},{3,7},{4,0},{5,1},{6,2},{7,3},{8,12},{9,13},{10,... | collective-permute-start | bytes 786440 | tf_op jit(solution)/shard_map/ppermute | solution.py:327
  6.9 12.6 %collective-permute-start.1 = (bf16[2,256,256]{2,1,0:T(8,128)(2,1)S(1)}, bf16[2,256,256]{2,1,0:T(8,128)(2,1)S(1)}, u32[]{:S(2)}, u32[]{:S(2)}) collective-permute-start(bf16[2,256,256]{2,1,0:T(8,128)(2,1)S(1)} %pad_maximum_fusion.refs_4_.refs_7_), channel_id=1, source_target_pairs={{0,2},{1,3},{2,0},{3,1},{4,6},{5,7},{6,4},{7,5},{8,10},{9,11},{10,... | collective-permute-start | bytes 786440 | tf_op jit(solution)/shard_map/ppermute | solution.py:327
  16.7 9.3 %collective-permute-start.5 = (f32[2,128,256]{2,1,0:T(8,128)}, f32[2,128,256]{2,1,0:T(8,128)S(1)}, u32[]{:S(2)}, u32[]{:S(2)}) collective-permute-start(f32[2,128,256]{2,1,0:T(8,128)} %get-tuple-element.57.refs_2_), channel_id=1, source_target_pairs={{0,8},{8,0},{16,24},{24,16},{32,40},{40,32},{48,56},{56,48},{64,72... | collective-permute-start | bytes 786440 | tf_op jit(solution)/shard_map/ppermute | solution.py:327
  18.9 5.1 %copy-start.1 = (bf16[2,256,256]{2,1,0:T(8,128)(2,1)}, bf16[2,256,256]{2,1,0:T(8,128)(2,1)S(1)}, u32[]{:S(2)}) copy-start(bf16[2,256,256]{2,1,0:T(8,128)(2,1)S(1)} %collective-permute-done.3.refs_7_.refs_10_) | copy-start | bytes 786436
  18.9 5.1 %copy-start.2 = (bf16[2,256,256]{2,1,0:T(8,128)(2,1)}, bf16[2,256,256]{2,1,0:T(8,128)(2,1)S(1)}, u32[]{:S(2)}) copy-start(bf16[2,256,256]{2,1,0:T(8,128)(2,1)S(1)} %collective-permute-done.2.refs_6_.refs_9_) | copy-start | bytes 786436
  19.5 4.5 %copy-start.3 = (bf16[2,256,256]{2,1,0:T(8,128)(2,1)}, bf16[2,256,256]{2,1,0:T(8,128)(2,1)S(1)}, u32[]{:S(2)}) copy-start(bf16[2,256,256]{2,1,0:T(8,128)(2,1)S(1)} %collective-permute-done.1.refs_5_.refs_8_) | copy-start | bytes 786436
  24.0 6.0 %collective-permute-start.4 = (f32[2,128,128]{2,1,0:T(8,128)}, f32[2,128,128]{2,1,0:T(8,128)S(1)}, u32[]{:S(2)}, u32[]{:S(2)}) collective-permute-start(f32[2,128,128]{2,1,0:T(8,128)} %get-tuple-element.56.refs_0_.refs_1_), channel_id=1, source_target_pairs={{0,8},{8,0},{16,24},{24,16},{32,40},{40,32},{48,56},{56,48},{64,72... | collective-permute-start | bytes 393224 | tf_op jit(solution)/shard_map/ppermute | solution.py:327
  28.1 9.1 %collective-permute-start.7 = (bf16[2,128,256]{2,1,0:T(8,128)(2,1)}, bf16[2,128,256]{2,1,0:T(8,128)(2,1)S(1)}, u32[]{:S(2)}, u32[]{:S(2)}) collective-permute-start(bf16[2,128,256]{2,1,0:T(8,128)(2,1)} %get-tuple-element.62), channel_id=1, source_target_pairs={{0,24},{8,16},{16,8},{24,0},{32,56},{40,48},{48,40},{56,32},{64,88... | collective-permute-start | bytes 393224 | tf_op jit(solution)/shard_map/ppermute | solution.py:327
  31.9 12.4 %collective-permute-start.6 = (bf16[2,128,128]{2,1,0:T(8,128)(2,1)}, bf16[2,128,128]{2,1,0:T(8,128)(2,1)S(1)}, u32[]{:S(2)}, u32[]{:S(2)}) collective-permute-start(bf16[2,128,128]{2,1,0:T(8,128)(2,1)} %get-tuple-element.60), channel_id=1, source_target_pairs={{0,24},{8,16},{16,8},{24,0},{32,56},{40,48},{48,40},{56,32},{64,88... | collective-permute-start | bytes 196616 | tf_op jit(solution)/shard_map/ppermute | solution.py:327
  39.4 8.9 %collective-permute-start.9 = (bf16[2,128,256]{2,1,0:T(8,128)(2,1)}, bf16[2,128,256]{2,1,0:T(8,128)(2,1)S(1)}, u32[]{:S(2)}, u32[]{:S(2)}) collective-permute-start(bf16[2,128,256]{2,1,0:T(8,128)(2,1)} %get-tuple-element.70), channel_id=1, source_target_pairs={{0,56},{8,48},{16,40},{24,32},{32,24},{40,16},{48,8},{56,0},{64,12... | collective-permute-start | bytes 393224 | tf_op jit(solution)/shard_map/ppermute | solution.py:327
  46.4 12.5 %collective-permute-start.8 = (bf16[2,128,128]{2,1,0:T(8,128)(2,1)}, bf16[2,128,128]{2,1,0:T(8,128)(2,1)S(1)}, u32[]{:S(2)}, u32[]{:S(2)}) collective-permute-start(bf16[2,128,128]{2,1,0:T(8,128)(2,1)} %get-tuple-element.68), channel_id=1, source_target_pairs={{0,56},{8,48},{16,40},{24,32},{32,24},{40,16},{48,8},{56,0},{64,12... | collective-permute-start | bytes 196616 | tf_op jit(solution)/shard_map/ppermute | solution.py:327
  50.6 10.7 %collective-permute-start.11 = (f32[2,128,256]{2,1,0:T(8,128)}, f32[2,128,256]{2,1,0:T(8,128)S(1)}, u32[]{:S(2)}, u32[]{:S(2)}) collective-permute-start(f32[2,128,256]{2,1,0:T(8,128)} %get-tuple-element.78), channel_id=1, source_target_pairs={{0,64},{8,72},{16,80},{24,88},{32,96},{40,104},{48,112},{56,120},{... | collective-permute-start | bytes 786440 | tf_op jit(solution)/shard_map/ppermute | solution.py:327
  54.5 21.8 %all-to-all-start = ((bf16[8,256,256]{2,1,0:T(8,128)(2,1)}), bf16[8,256,256]{2,1,0:T(8,128)(2,1)S(1)}, u32[]{:S(2)}, u32[]{:S(2)}) async-start(bf16[8,256,256]{2,1,0:T(8,128)(2,1)} %cut.1.refs_1_), calls=%async_computation | async-start | bytes 2097152 | tf_op jit(solution)/shard_map/all_to_all | solution.py:468
  60.9 7.6 %collective-permute-start.10 = (f32[2,128,128]{2,1,0:T(8,128)}, f32[2,128,128]{2,1,0:T(8,128)S(1)}, u32[]{:S(2)}, u32[]{:S(2)}) collective-permute-start(f32[2,128,128]{2,1,0:T(8,128)} %get-tuple-element.76), channel_id=1, source_target_pairs={{0,64},{8,72},{16,80},{24,88},{32,96},{40,104},{48,112},{56,120},{... | collective-permute-start | bytes 393224 | tf_op jit(solution)/shard_map/ppermute | solution.py:327
  63.6 8.4 %collective-permute-start.12 = (f32[2,128,128]{2,1,0:T(8,128)}, f32[2,128,128]{2,1,0:T(8,128)S(1)}, u32[]{:S(2)}, u32[]{:S(2)}) collective-permute-start(f32[2,128,128]{2,1,0:T(8,128)} %get-tuple-element.85), channel_id=1, source_target_pairs={{0,192},{8,200},{16,208},{24,216},{32,224},{40,232},{48,240},{56,2... | collective-permute-start | bytes 393224 | tf_op jit(solution)/shard_map/ppermute | solution.py:333
  76.3 10.6 %copy-start.4 = (bf16[256,256]{1,0:T(8,128)(2,1)S(1)}, bf16[256,256]{1,0:T(8,128)(2,1)}, u32[]{:S(2)}) copy-start(bf16[256,256]{1,0:T(8,128)(2,1)} %get-tuple-element.88) | copy-start | bytes 393220
  76.4 10.7 %copy-start.5 = (f32[2,128,128]{2,1,0:T(8,128)S(1)}, f32[2,128,128]{2,1,0:T(8,128)}, u32[]{:S(2)}) copy-start(f32[2,128,128]{2,1,0:T(8,128)} %get-tuple-element.96) | copy-start | bytes 393220
  76.4 38.7 %all-to-all-start.1 = ((bf16[32,8,2048]{2,1,0:T(8,128)(2,1)}), bf16[32,8,2048]{2,1,0:T(8,128)(2,1)S(1)}, u32[]{:S(2)}, u32[]{:S(2)}) async-start(bf16[32,8,2048]{2,1,0:T(8,128)(2,1)} %bitcast.14), calls=%async_computation.1 | async-start | bytes 2097152 | tf_op jit(solution)/shard_map/all_to_all | solution.py:503
  87.0 1.4 %collective-permute-start.13 = (bf16[256,256]{1,0:T(8,128)(2,1)S(1)}, bf16[256,256]{1,0:T(8,128)(2,1)S(1)}, u32[]{:S(2)}, u32[]{:S(2)}) collective-permute-start(bf16[256,256]{1,0:T(8,128)(2,1)S(1)} %copy-done.4), channel_id=1, source_target_pairs={{0,1},{1,0},{2,3},{3,2},{4,5},{5,4},{6,7},{7,6},{8,9},{9,8},{10,11... | collective-permute-start | bytes 393224 | tf_op jit(solution)/shard_map/ppermute | solution.py:327
  87.1 11.1 %collective-permute-start.17 = (f32[2,128,128]{2,1,0:T(8,128)S(1)}, f32[2,128,128]{2,1,0:T(8,128)S(1)}, u32[]{:S(2)}, u32[]{:S(2)}) collective-permute-start(f32[2,128,128]{2,1,0:T(8,128)S(1)} %copy-done.5), channel_id=1, source_target_pairs={{128,64},{136,72},{144,80},{152,88},{160,96},{168,104},{176,112},{... | collective-permute-start | bytes 393224 | tf_op jit(solution)/shard_map/ppermute | solution.py:333
  88.4 21.5 %collective-permute-start.16 = (bf16[2,256,256]{2,1,0:T(8,128)(2,1)S(1)}, bf16[2,256,256]{2,1,0:T(8,128)(2,1)S(1)}, u32[]{:S(2)}, u32[]{:S(2)}) collective-permute-start(bf16[2,256,256]{2,1,0:T(8,128)(2,1)S(1)} %pad_maximum_fusion.1.refs_0_), channel_id=1, source_target_pairs={{0,6},{1,7},{2,4},{3,5},{4,2},{5,3},{6,0},{7,1},{8,14},{9,15},{10,... | collective-permute-start | bytes 786440 | tf_op jit(solution)/shard_map/ppermute | solution.py:327
  91.4 18.6 %collective-permute-start.15 = (bf16[2,256,256]{2,1,0:T(8,128)(2,1)S(1)}, bf16[2,256,256]{2,1,0:T(8,128)(2,1)S(1)}, u32[]{:S(2)}, u32[]{:S(2)}) collective-permute-start(bf16[2,256,256]{2,1,0:T(8,128)(2,1)S(1)} %pad_maximum_fusion.1.refs_0_), channel_id=1, source_target_pairs={{0,4},{1,5},{2,6},{3,7},{4,0},{5,1},{6,2},{7,3},{8,12},{9,13},{10,... | collective-permute-start | bytes 786440 | tf_op jit(solution)/shard_map/ppermute | solution.py:327
  92.3 17.7 %collective-permute-start.14 = (bf16[2,256,256]{2,1,0:T(8,128)(2,1)S(1)}, bf16[2,256,256]{2,1,0:T(8,128)(2,1)S(1)}, u32[]{:S(2)}, u32[]{:S(2)}) collective-permute-start(bf16[2,256,256]{2,1,0:T(8,128)(2,1)S(1)} %pad_maximum_fusion.1.refs_0_), channel_id=1, source_target_pairs={{0,2},{1,3},{2,0},{3,1},{4,6},{5,7},{6,4},{7,5},{8,10},{9,11},{10,... | collective-permute-start | bytes 786440 | tf_op jit(solution)/shard_map/ppermute | solution.py:327

commit v4 on v3

--- a/solution.py
+++ b/solution.py
@@ -16,9 +16,9 @@
 NN = (((1,), (0,)), ((), ()))
 NT = (((1,), (1,)), ((), ()))
 TN = (((0,), (0,)), ((), ()))
-SCALE = 1_000_000_000
+SCALE = 2_000_000_000
 COST = {
-    "prepare": 9, "local": 5, "merge": 2, "merge_adjoint": 2, "cut": 2, "mix": 5, "gradients": 10, "project": 2
+    "prepare": 9, "local": 5, "merge": 2, "merge_adjoint": 2, "mix": 5, "gradients": 3, "project": 3
 }
 VMEM_LIMIT = 24 * 1024 * 1024
 
@@ -309,7 +309,10 @@
         in_specs=[pl.BlockSpec(memory_space=pl.ANY)] * len(following)
         + [spec(kind, array.shape) for kind, array in operands],
         out_specs=[spec(kind, shape) for kind, shape, _ in outs],
-        out_shape=[pltpu.HBM(shape, dtype) for _, shape, dtype in outs],
+        out_shape=[
+            jax.ShapeDtypeStruct(shape, dtype) if kind == "free" else pltpu.HBM(shape, dtype)
+            for kind, shape, dtype in outs
+        ],
         cost_estimate=pl.CostEstimate(flops=COST[name] * SCALE, bytes_accessed=0, transcendentals=0),
         compiler_params=pltpu.CompilerParams(
             dimension_semantics=("arbitrary",), vmem_limit_bytes=VMEM_LIMIT
@@ -354,19 +357,11 @@
             yield 2 * place + part, ref[part]
 
 
-def cut_kernel(weight_ref, out_ref):
-    width = out_ref.shape[2]
-    for part in range(out_ref.shape[0]):
-        out_ref[part] = weight_ref[:, part * width : (part + 1) * width]
-
-
-def project_kernel(place_ref, weight_ref, *refs):
-    out_ref = refs[-1]
-    total = None
-    for mask, mixed in each(refs[:-1]):
-        term = dot(mixed, weight_ref[place_ref[0] ^ mask], NN)
-        total = term if total is None else total + term
-    out_ref[...] = total.astype(bf16)
+def project_kernel(place_ref, mixed_ref, weight_ref, own_ref, *sent_refs):
+    mixed = mixed_ref[...]
+    for mask, ref in enumerate((own_ref, *sent_refs)):
+        share = dot(mixed, weight_ref[:, columns(place_ref, mask, ref.shape[1])], NN)
+        ref[...] = share.astype(ref.dtype)
 
 
 def body(queries, reflect_keys, reflect_values, beta_logit, out_weight, out_grad):
@@ -438,7 +433,7 @@
             functools.partial(adjoint_kernel, first),
             "merge_adjoint",
             heads,
-            [("first", tile, f32), ("first", tile, send_dtype), ("first", tile, f32)],
+            [("first", tile, f32), ("free", tile, send_dtype), ("first", tile, f32)],
             ("scalar", upper[level]),
             ("first", adjoint),
             ("free", far_adjoint),
@@ -455,17 +450,6 @@
         first, last = level == 0, level == levels - 1
         if level >= 1:
             join_adjoint(level - 1, ())
-        if level == min(2, levels - 1):
-            (weight_cut,) = head_call(
-                cut_kernel,
-                "cut",
-                heads,
-                [("whole", (parts, features, features), bf16)],
-                ("whole", out_weight),
-                steps=1,
-                following=(adjoint,),
-            )
-            weight_parts = lax.all_to_all(weight_cut, "head", 0, 0, tiled=True)
         send_dtype = bf16 if level < 2 and not last else f32
         before_join = after
         before, after, low, sent, *rest = head_call(
@@ -479,7 +463,7 @@
             ("free", far),
             *([] if first else [("first", before), ("first", after)]),
             steps=1,
-            following=(adjoint, weight_cut) if level == 3 else (adjoint,),
+            following=(adjoint,),
         )
         held.append((low, before_join))
         total = rest[0] if rest else None
@@ -504,6 +488,16 @@
             weight_share.reshape(seq_count, features // seq_count, out_weight.shape[1]), "seq", 0, 0, tiled=True
         ).astype(f32),
         axis=0,
+    )
+    own, *sent = head_call(
+        project_kernel,
+        "project",
+        heads,
+        [("whole", (tokens, features), f32)] + [("whole", (tokens, features), bf16)] * (parts - 1),
+        ("scalar", head_place),
+        ("whole", mixed),
+        ("whole", out_weight),
+        steps=1,
     )
     query_grad, key_grad, value_grad, logit_grad = head_call(
         gradient_kernel,
@@ -528,16 +522,9 @@
         ("first", behind),
         ("free", far_adjoint),
     )
-    mixed_parts = gathered(mixed, "head")
-    vmem = pl.BlockSpec(memory_space=pltpu.VMEM)
-    output = pl.pallas_call(
-        project_kernel,
-        name="project",
-        in_specs=[pl.BlockSpec(memory_space=pltpu.SMEM)] + [vmem] * (1 + len(mixed_parts)),
-        out_specs=vmem,
-        out_shape=jax.ShapeDtypeStruct((tokens, features), bf16),
-        compiler_params=pltpu.CompilerParams(vmem_limit_bytes=VMEM_LIMIT),
-    )(head_place, weight_parts, *mixed_parts)
+    for mask, share in enumerate(sent, 1):
+        own = own + exchanged(share, "head", mask).astype(f32)
+    output = own.astype(bf16)
     logit_grad = logit_grad.reshape(heads, blocks, 2, BLOCK).transpose(2, 0, 1, 3).reshape(beta_logit.shape)
     return (
         output,

time: 117 us -> 112 us (0.957)
  waiting for transfers between devices: 17.6 us -> 11.6 us
  starting transfers between devices: 43.7 us -> 46 us
    ppermute x16 -> x19, starting transfers between devices: 22.6 us -> 30.1 us  [exchanged(): lax.ppermute(array, axis, [(i, i ^ mask) for i in range(lax.axis_size(axi...]
    all_to_all x1 -> x0, starting transfers between devices: 4.3 us -> none  [body(): weight_parts = lax.all_to_all(weight_cut, 'head', 0, 0, tiled=True)]
    ppermute x2, waiting for transfers between devices: 6.83 us -> 2.69 us  [passed(): return lax.ppermute(array, 'seq', pairs)]
    all_to_all x1, waiting for transfers between devices: 3.99 us -> 0.01 us  [body(): lax.all_to_all(weight_share.reshape(seq_count, features // seq_count, out...]
    ppermute x16 -> x19, waiting for transfers between devices: 6.75 us -> 8.85 us  [exchanged(): lax.ppermute(array, axis, [(i, i ^ mask) for i in range(lax.axis_size(axi...]
  transfers between devices with their start and end apart: 20 -> 22, of which waited for: 7 -> 8; matrix products, arithmetic and copies ran while one was open for 3% -> 3% of each run, Pallas kernels for 42% -> 39%
where the time goes in v4:
time: 112 us
  Pallas kernels  48 us (43%)
  starting transfers between devices  46 us (41%)
  waiting for transfers between devices  11.6 us (10%)
  other arithmetic  3.1 us (3%)
  local copies, waits for them, and re-layouts  2.46 us (2%)
    pallas_call x13, Pallas kernels, head_call(): pl.pallas_call(run, name=name, grid=(steps or heads,), in_specs=[pl.Block...  48 us
    ppermute x19, starting transfers between devices, exchanged(): lax.ppermute(array, axis, [(i, i ^ mask) for i in range(lax.axis_size(axi...  30.1 us
    all_to_all x1, starting transfers between devices, body(): lax.all_to_all(weight_share.reshape(seq_count, features // seq_count, out...  9.96 us
    ppermute x19, waiting for transfers between devices, exchanged(): lax.ppermute(array, axis, [(i, i ^ mask) for i in range(lax.axis_size(axi...  8.85 us
    ppermute x2, starting transfers between devices, passed(): return lax.ppermute(array, 'seq', pairs)  5.89 us
    ppermute x2, waiting for transfers between devices, passed(): return lax.ppermute(array, 'seq', pairs)  2.69 us
  transfers between devices with their start and end apart: 22, of which 8 were waited for; matrix products, arithmetic and copies ran while one was open for 3% of the time, Pallas kernels for 39%

profile of v4, /device:TPU:32, one launch (start us, length us, event | category | flops | bytes accessed | tf_op | source)
XLA Modules:
  0.0 111.9 jit_solution(13867545700950936183)
XLA Ops:
  0.6 0.1 collective-permute-start
  0.7 0.8 reshape.50
  1.5 0.1 reshape.51
  1.6 0.1 reshape.52
  1.7 0.6 pad_maximum_fusion.1.refs_3_.refs_2_
  2.3 0.0 collective-permute-done
  2.3 0.9 pad_maximum_fusion.refs_4_.refs_7_
  3.3 2.8 %collective-permute-start.3 = (bf16[2,256,256]{2,1,0:T(8,128)(2,1)S(1)}, bf16[2,256,256]{2,1,0:T(8,128)(2,1)S(1)}, u32[]{:S(2)}, u32[]{:S(2)}) collective-permute-start(bf16[2,256,256]{2,1,0:T(8,128)(2,1)S(1)} %pad_maximum_fusion.refs_4_.refs_7_), channel_id=1, source_target_pairs={{0,6},{1,7},{2,4},{3,5},{4,2},{5,3},{6,0},{7,1},{8,14},{9,15},{10,... | collective-permute-start | bytes 786440 | tf_op jit(solution)/shard_map/ppermute | solution.py:330
  6.1 0.8 collective-permute-start.2
  6.9 0.5 collective-permute-start.1
  7.5 9.3 %prepare.1 = (f32[2,4,128,128]{3,2,1,0:T(8,128)}, f32[2,4,128,256]{3,2,1,0:T(8,128)}, f32[2,4,128,128]{3,2,1,0:T(8,128)}, f32[2,4,128,256]{3,2,1,0:T(8,128)}, f3...) custom-call(f32[256,256]{1,0:T(8,128)} %refs_0_.3, f32[256,2,256]{2,1,0:T(2,128)} %refs_1_.3, ...), custom_call_target="tpu_custom_call" | custom-call | flops 17999998976 | tf_op jit(solution)/shard_map/prepare/pallas_call | solution.py:305
  16.7 1.9 %collective-permute-start.5 = (f32[2,128,256]{2,1,0:T(8,128)}, f32[2,128,256]{2,1,0:T(8,128)S(1)}, u32[]{:S(2)}, u32[]{:S(2)}) collective-permute-start(f32[2,128,256]{2,1,0:T(8,128)} %get-tuple-element.65.refs_2_), channel_id=1, source_target_pairs={{0,8},{8,0},{16,24},{24,16},{32,40},{40,32},{48,56},{56,48},{64,72... | collective-permute-start | bytes 786440 | tf_op jit(solution)/shard_map/ppermute | solution.py:330
  18.6 0.2 collective-permute-done.3.refs_7_.refs_10_
  18.9 0.0 collective-permute-done.2.refs_6_.refs_9_
  18.9 0.6 collective-permute-done.1.refs_5_.refs_8_
  19.5 4.5 %local.1 = (f32[256,256]{1,0:T(8,128)}, f32[2,4,128,128]{3,2,1,0:T(8,128)}, f32[2,128,128]{2,1,0:T(8,128)}) custom-call(s32[1]{0:T(128)} %bitcast.refs_0_.refs_1_, f32[2,4,64,128]{3,2,1,0:T(8,128)} %get-tuple-element.62.refs_1_.refs_5_, f32[2,4,128,128]{3,2,1,0:T(8,128)} %get-tuple-element.63.refs_2_.refs_5_, bf16[256,2048]{1,0:T(8,128)(2,1)} %refs_2_.3, ...), custom_call_target="tpu_custom_call" | custom-call | flops 10000000000 | tf_op jit(solution)/shard_map/local/pallas_call | solution.py:305
  24.0 1.9 %collective-permute-start.4 = (f32[2,128,128]{2,1,0:T(8,128)}, f32[2,128,128]{2,1,0:T(8,128)S(1)}, u32[]{:S(2)}, u32[]{:S(2)}) collective-permute-start(f32[2,128,128]{2,1,0:T(8,128)} %get-tuple-element.64.refs_0_.refs_1_), channel_id=1, source_target_pairs={{0,8},{8,0},{16,24},{24,16},{32,40},{40,32},{48,56},{56,48},{64,72... | collective-permute-start | bytes 393224 | tf_op jit(solution)/shard_map/ppermute | solution.py:330
  26.0 0.0 collective-permute-done.5.refs_3_
  26.0 2.1 %merge.4 = (f32[2,128,256]{2,1,0:T(8,128)}, f32[2,128,128]{2,1,0:T(8,128)}, f32[2,128,128]{2,1,0:T(8,128)}, bf16[2,128,256]{2,1,0:T(8,128)(2,1)}, f32[2,128,256]{2,1,0:T(8,128)}) custom-call(f32[2,128,128]{2,1,0:T(8,128)} %get-tuple-element.64.refs_0_.refs_1_, s32[1]{0:T(128)} %bitcast.4.refs_1_.refs_0_, f32[2,128,256]{2,1,0:T(8,128)} %get-tuple-element.65.refs_2_, ...), custom_call_target="tpu_custom_call" | custom-call | flops 4000000000 | tf_op jit(solution)/shard_map/merge/pallas_call | solution.py:305
  28.1 2.0 %collective-permute-start.7 = (bf16[2,128,256]{2,1,0:T(8,128)(2,1)}, bf16[2,128,256]{2,1,0:T(8,128)(2,1)S(1)}, u32[]{:S(2)}, u32[]{:S(2)}) collective-permute-start(bf16[2,128,256]{2,1,0:T(8,128)(2,1)} %get-tuple-element.70), channel_id=1, source_target_pairs={{0,24},{8,16},{16,8},{24,0},{32,56},{40,48},{48,40},{56,32},{64,88... | collective-permute-start | bytes 393224 | tf_op jit(solution)/shard_map/ppermute | solution.py:330
  30.1 0.0 collective-permute-done.4.refs_2_
  30.1 1.9 %merge_adjoint.4 = (f32[2,128,128]{2,1,0:T(8,128)}, bf16[2,128,128]{2,1,0:T(8,128)(2,1)S(1)}, f32[2,128,128]{2,1,0:T(8,128)}) custom-call(s32[1]{0:T(128)} %bitcast.4.refs_1_.refs_0_, f32[2,128,128]{2,1,0:T(8,128)} %get-tuple-element.64.refs_0_.refs_1_, f32[2,128,128]{2,1,0:T(8,128)S(1)} %collective-permute-done.4.refs_2_, ...), custom_call_target="tpu_custom_call" | custom-call | flops 4000000000 | tf_op jit(solution)/shard_map/merge_adjoint/pallas_call | solution.py:305
  31.9 1.2 %collective-permute-start.6 = (bf16[2,128,128]{2,1,0:T(8,128)(2,1)S(1)}, bf16[2,128,128]{2,1,0:T(8,128)(2,1)S(1)}, u32[]{:S(2)}, u32[]{:S(2)}) collective-permute-start(bf16[2,128,128]{2,1,0:T(8,128)(2,1)S(1)} %get-tuple-element.68), channel_id=1, source_target_pairs={{0,24},{8,16},{16,8},{24,0},{32,56},{40,48},{48,40},{56,32},{64,88... | collective-permute-start | bytes 196616 | tf_op jit(solution)/shard_map/ppermute | solution.py:330
  33.1 4.1 %collective-permute-done.7.refs_3_ = bf16[2,128,256]{2,1,0:T(8,128)(2,1)S(1)} collective-permute-done((bf16[2,128,256]{2,1,0:T(8,128)(2,1)}, bf16[2,128,256]{2,1,0:T(8,128)(2,1)S(1)}, u32[]{:S(2)}, u32[]{:S(2)}) %collective-permute-start.7) | collective-permute-done | bytes 131104 | tf_op jit(solution)/shard_map/ppermute | solution.py:330
  37.2 2.3 %merge.5 = (f32[2,128,256]{2,1,0:T(8,128)}, f32[2,128,128]{2,1,0:T(8,128)}, f32[2,128,128]{2,1,0:T(8,128)}, bf16[2,128,256]{2,1,0:T(8,128)(2,1)}, f32[2,128,256]{2,1,0:T(8,128)}) custom-call(f32[2,128,128]{2,1,0:T(8,128)} %get-tuple-element.67.refs_0_.refs_1_, s32[1]{0:T(128)} %bitcast.3.refs_1_.refs_0_, f32[2,128,256]{2,1,0:T(8,128)} %get-tuple-element.69.refs_2_, ...), custom_call_target="tpu_custom_call" | custom-call | flops 4000000000 | tf_op jit(solution)/shard_map/merge/pallas_call | solution.py:305
  39.5 4.9 %collective-permute-start.9 = (bf16[2,128,256]{2,1,0:T(8,128)(2,1)}, bf16[2,128,256]{2,1,0:T(8,128)(2,1)S(1)}, u32[]{:S(2)}, u32[]{:S(2)}) collective-permute-start(bf16[2,128,256]{2,1,0:T(8,128)(2,1)} %get-tuple-element.78), channel_id=1, source_target_pairs={{0,56},{8,48},{16,40},{24,32},{32,24},{40,16},{48,8},{56,0},{64,12... | collective-permute-start | bytes 393224 | tf_op jit(solution)/shard_map/ppermute | solution.py:330
  44.3 0.0 collective-permute-done.6.refs_2_
  44.3 2.0 %merge_adjoint.5 = (f32[2,128,128]{2,1,0:T(8,128)}, bf16[2,128,128]{2,1,0:T(8,128)(2,1)S(1)}, f32[2,128,128]{2,1,0:T(8,128)}) custom-call(s32[1]{0:T(128)} %bitcast.3.refs_1_.refs_0_, f32[2,128,128]{2,1,0:T(8,128)} %get-tuple-element.67.refs_0_.refs_1_, bf16[2,128,128]{2,1,0:T(8,128)(2,1)S(1)} %collective-permute-done.6.refs_2_, ...), custom_call_target="tpu_custom_call" | custom-call | flops 4000000000 | tf_op jit(solution)/shard_map/merge_adjoint/pallas_call | solution.py:305
  46.4 0.2 collective-permute-start.8
  46.5 1.6 %collective-permute-done.9.refs_3_ = bf16[2,128,256]{2,1,0:T(8,128)(2,1)S(1)} collective-permute-done((bf16[2,128,256]{2,1,0:T(8,128)(2,1)}, bf16[2,128,256]{2,1,0:T(8,128)(2,1)S(1)}, u32[]{:S(2)}, u32[]{:S(2)}) %collective-permute-start.9) | collective-permute-done | bytes 131104 | tf_op jit(solution)/shard_map/ppermute | solution.py:330
  48.1 2.4 %merge.6 = (f32[2,128,256]{2,1,0:T(8,128)}, f32[2,128,128]{2,1,0:T(8,128)}, f32[2,128,128]{2,1,0:T(8,128)}, f32[2,128,256]{2,1,0:T(8,128)}, f32[2,128,256]{2,1,0:T(8,128)}) custom-call(f32[2,128,128]{2,1,0:T(8,128)} %get-tuple-element.75.refs_0_.refs_1_, s32[1]{0:T(128)} %bitcast.2.refs_1_.refs_0_, f32[2,128,256]{2,1,0:T(8,128)} %get-tuple-element.77.refs_2_, ...), custom_call_target="tpu_custom_call" | custom-call | flops 4000000000 | tf_op jit(solution)/shard_map/merge/pallas_call | solution.py:305
  50.5 1.6 %collective-permute-start.11 = (f32[2,128,256]{2,1,0:T(8,128)}, f32[2,128,256]{2,1,0:T(8,128)S(1)}, u32[]{:S(2)}, u32[]{:S(2)}) collective-permute-start(f32[2,128,256]{2,1,0:T(8,128)} %get-tuple-element.86), channel_id=1, source_target_pairs={{0,64},{8,72},{16,80},{24,88},{32,96},{40,104},{48,112},{56,120},{... | collective-permute-start | bytes 786440 | tf_op jit(solution)/shard_map/ppermute | solution.py:330
  52.1 1.5 %collective-permute-done.8.refs_2_ = bf16[2,128,128]{2,1,0:T(8,128)(2,1)S(1)} collective-permute-done((bf16[2,128,128]{2,1,0:T(8,128)(2,1)S(1)}, bf16[2,128,128]{2,1,0:T(8,128)(2,1)S(1)}, u32[]{:S(2)}, u32[]{:S(2)}) %collective-permute-start.8) | collective-permute-done | bytes 65568 | tf_op jit(solution)/shard_map/ppermute | solution.py:330
  53.6 2.0 %merge_adjoint.6 = (f32[2,128,128]{2,1,0:T(8,128)}, f32[2,128,128]{2,1,0:T(8,128)S(1)}, f32[2,128,128]{2,1,0:T(8,128)}) custom-call(s32[1]{0:T(128)} %bitcast.2.refs_1_.refs_0_, f32[2,128,128]{2,1,0:T(8,128)} %get-tuple-element.75.refs_0_.refs_1_, bf16[2,128,128]{2,1,0:T(8,128)(2,1)S(1)} %collective-permute-done.8.refs_2_, ...), custom_call_target="tpu_custom_call" | custom-call | flops 4000000000 | tf_op jit(solution)/shard_map/merge_adjoint/pallas_call | solution.py:305
  55.7 1.6 %collective-permute-start.10 = (f32[2,128,128]{2,1,0:T(8,128)S(1)}, f32[2,128,128]{2,1,0:T(8,128)S(1)}, u32[]{:S(2)}, u32[]{:S(2)}) collective-permute-start(f32[2,128,128]{2,1,0:T(8,128)S(1)} %get-tuple-element.84), channel_id=1, source_target_pairs={{0,64},{8,72},{16,80},{24,88},{32,96},{40,104},{48,112},{56,120},{... | collective-permute-start | bytes 393224 | tf_op jit(solution)/shard_map/ppermute | solution.py:330
  57.2 0.8 collective-permute-done.11.refs_3_
  58.0 2.2 %merge.7 = (f32[2,128,256]{2,1,0:T(8,128)}, f32[2,128,128]{2,1,0:T(8,128)}, f32[2,128,128]{2,1,0:T(8,128)}, f32[2,128,128]{2,1,0:T(8,128)}) custom-call(f32[2,128,128]{2,1,0:T(8,128)} %get-tuple-element.83.refs_0_.refs_1_, s32[1]{0:T(128)} %bitcast.1.refs_1_.refs_0_, f32[2,128,256]{2,1,0:T(8,128)} %get-tuple-element.85.refs_2_, ...), custom_call_target="tpu_custom_call" | custom-call | flops 4000000000 | tf_op jit(solution)/shard_map/merge/pallas_call | solution.py:305
  60.2 4.6 %collective-permute-start.12 = (f32[2,128,128]{2,1,0:T(8,128)}, f32[2,128,128]{2,1,0:T(8,128)S(1)}, u32[]{:S(2)}, u32[]{:S(2)}) collective-permute-start(f32[2,128,128]{2,1,0:T(8,128)} %get-tuple-element.93), channel_id=1, source_target_pairs={{0,192},{8,200},{16,208},{24,216},{32,224},{40,232},{48,240},{56,2... | collective-permute-start | bytes 393224 | tf_op jit(solution)/shard_map/ppermute | solution.py:336
  64.8 0.0 collective-permute-done.10.refs_2_
  64.8 2.1 %merge_adjoint.7 = (f32[2,128,128]{2,1,0:T(8,128)}, f32[2,128,128]{2,1,0:T(8,128)S(1)}, f32[2,128,128]{2,1,0:T(8,128)}) custom-call(s32[1]{0:T(128)} %bitcast.1.refs_1_.refs_0_, f32[2,128,128]{2,1,0:T(8,128)} %get-tuple-element.83.refs_0_.refs_1_, f32[2,128,128]{2,1,0:T(8,128)S(1)} %collective-permute-done.10.refs_2_, ...), custom_call_target="tpu_custom_call" | custom-call | flops 4000000000 | tf_op jit(solution)/shard_map/merge_adjoint/pallas_call | solution.py:305
  66.9 0.7 collective-permute-done.12.refs_3_
  67.6 4.4 %mix.1 = (f32[2,4,128,128]{3,2,1,0:T(8,128)}, bf16[256,256]{1,0:T(8,128)(2,1)}, bf16[256,2048]{1,0:T(8,128)(2,1)}) custom-call(f32[2,128,128]{2,1,0:T(8,128)} %get-tuple-element.91.refs_0_, s32[1]{0:T(128)} %bitcast.refs_0_.refs_1_, f32[2,128,256]{2,1,0:T(8,128)} %get-tuple-element.92.refs_2_, f32[2,128,128]{2,1,0:T(8,128)S(1)} %collective-permute-done.12.refs_3_, ...), custom_call_target="tpu_custom_call" | custom-call | flops 10000000000 | tf_op jit(solution)/shard_map/mix/pallas_call | solution.py:305
  72.0 10.0 %all-to-all-start = ((bf16[32,8,2048]{2,1,0:T(8,128)(2,1)}), bf16[32,8,2048]{2,1,0:T(8,128)(2,1)S(1)}, u32[]{:S(2)}, u32[]{:S(2)}) async-start(bf16[32,8,2048]{2,1,0:T(8,128)(2,1)} %bitcast.12), calls=%async_computation | async-start | bytes 2097152 | tf_op jit(solution)/shard_map/all_to_all | solution.py:487
  82.0 1.3 %collective-permute-start.20 = (f32[2,128,128]{2,1,0:T(8,128)S(1)}, f32[2,128,128]{2,1,0:T(8,128)S(1)}, u32[]{:S(2)}, u32[]{:S(2)}) collective-permute-start(f32[2,128,128]{2,1,0:T(8,128)S(1)} %get-tuple-element.112), channel_id=1, source_target_pairs={{128,64},{136,72},{144,80},{152,88},{160,96},{168,104},{176,112},{... | collective-permute-start | bytes 393224 | tf_op jit(solution)/shard_map/ppermute | solution.py:336
  83.3 2.5 %project.1 = (f32[256,256]{1,0:T(8,128)}, bf16[256,256]{1,0:T(8,128)(2,1)}, bf16[256,256]{1,0:T(8,128)(2,1)}, bf16[256,256]{1,0:T(8,128)(2,1)}, bf16[256,256]{1,...) custom-call(s32[1]{0:T(128)} %bitcast.refs_0_.refs_1_, ...), custom_call_target="tpu_custom_call" | custom-call | flops 6000000000 | tf_op jit(solution)/shard_map/project/pallas_call | solution.py:305
  85.8 0.0 collective-permute-start.13
  85.8 1.5 %collective-permute-start.14 = (bf16[256,256]{1,0:T(8,128)(2,1)}, bf16[256,256]{1,0:T(8,128)(2,1)S(1)}, u32[]{:S(2)}, u32[]{:S(2)}) collective-permute-start(bf16[256,256]{1,0:T(8,128)(2,1)} %get-tuple-element.99), channel_id=1, source_target_pairs={{0,2},{1,3},{2,0},{3,1},{4,6},{5,7},{6,4},{7,5},{8,10},{9,11},{10,... | collective-permute-start | bytes 393224 | tf_op jit(solution)/shard_map/ppermute | solution.py:330
  87.4 0.3 collective-permute-start.15
  87.7 3.0 %collective-permute-start.16 = (bf16[256,256]{1,0:T(8,128)(2,1)}, bf16[256,256]{1,0:T(8,128)(2,1)S(1)}, u32[]{:S(2)}, u32[]{:S(2)}) collective-permute-start(bf16[256,256]{1,0:T(8,128)(2,1)} %get-tuple-element.101), channel_id=1, source_target_pairs={{0,4},{1,5},{2,6},{3,7},{4,0},{5,1},{6,2},{7,3},{8,12},{9,13},{10,... | collective-permute-start | bytes 393224 | tf_op jit(solution)/shard_map/ppermute | solution.py:330
  90.7 1.9 %collective-permute-done.20.refs_11_ = f32[2,128,128]{2,1,0:T(8,128)S(1)} collective-permute-done((f32[2,128,128]{2,1,0:T(8,128)S(1)}, f32[2,128,128]{2,1,0:T(8,128)S(1)}, u32[]{:S(2)}, u32[]{:S(2)}) %collective-permute-start.20) | collective-permute-done | bytes 131104 | tf_op jit(solution)/shard_map/ppermute | solution.py:336
  92.7 0.0 collective-permute-start.17
  92.7 0.0 collective-permute-done.13
  92.7 2.8 %collective-permute-start.18 = (bf16[256,256]{1,0:T(8,128)(2,1)}, bf16[256,256]{1,0:T(8,128)(2,1)S(1)}, u32[]{:S(2)}, u32[]{:S(2)}) collective-permute-start(bf16[256,256]{1,0:T(8,128)(2,1)} %get-tuple-element.103), channel_id=1, source_target_pairs={{0,6},{1,7},{2,4},{3,5},{4,2},{5,3},{6,0},{7,1},{8,14},{9,15},{10,... | collective-permute-start | bytes 393224 | tf_op jit(solution)/shard_map/ppermute | solution.py:330
  95.4 0.0 collective-permute-done.14
  95.4 3.0 %collective-permute-start.19 = (bf16[256,256]{1,0:T(8,128)(2,1)}, bf16[256,256]{1,0:T(8,128)(2,1)S(1)}, u32[]{:S(2)}, u32[]{:S(2)}) collective-permute-start(bf16[256,256]{1,0:T(8,128)(2,1)} %get-tuple-element.104), channel_id=1, source_target_pairs={{0,7},{1,6},{2,5},{3,4},{4,3},{5,2},{6,1},{7,0},{8,15},{9,14},{10,... | collective-permute-start | bytes 393224 | tf_op jit(solution)/shard_map/ppermute | solution.py:330
  98.4 10.4 %gradients.1 = (f32[256,256]{1,0:T(8,128)}, f32[256,2,256]{2,1,0:T(2,128)}, f32[256,2,256]{2,1,0:T(2,128)}, f32[2,4,128]{2,1,0:T(4,128)}) custom-call(f32[256,256]{1,0:T(8,128)} %refs_0_.3, f32[256,2,256]{2,1,0:T(2,128)} %refs_1_.3, f32[2,8,128]{2,1,0:T(8,128)} %pad_maximum_fusion.1.refs_3_.refs_2_, f32[2,4,128,128]{3,2,1,0:T(8,128)} %get-tuple-element.105.refs_3_, ...), custom_call_target="tpu_custom_call" | custom-call | flops 6000000000 | tf_op jit(solution)/shard_map/gradients/pallas_call | solution.py:305
  108.8 0.8 reshape.53
  109.6 0.7 reshape.54
  110.2 0.0 collective-permute-done.15
  110.2 0.0 collective-permute-done.16
  110.3 0.0 collective-permute-done.18
  110.3 0.8 add_convert_fusion
  111.1 0.0 all-to-all-done
  111.1 0.8 convert_reduce_fusion
  (15 shorter events, 0.1 us)
Async XLA Ops:
  0.6 1.7 %collective-permute-start = (bf16[256,256]{1,0:T(8,128)(2,1)}, bf16[256,256]{1,0:T(8,128)(2,1)S(1)}, u32[]{:S(2)}, u32[]{:S(2)}) collective-permute-start(bf16[256,256]{1,0:T(8,128)(2,1)} %param.11), channel_id=1, source_target_pairs={{0,1},{1,0},{2,3},{3,2},{4,5},{5,4},{6,7},{7,6},{8,9},{9,8},{10,11... | collective-permute-start | bytes 393224 | tf_op jit(solution)/shard_map/ppermute | solution.py:330
  3.3 16.3 %copy-start = (bf16[2,256,256]{2,1,0:T(8,128)(2,1)}, bf16[2,256,256]{2,1,0:T(8,128)(2,1)S(1)}, u32[]{:S(2)}) copy-start(bf16[2,256,256]{2,1,0:T(8,128)(2,1)S(1)} %pad_maximum_fusion.refs_4_.refs_7_) | copy-start | bytes 786436
  3.3 15.6 %collective-permute-start.3 = (bf16[2,256,256]{2,1,0:T(8,128)(2,1)S(1)}, bf16[2,256,256]{2,1,0:T(8,128)(2,1)S(1)}, u32[]{:S(2)}, u32[]{:S(2)}) collective-permute-start(bf16[2,256,256]{2,1,0:T(8,128)(2,1)S(1)} %pad_maximum_fusion.refs_4_.refs_7_), channel_id=1, source_target_pairs={{0,6},{1,7},{2,4},{3,5},{4,2},{5,3},{6,0},{7,1},{8,14},{9,15},{10,... | collective-permute-start | bytes 786440 | tf_op jit(solution)/shard_map/ppermute | solution.py:330
  6.1 12.8 %collective-permute-start.2 = (bf16[2,256,256]{2,1,0:T(8,128)(2,1)S(1)}, bf16[2,256,256]{2,1,0:T(8,128)(2,1)S(1)}, u32[]{:S(2)}, u32[]{:S(2)}) collective-permute-start(bf16[2,256,256]{2,1,0:T(8,128)(2,1)S(1)} %pad_maximum_fusion.refs_4_.refs_7_), channel_id=1, source_target_pairs={{0,4},{1,5},{2,6},{3,7},{4,0},{5,1},{6,2},{7,3},{8,12},{9,13},{10,... | collective-permute-start | bytes 786440 | tf_op jit(solution)/shard_map/ppermute | solution.py:330
  6.9 12.6 %collective-permute-start.1 = (bf16[2,256,256]{2,1,0:T(8,128)(2,1)S(1)}, bf16[2,256,256]{2,1,0:T(8,128)(2,1)S(1)}, u32[]{:S(2)}, u32[]{:S(2)}) collective-permute-start(bf16[2,256,256]{2,1,0:T(8,128)(2,1)S(1)} %pad_maximum_fusion.refs_4_.refs_7_), channel_id=1, source_target_pairs={{0,2},{1,3},{2,0},{3,1},{4,6},{5,7},{6,4},{7,5},{8,10},{9,11},{10,... | collective-permute-start | bytes 786440 | tf_op jit(solution)/shard_map/ppermute | solution.py:330
  16.7 9.3 %collective-permute-start.5 = (f32[2,128,256]{2,1,0:T(8,128)}, f32[2,128,256]{2,1,0:T(8,128)S(1)}, u32[]{:S(2)}, u32[]{:S(2)}) collective-permute-start(f32[2,128,256]{2,1,0:T(8,128)} %get-tuple-element.65.refs_2_), channel_id=1, source_target_pairs={{0,8},{8,0},{16,24},{24,16},{32,40},{40,32},{48,56},{56,48},{64,72... | collective-permute-start | bytes 786440 | tf_op jit(solution)/shard_map/ppermute | solution.py:330
  18.9 5.1 %copy-start.1 = (bf16[2,256,256]{2,1,0:T(8,128)(2,1)}, bf16[2,256,256]{2,1,0:T(8,128)(2,1)S(1)}, u32[]{:S(2)}) copy-start(bf16[2,256,256]{2,1,0:T(8,128)(2,1)S(1)} %collective-permute-done.3.refs_7_.refs_10_) | copy-start | bytes 786436
  18.9 5.1 %copy-start.2 = (bf16[2,256,256]{2,1,0:T(8,128)(2,1)}, bf16[2,256,256]{2,1,0:T(8,128)(2,1)S(1)}, u32[]{:S(2)}) copy-start(bf16[2,256,256]{2,1,0:T(8,128)(2,1)S(1)} %collective-permute-done.2.refs_6_.refs_9_) | copy-start | bytes 786436
  19.5 4.5 %copy-start.3 = (bf16[2,256,256]{2,1,0:T(8,128)(2,1)}, bf16[2,256,256]{2,1,0:T(8,128)(2,1)S(1)}, u32[]{:S(2)}) copy-start(bf16[2,256,256]{2,1,0:T(8,128)(2,1)S(1)} %collective-permute-done.1.refs_5_.refs_8_) | copy-start | bytes 786436
  24.0 6.0 %collective-permute-start.4 = (f32[2,128,128]{2,1,0:T(8,128)}, f32[2,128,128]{2,1,0:T(8,128)S(1)}, u32[]{:S(2)}, u32[]{:S(2)}) collective-permute-start(f32[2,128,128]{2,1,0:T(8,128)} %get-tuple-element.64.refs_0_.refs_1_), channel_id=1, source_target_pairs={{0,8},{8,0},{16,24},{24,16},{32,40},{40,32},{48,56},{56,48},{64,72... | collective-permute-start | bytes 393224 | tf_op jit(solution)/shard_map/ppermute | solution.py:330
  28.1 9.1 %collective-permute-start.7 = (bf16[2,128,256]{2,1,0:T(8,128)(2,1)}, bf16[2,128,256]{2,1,0:T(8,128)(2,1)S(1)}, u32[]{:S(2)}, u32[]{:S(2)}) collective-permute-start(bf16[2,128,256]{2,1,0:T(8,128)(2,1)} %get-tuple-element.70), channel_id=1, source_target_pairs={{0,24},{8,16},{16,8},{24,0},{32,56},{40,48},{48,40},{56,32},{64,88... | collective-permute-start | bytes 393224 | tf_op jit(solution)/shard_map/ppermute | solution.py:330
  31.9 12.4 %collective-permute-start.6 = (bf16[2,128,128]{2,1,0:T(8,128)(2,1)S(1)}, bf16[2,128,128]{2,1,0:T(8,128)(2,1)S(1)}, u32[]{:S(2)}, u32[]{:S(2)}) collective-permute-start(bf16[2,128,128]{2,1,0:T(8,128)(2,1)S(1)} %get-tuple-element.68), channel_id=1, source_target_pairs={{0,24},{8,16},{16,8},{24,0},{32,56},{40,48},{48,40},{56,32},{64,88... | collective-permute-start | bytes 196616 | tf_op jit(solution)/shard_map/ppermute | solution.py:330
  39.5 8.7 %collective-permute-start.9 = (bf16[2,128,256]{2,1,0:T(8,128)(2,1)}, bf16[2,128,256]{2,1,0:T(8,128)(2,1)S(1)}, u32[]{:S(2)}, u32[]{:S(2)}) collective-permute-start(bf16[2,128,256]{2,1,0:T(8,128)(2,1)} %get-tuple-element.78), channel_id=1, source_target_pairs={{0,56},{8,48},{16,40},{24,32},{32,24},{40,16},{48,8},{56,0},{64,12... | collective-permute-start | bytes 393224 | tf_op jit(solution)/shard_map/ppermute | solution.py:330
  46.4 7.3 %collective-permute-start.8 = (bf16[2,128,128]{2,1,0:T(8,128)(2,1)S(1)}, bf16[2,128,128]{2,1,0:T(8,128)(2,1)S(1)}, u32[]{:S(2)}, u32[]{:S(2)}) collective-permute-start(bf16[2,128,128]{2,1,0:T(8,128)(2,1)S(1)} %get-tuple-element.76), channel_id=1, source_target_pairs={{0,56},{8,48},{16,40},{24,32},{32,24},{40,16},{48,8},{56,0},{64,12... | collective-permute-start | bytes 196616 | tf_op jit(solution)/shard_map/ppermute | solution.py:330
  50.5 7.5 %collective-permute-start.11 = (f32[2,128,256]{2,1,0:T(8,128)}, f32[2,128,256]{2,1,0:T(8,128)S(1)}, u32[]{:S(2)}, u32[]{:S(2)}) collective-permute-start(f32[2,128,256]{2,1,0:T(8,128)} %get-tuple-element.86), channel_id=1, source_target_pairs={{0,64},{8,72},{16,80},{24,88},{32,96},{40,104},{48,112},{56,120},{... | collective-permute-start | bytes 786440 | tf_op jit(solution)/shard_map/ppermute | solution.py:330
  55.7 9.2 %collective-permute-start.10 = (f32[2,128,128]{2,1,0:T(8,128)S(1)}, f32[2,128,128]{2,1,0:T(8,128)S(1)}, u32[]{:S(2)}, u32[]{:S(2)}) collective-permute-start(f32[2,128,128]{2,1,0:T(8,128)S(1)} %get-tuple-element.84), channel_id=1, source_target_pairs={{0,64},{8,72},{16,80},{24,88},{32,96},{40,104},{48,112},{56,120},{... | collective-permute-start | bytes 393224 | tf_op jit(solution)/shard_map/ppermute | solution.py:330
  60.2 7.4 %collective-permute-start.12 = (f32[2,128,128]{2,1,0:T(8,128)}, f32[2,128,128]{2,1,0:T(8,128)S(1)}, u32[]{:S(2)}, u32[]{:S(2)}) collective-permute-start(f32[2,128,128]{2,1,0:T(8,128)} %get-tuple-element.93), channel_id=1, source_target_pairs={{0,192},{8,200},{16,208},{24,216},{32,224},{40,232},{48,240},{56,2... | collective-permute-start | bytes 393224 | tf_op jit(solution)/shard_map/ppermute | solution.py:336
  72.0 39.0 %all-to-all-start = ((bf16[32,8,2048]{2,1,0:T(8,128)(2,1)}), bf16[32,8,2048]{2,1,0:T(8,128)(2,1)S(1)}, u32[]{:S(2)}, u32[]{:S(2)}) async-start(bf16[32,8,2048]{2,1,0:T(8,128)(2,1)} %bitcast.12), calls=%async_computation | async-start | bytes 2097152 | tf_op jit(solution)/shard_map/all_to_all | solution.py:487
  82.0 10.7 %collective-permute-start.20 = (f32[2,128,128]{2,1,0:T(8,128)S(1)}, f32[2,128,128]{2,1,0:T(8,128)S(1)}, u32[]{:S(2)}, u32[]{:S(2)}) collective-permute-start(f32[2,128,128]{2,1,0:T(8,128)S(1)} %get-tuple-element.112), channel_id=1, source_target_pairs={{128,64},{136,72},{144,80},{152,88},{160,96},{168,104},{176,112},{... | collective-permute-start | bytes 393224 | tf_op jit(solution)/shard_map/ppermute | solution.py:336
  85.8 6.8 %collective-permute-start.13 = (bf16[256,256]{1,0:T(8,128)(2,1)}, bf16[256,256]{1,0:T(8,128)(2,1)S(1)}, u32[]{:S(2)}, u32[]{:S(2)}) collective-permute-start(bf16[256,256]{1,0:T(8,128)(2,1)} %get-tuple-element.98), channel_id=1, source_target_pairs={{0,1},{1,0},{2,3},{3,2},{4,5},{5,4},{6,7},{7,6},{8,9},{9,8},{10,11... | collective-permute-start | bytes 393224 | tf_op jit(solution)/shard_map/ppermute | solution.py:330
  85.8 9.6 %collective-permute-start.14 = (bf16[256,256]{1,0:T(8,128)(2,1)}, bf16[256,256]{1,0:T(8,128)(2,1)S(1)}, u32[]{:S(2)}, u32[]{:S(2)}) collective-permute-start(bf16[256,256]{1,0:T(8,128)(2,1)} %get-tuple-element.99), channel_id=1, source_target_pairs={{0,2},{1,3},{2,0},{3,1},{4,6},{5,7},{6,4},{7,5},{8,10},{9,11},{10,... | collective-permute-start | bytes 393224 | tf_op jit(solution)/shard_map/ppermute | solution.py:330
  87.4 22.9 %collective-permute-start.15 = (bf16[256,256]{1,0:T(8,128)(2,1)}, bf16[256,256]{1,0:T(8,128)(2,1)S(1)}, u32[]{:S(2)}, u32[]{:S(2)}) collective-permute-start(bf16[256,256]{1,0:T(8,128)(2,1)} %get-tuple-element.100), channel_id=1, source_target_pairs={{0,3},{1,2},{2,1},{3,0},{4,7},{5,6},{6,5},{7,4},{8,11},{9,10},{10,... | collective-permute-start | bytes 393224 | tf_op jit(solution)/shard_map/ppermute | solution.py:330
  87.7 22.5 %collective-permute-start.16 = (bf16[256,256]{1,0:T(8,128)(2,1)}, bf16[256,256]{1,0:T(8,128)(2,1)S(1)}, u32[]{:S(2)}, u32[]{:S(2)}) collective-permute-start(bf16[256,256]{1,0:T(8,128)(2,1)} %get-tuple-element.101), channel_id=1, source_target_pairs={{0,4},{1,5},{2,6},{3,7},{4,0},{5,1},{6,2},{7,3},{8,12},{9,13},{10,... | collective-permute-start | bytes 393224 | tf_op jit(solution)/shard_map/ppermute | solution.py:330
  92.7 17.6 %collective-permute-start.17 = (bf16[256,256]{1,0:T(8,128)(2,1)}, bf16[256,256]{1,0:T(8,128)(2,1)S(1)}, u32[]{:S(2)}, u32[]{:S(2)}) collective-permute-start(bf16[256,256]{1,0:T(8,128)(2,1)} %get-tuple-element.102), channel_id=1, source_target_pairs={{0,5},{1,4},{2,7},{3,6},{4,1},{5,0},{6,3},{7,2},{8,13},{9,12},{10,... | collective-permute-start | bytes 393224 | tf_op jit(solution)/shard_map/ppermute | solution.py:330
  92.7 17.6 %collective-permute-start.18 = (bf16[256,256]{1,0:T(8,128)(2,1)}, bf16[256,256]{1,0:T(8,128)(2,1)S(1)}, u32[]{:S(2)}, u32[]{:S(2)}) collective-permute-start(bf16[256,256]{1,0:T(8,128)(2,1)} %get-tuple-element.103), channel_id=1, source_target_pairs={{0,6},{1,7},{2,4},{3,5},{4,2},{5,3},{6,0},{7,1},{8,14},{9,15},{10,... | collective-permute-start | bytes 393224 | tf_op jit(solution)/shard_map/ppermute | solution.py:330
  95.4 14.8 %collective-permute-start.19 = (bf16[256,256]{1,0:T(8,128)(2,1)}, bf16[256,256]{1,0:T(8,128)(2,1)S(1)}, u32[]{:S(2)}, u32[]{:S(2)}) collective-permute-start(bf16[256,256]{1,0:T(8,128)(2,1)} %get-tuple-element.104), channel_id=1, source_target_pairs={{0,7},{1,6},{2,5},{3,4},{4,3},{5,2},{6,1},{7,0},{8,15},{9,14},{10,... | collective-permute-start | bytes 393224 | tf_op jit(solution)/shard_map/ppermute | solution.py:330
  98.4 11.9 %copy-start.4 = (f32[256,256]{1,0:T(8,128)S(1)}, f32[256,256]{1,0:T(8,128)}, u32[]{:S(2)}) copy-start(f32[256,256]{1,0:T(8,128)} %get-tuple-element.97) | copy-start | bytes 786436
